TPU v7x, 128 devices: a whole 4x4x4 slice. The times are simulated.
128 devices in a mesh: ctx: 32 (over z, x, core), head: 4 (over y).
Axes of the slice: x: 4, y: 4, z: 4, core: 2. Of those that a mesh axis runs over, the one named last changes fastest.
Arguments:
- query: bfloat16 [8, 16384, 256], P(None, ('ctx', 'head')), may hold values from -6 to 6
- keys: bfloat16 [8, 16384, 256], P(None, ('ctx', 'head')), may hold values from -6 to 6
- values: bfloat16 [8, 16384, 512], P(None, ('ctx', 'head')), may hold values from -6 to 6
- igate: bfloat16 [8, 16384], P(None, ('ctx', 'head')), may hold values from -8 to 0
- fgate: bfloat16 [8, 16384], P(None, ('ctx', 'head')), may hold values from 0 to 16
- hidden_output_gradient: bfloat16 [8, 16384, 512], P(None, ('ctx', 'head')), may hold values from -6 to 6
- doc_start: int32 [16384], P('ctx'), may hold values 0 or 1
Outputs:
- hidden_out: bfloat16 [8, 16384, 512], P(None, ('ctx', 'head'))
- grad_query: bfloat16 [8, 16384, 256], P(None, ('ctx', 'head'))
- grad_keys: bfloat16 [8, 16384, 256], P(None, ('ctx', 'head'))
- grad_values: bfloat16 [8, 16384, 512], P(None, ('ctx', 'head'))
- input_gate_gradient: bfloat16 [8, 16384], P(None, ('ctx', 'head'))
- grad_fgate: bfloat16 [8, 16384], P(None, ('ctx', 'head'))
Inputs may be any that keep to these rules, and one draw needn't show every extreme that they name: `doc_start`: 1 marks the first token of a document; tokens separated by a document start do not interact.
All inputs are finite; a program needn't handle non-finite values. No bound on the sum of `doc_start` on one device may be relied on, other than what follows from the above.
Results may differ from a plain program's by a relative error of at most 0.038.
Values may be sent and summed in bfloat16 or wider, within the bound.
No kernel may reach another device: no remote copies, remote signals or barrier semaphores. Data moves between devices by JAX's collectives and lax.ppermute only.
A program may use at most 192 MiB of HBM per device.

v0:
```python
import jax
import jax.numpy as jnp
from jax import lax
from jax.sharding import PartitionSpec as P

neg_large = -1e30


def entering(value, axis, join, neutral, backward):
    count, mine = (lax.axis_size(axis), lax.axis_index(axis))
    pieces = jax.tree.map(lambda part: lax.all_gather(part, axis), value)
    if backward:
        pieces = jax.tree.map(lambda part: part[::-1], pieces)
        mine = count - 1 - mine
    running = jax.tree.map(
        lambda part, zero: jnp.full_like(part, 0) + jnp.asarray(zero, part.dtype), value, neutral
    )

    def hop(position, running):
        longer = join(running, jax.tree.map(lambda part: part[position], pieces))
        return jax.tree.map(lambda new, old: jnp.where(position < mine, new, old), longer, running)

    return lax.fori_loop(0, count - 1, hop, running)


def contract(form, left, right):
    return jnp.einsum(form, left, right, preferred_element_type=jnp.float32)


def block_local(query, keys, values, igate, fgate, starts):
    length = query.shape[1]
    query_scale = query.shape[2] ** (-0.5)
    log_forget = jax.nn.log_sigmoid(fgate.astype(jnp.float32))
    cumulative = jnp.cumsum(log_forget, axis=1)
    segment = jnp.cumsum(starts)
    ingate = igate.astype(jnp.float32)
    position = lax.broadcasted_iota(jnp.int32, (length, length), 0)
    source = lax.broadcasted_iota(jnp.int32, (length, length), 1)
    allowed = (position >= source) & (segment[:, None] == segment[None, :])
    log_weight = cumulative[:, :, None] - cumulative[:, None, :] + ingate[:, None, :]
    weight = jnp.exp(jnp.where(allowed[None], log_weight, neg_large))
    scores = contract("htd,hsd->hts", query, keys) * query_scale
    pair_weight = (weight * scores).astype(jnp.bfloat16)
    tail_mask = (segment == segment[length - 1])[None, :]
    alpha_weight = jnp.where(
        tail_mask, jnp.exp(cumulative[:, length - 1 :] - cumulative + ingate), 0.0
    )
    beta_weight = jnp.where((segment == 0)[None, :], jnp.exp(cumulative), 0.0)
    decay_factor = jnp.where(segment[length - 1] == 0, jnp.exp(cumulative[:, length - 1]), 0.0)
    keys_alpha = (alpha_weight[:, :, None] * keys).astype(jnp.bfloat16)
    update = contract("hsd,hsv->hdv", keys_alpha, values)
    update_n = jnp.sum(keys_alpha.astype(jnp.float32), axis=1)
    return (weight, pair_weight, alpha_weight, beta_weight, decay_factor, update, update_n)


def block_output(query, values, pair_weight, beta_weight, state_in, state_n_in):
    query_scale = query.shape[2] ** (-0.5)
    state_bf = state_in.astype(jnp.bfloat16)
    state_n_bf = state_n_in.astype(jnp.bfloat16)
    cross = contract("htd,hdv->htv", query, state_bf)
    numerator = (
        contract("hts,hsv->htv", pair_weight, values)
        + beta_weight[:, :, None] * cross * query_scale
    )
    cross_n = jnp.sum(query * state_n_bf.astype(jnp.float32)[:, None, :], axis=2)
    denominator = (
        jnp.sum(pair_weight.astype(jnp.float32), axis=2) + beta_weight * cross_n * query_scale
    )
    norm_value = jnp.sqrt(denominator * denominator + 1.0)
    hidden = numerator / norm_value[:, :, None]
    return (hidden, denominator, norm_value, state_bf, state_n_bf)


def block_backward(
    query,
    keys,
    values,
    hidden_output_gradient,
    weight,
    pair_weight,
    beta_weight,
    hidden,
    denominator,
    norm_value,
):
    query_scale = query.shape[2] ** (-0.5)
    num_grad = (hidden_output_gradient / norm_value[:, :, None]).astype(jnp.bfloat16)
    den_grad = (
        -jnp.sum(hidden_output_gradient * hidden, axis=2) * denominator / (norm_value * norm_value)
    )
    pair_grad = contract("htv,hsv->hts", num_grad, values) + den_grad[:, :, None]
    score_grad = (weight * pair_grad).astype(jnp.bfloat16)
    query_grad = contract("hts,hsd->htd", score_grad, keys) * query_scale
    key_grad = contract("hts,htd->hsd", score_grad, query) * query_scale
    value_grad = contract("hts,htv->hsv", pair_weight, num_grad)
    query_beta = (beta_weight[:, :, None] * query * query_scale).astype(jnp.bfloat16)
    adjoint = contract("htd,htv->hdv", query_beta, num_grad)
    adjoint_n = jnp.sum(query_beta * den_grad[:, :, None], axis=1)
    return (num_grad, den_grad, query_grad, key_grad, value_grad, adjoint, adjoint_n)


def block_grads(
    query,
    keys,
    values,
    num_grad,
    den_grad,
    beta_weight,
    alpha_weight,
    state_bf,
    state_n_bf,
    query_grad,
    key_grad,
    value_grad,
    back_in,
    back_n_in,
):
    query_scale = query.shape[2] ** (-0.5)
    back_bf = back_in.astype(jnp.bfloat16)
    back_n_bf = back_n_in.astype(jnp.bfloat16)
    from_state = (
        contract("htv,hdv->htd", num_grad, state_bf)
        + den_grad[:, :, None] * state_n_bf.astype(jnp.float32)[:, None, :]
    )
    query_grad = query_grad + beta_weight[:, :, None] * from_state * query_scale
    from_back = (
        contract("hsv,hdv->hsd", values, back_bf) + back_n_bf.astype(jnp.float32)[:, None, :]
    )
    key_grad = key_grad + alpha_weight[:, :, None] * from_back
    value_grad = value_grad + alpha_weight[:, :, None] * contract("hsd,hdv->hsv", keys, back_bf)
    row_term = jnp.sum(query * query_grad, axis=2)
    key_term = jnp.sum(keys * key_grad, axis=2)
    return (query_grad, key_grad, value_grad, row_term, key_term)


def combine_states(earlier, latter):
    return (
        earlier[0] * latter[0],
        latter[0][:, None, None] * earlier[1] + latter[1],
        latter[0][:, None] * earlier[2] + latter[2],
    )


def add_totals(earlier, latter):
    return earlier + latter


def shards(query, keys, values, igate, fgate, hidden_output_gradient, doc_start):
    query, keys, values, igate, fgate, hidden_output_gradient = (
        lax.all_to_all(query, "head", split_axis=0, concat_axis=1, tiled=True),
        lax.all_to_all(keys, "head", split_axis=0, concat_axis=1, tiled=True),
        lax.all_to_all(values, "head", split_axis=0, concat_axis=1, tiled=True),
        lax.all_to_all(igate, "head", split_axis=0, concat_axis=1, tiled=True),
        lax.all_to_all(fgate, "head", split_axis=0, concat_axis=1, tiled=True),
        lax.all_to_all(hidden_output_gradient, "head", split_axis=0, concat_axis=1, tiled=True),
    )
    weight, pair_weight, alpha_weight, beta_weight, decay_factor, update, update_n = block_local(
        query, keys, values, igate, fgate, doc_start
    )
    identity = (jnp.ones_like(decay_factor), jnp.zeros_like(update), jnp.zeros_like(update_n))
    decay_prior, state_in, state_n_in = entering(
        (decay_factor, update, update_n), "ctx", combine_states, identity, False
    )
    hidden, denominator, norm_value, state_bf, state_n_bf = block_output(
        query, values, pair_weight, beta_weight, state_in, state_n_in
    )
    hidden_bf = hidden.astype(jnp.bfloat16)
    num_grad, den_grad, query_grad, key_grad, value_grad, adjoint, adjoint_n = block_backward(
        query,
        keys,
        values,
        hidden_output_gradient,
        weight,
        pair_weight,
        beta_weight,
        hidden,
        denominator,
        norm_value,
    )
    decay_after, back_in, back_n_in = entering(
        (decay_factor, adjoint, adjoint_n), "ctx", combine_states, identity, True
    )
    query_grad, key_grad, value_grad, row_term, key_term = block_grads(
        query,
        keys,
        values,
        num_grad,
        den_grad,
        beta_weight,
        alpha_weight,
        state_bf,
        state_n_bf,
        query_grad,
        key_grad,
        value_grad,
        back_in,
        back_n_in,
    )
    gate_term = row_term - key_term
    later_total = entering(
        jnp.sum(gate_term, axis=1), "ctx", add_totals, jnp.zeros_like(decay_factor), True
    )
    forget_grad = jnp.flip(jnp.cumsum(jnp.flip(gate_term, 1), axis=1), 1) + later_total[:, None]
    grad_forget = (forget_grad * jax.nn.sigmoid(-fgate.astype(jnp.float32))).astype(jnp.bfloat16)
    grad_input = key_term.astype(jnp.bfloat16)
    query_bf = query_grad.astype(jnp.bfloat16)
    key_bf = key_grad.astype(jnp.bfloat16)
    value_bf = value_grad.astype(jnp.bfloat16)
    hidden_home, query_home, key_home, value_home, input_home, forget_home = (
        lax.all_to_all(hidden_bf, "head", split_axis=1, concat_axis=0, tiled=True),
        lax.all_to_all(query_bf, "head", split_axis=1, concat_axis=0, tiled=True),
        lax.all_to_all(key_bf, "head", split_axis=1, concat_axis=0, tiled=True),
        lax.all_to_all(value_bf, "head", split_axis=1, concat_axis=0, tiled=True),
        lax.all_to_all(grad_input, "head", split_axis=1, concat_axis=0, tiled=True),
        lax.all_to_all(grad_forget, "head", split_axis=1, concat_axis=0, tiled=True),
    )
    return (hidden_home, query_home, key_home, value_home, input_home, forget_home)


def solution(mesh):
    return jax.shard_map(
        shards,
        mesh=mesh,
        in_specs=(
            P(None, ("ctx", "head"), None),
            P(None, ("ctx", "head"), None),
            P(None, ("ctx", "head"), None),
            P(None, ("ctx", "head")),
            P(None, ("ctx", "head")),
            P(None, ("ctx", "head"), None),
            P("ctx"),
        ),
        out_specs=(
            P(None, ("ctx", "head"), None),
            P(None, ("ctx", "head"), None),
            P(None, ("ctx", "head"), None),
            P(None, ("ctx", "head"), None),
            P(None, ("ctx", "head")),
            P(None, ("ctx", "head")),
        ),
        check_vma=False,
    )
```

profile of v0, /device:TPU:2, one launch (start us, length us, event | category | flops | bytes accessed | tf_op | source)
XLA Modules:
  0.0 574.5 jit_solution(6999822956686224585)
XLA Ops:
  7.2 4.5 all-to-all-start
  12.7 4.1 all-to-all-done
  16.8 3.2 all-to-all-start.1
  20.2 5.0 all-to-all-done.1
  25.2 3.5 all-to-all-start.3
  30.0 6.7 %all-to-all-done.3 = bf16[8,128,256]{2,1,0:T(8,128)(2,1)S(1)} async-done(((bf16[8,128,256]{2,1,0:T(8,128)(2,1)}), bf16[8,128,256]{2,1,0:T(8,128)(2,1)S(1)}, u32[]{:S(2)}, u32[]{:S(2)}) %all-to-all-start.3) | async-done | bytes 524320 | tf_op jit(solution)/shard_map/all_to_all | solution.py:151
  36.7 3.5 all-to-all-start.4
  41.7 10.2 %all-to-all-done.4 = bf16[8,128,512]{2,1,0:T(8,128)(2,1)S(1)} async-done(((bf16[8,128,512]{2,1,0:T(8,128)(2,1)}), bf16[8,128,512]{2,1,0:T(8,128)(2,1)S(1)}, u32[]{:S(2)}, u32[]{:S(2)}) %all-to-all-start.4) | async-done | bytes 1048608 | tf_op jit(solution)/shard_map/all_to_all | solution.py:152
  54.8 1.7 fusion.27
  56.5 3.5 all-to-all-start.2
  62.8 5.2 all-to-all-done.2
  68.0 4.3 all-to-all-start.6
  72.5 59.6 %all-reduce = f32[64]{0:T(128)S(1)} all-reduce(f32[64]{0:T(128)S(1)} %fusion.55), channel_id=2, replica_groups=mesh['ctx'=32,'head'=4] {'ctx'}, use_global_device_ids=true, to_apply=%add | all-reduce | flops 64 | bytes 512
  134.8 26.9 %all-gather.6 = f32[32,2,256]{2,1,0:T(2,128)S(1)} all-gather(f32[1,2,256]{2,1,0:T(2,128)S(1)} %bitcast.241), channel_id=4, replica_groups=mesh['ctx'=32,'head'=4] {'ctx'}, dimensions={0}, use_global_device_ids=true | all-gather | bytes 67584 | tf_op jit(solution)/shard_map/all_gather | solution.py:11
  161.7 1.9 convert_reduce_fusion
  163.6 2.9 copy.89
  166.5 2.3 fusion.59
  168.8 2.2 all-gather.11.cloned.1.call-done
  171.1 53.0 %while.46 = (s32[]{:T(128)}, f32[2,256,512]{2,1,0:T(8,128)S(1)}, f32[2,256]{1,0:T(2,128)S(1)}, s32[]{:T(128)}, f32[32,2]{1,0:T(8,128)S(1)}, /*index=5*/f32[32,2,...) while((s32[]{:T(128)}, f32[2,256,512]{2,1,0:T(8,128)S(1)}, ...), condition=%wide.region_6.7_spmd.clone, body=%wide.region_5.6_spmd.clone.sunk | while | flops 1050628 | bytes 3152031 | solution.py:23
  171.1 1.7 fusion.87
  172.8 1.6 fusion.87
  177.9 1.6 fusion.87
  179.7 1.6 fusion.87
  181.4 1.6 fusion.87
  183.1 1.6 fusion.87
  184.8 1.6 fusion.87
  186.5 1.6 fusion.87
  188.2 1.6 fusion.87
  195.0 1.6 fusion.87
  196.7 1.6 fusion.87
  198.4 1.6 fusion.87
  200.1 1.6 fusion.87
  201.8 1.6 fusion.87
  203.5 1.6 fusion.87
  205.3 1.6 fusion.87
  210.4 1.6 fusion.87
  212.1 1.6 fusion.87
  213.8 1.6 fusion.87
  215.5 1.6 fusion.87
  224.3 4.0 fusion.8
  229.2 1.6 fusion.25
  234.3 22.6 %all-gather.7 = f32[32,2,256]{2,1,0:T(2,128)S(1)} all-gather(f32[1,2,256]{2,1,0:T(2,128)S(1)} %bitcast.240), channel_id=6, replica_groups=mesh['ctx'=32,'head'=4] {'ctx'}, dimensions={0}, use_global_device_ids=true | all-gather | bytes 67584 | tf_op jit(solution)/shard_map/all_gather | solution.py:11
  256.9 2.4 multiply_convert_fusion
  263.3 4.3 all-to-all-start.7
  267.6 3.4 copy.87
  272.4 72.0 %all-gather.13.cloned.1.call-done = f32[64,256,512]{2,1,0:T(8,128)} async-done(((f32[2,256,512]{2,1,0:T(8,128)}), f32[64,256,512]{2,1,0:T(8,128)}) %all-gather.13.cloned.1.call-update) | async-done | bytes 33554448 | tf_op jit(solution)/shard_map/all_gather | solution.py:11
  344.4 22.9 %rev.20 = f32[32,2,256,512]{3,2,1,0:T(8,128)} reverse(f32[32,2,256,512]{3,2,1,0:T(8,128)} %bitcast.211), dimensions={0} | reverse | bytes 67108864 | tf_op jit(solution)/shard_map/rev | solution.py:13
  367.3 74.2 %while.47 = (s32[]{:T(128)}, f32[2,256,512]{2,1,0:T(8,128)S(1)}, f32[2,256]{1,0:T(2,128)S(1)}, s32[]{:T(128)}, f32[32,2]{1,0:T(8,128)}, /*index=5*/f32[32,2,256,...) while((s32[]{:T(128)}, f32[2,256,512]{2,1,0:T(8,128)S(1)}, ...), condition=%wide.region_12.13_spmd.clone, body=%wide.region_11.12_spmd.clone.sunk | while | flops 1050628 | bytes 3152031 | solution.py:23
  441.5 2.7 fusion.17
  445.1 60.4 %all-reduce.1 = f32[64]{0:T(128)S(1)} all-reduce(f32[64]{0:T(128)S(1)} %dynamic-update-slice.1), channel_id=7, replica_groups=mesh['ctx'=32,'head'=4] {'ctx'}, use_global_device_ids=true, to_apply=%add.1 | all-reduce | flops 64 | bytes 512
  505.6 4.4 all-to-all-start.5
  513.2 9.6 %all-to-all-done.5 = bf16[2,512,512]{2,0,1:T(2,128)(2,1)} async-done(((bf16[2,512,512]{2,0,1:T(2,128)(2,1)}), bf16[2,512,512]{2,0,1:T(2,128)(2,1)}, u32[]{:S(2)}, u32[]{:S(2)}) %all-to-all-start.5) | async-done | bytes 1048608 | tf_op jit(solution)/shard_map/all_to_all | solution.py:210
  522.8 7.6 %all_to_all.196 = bf16[2,4,128]{2,0,1:T(2,128)(2,1)S(1)} all-to-all(bf16[2,4,128]{2,0,1:T(2,128)(2,1)S(1)} %fusion.53), channel_id=1, replica_groups=mesh['ctx'=32,'head'=4] {'head'}, dimensions={1} | all-to-all | bytes 4096 | tf_op jit(solution)/shard_map/all_to_all | solution.py:215
  530.3 3.2 all-to-all-start.10
  533.6 2.4 copy.104
  536.0 2.8 all-to-all-done.10
  538.7 4.1 all-to-all-start.8
  542.9 1.9 fusion.61
  545.3 2.0 copy.108
  547.3 3.7 all-to-all-done.8
  551.0 3.5 all-to-all-start.9
  555.4 2.4 copy.88
  557.8 1.9 copy.105
  559.7 5.7 all-to-all-done.9
  (316 shorter events, 123.9 us)
Async XLA Ops:
  7.2 9.7 %all-to-all-start = ((bf16[4,2,128]{2,1,0:T(2,128)(2,1)}), bf16[4,2,128]{2,1,0:T(2,128)(2,1)S(1)}, u32[]{:S(2)}, u32[]{:S(2)}) async-start(bf16[4,2,128]{2,1,0:T(2,128)(2,1)} %bitcast.253), calls=%async_computation | async-start | bytes 4096 | tf_op jit(solution)/shard_map/all_to_all | solution.py:154
  16.8 8.4 %all-to-all-start.1 = ((bf16[4,2,128]{2,1,0:T(2,128)(2,1)}), bf16[4,2,128]{2,1,0:T(2,128)(2,1)S(1)}, u32[]{:S(2)}, u32[]{:S(2)}) async-start(bf16[4,2,128]{2,1,0:T(2,128)(2,1)} %bitcast.254), calls=%async_computation.1 | async-start | bytes 4096 | tf_op jit(solution)/shard_map/all_to_all | solution.py:153
  25.2 11.5 %all-to-all-start.3 = ((bf16[8,128,256]{2,1,0:T(8,128)(2,1)}), bf16[8,128,256]{2,1,0:T(8,128)(2,1)S(1)}, u32[]{:S(2)}, u32[]{:S(2)}) async-start(bf16[8,128,256]{2,1,0:T(8,128)(2,1)} %param.14), calls=%async_computation.3 | async-start | bytes 1048576 | tf_op jit(solution)/shard_map/all_to_all | solution.py:151
  36.7 16.6 %copy-start.11 = (bf16[8,128,256]{2,1,0:T(8,128)(2,1)}, bf16[8,128,256]{2,1,0:T(8,128)(2,1)S(1)}, u32[]{:S(2)}) copy-start(bf16[8,128,256]{2,1,0:T(8,128)(2,1)S(1)} %all-to-all-done.3) | copy-start | bytes 1572868
  36.7 15.1 %all-to-all-start.4 = ((bf16[8,128,512]{2,1,0:T(8,128)(2,1)}), bf16[8,128,512]{2,1,0:T(8,128)(2,1)S(1)}, u32[]{:S(2)}, u32[]{:S(2)}) async-start(bf16[8,128,512]{2,1,0:T(8,128)(2,1)} %param.15), calls=%async_computation.4 | async-start | bytes 2097152 | tf_op jit(solution)/shard_map/all_to_all | solution.py:152
  40.3 130.8 %all-gather.11.cloned.1.call-start = ((), (), s32[]{:S(2)}) async-start(), calls=%async_computation.12 | async-start | bytes 34603008 | tf_op jit(solution)/shard_map/all_gather | solution.py:11
  41.4 120.3 %copy-start.18 = (f32[1,2,4,128]{3,1,2,0:T(2,128)}, f32[1,2,4,128]{3,1,2,0:T(2,128)S(1)}, u32[]{:S(2)}) copy-start(f32[1,2,4,128]{3,1,2,0:T(2,128)S(1)} %copy.164) | copy-start | bytes 12292
  41.7 120.0 %copy-start = (bf16[4,2,128,256]{3,2,0,1:T(8,128)(2,1)}, bf16[4,2,128,256]{3,2,0,1:T(8,128)(2,1)S(1)}, u32[]{:S(2)}) copy-start(bf16[4,2,128,256]{3,2,0,1:T(8,128)(2,1)S(1)} %copy.78) | copy-start | bytes 1572868
  54.8 5.9 %copy-start.20 = (u32[128]{0:T(128)S(1)}, u32[128]{0:T(128)}, u32[]{:S(2)}) copy-start(u32[128]{0:T(128)} %constant.102) | copy-start | bytes 1540
  56.5 11.5 %all-to-all-start.2 = ((bf16[8,128,256]{2,1,0:T(8,128)(2,1)}), bf16[8,128,256]{2,1,0:T(8,128)(2,1)S(1)}, u32[]{:S(2)}, u32[]{:S(2)}) async-start(bf16[8,128,256]{2,1,0:T(8,128)(2,1)} %param.13), calls=%async_computation.2 | async-start | bytes 1048576 | tf_op jit(solution)/shard_map/all_to_all | solution.py:150
  68.0 64.2 %copy-start.9 = (bf16[8,128,256]{2,1,0:T(8,128)(2,1)}, bf16[8,128,256]{2,1,0:T(8,128)(2,1)S(1)}, u32[]{:S(2)}) copy-start(bf16[8,128,256]{2,1,0:T(8,128)(2,1)S(1)} %all-to-all-done.2) | copy-start | bytes 1572868
  68.0 95.6 %all-to-all-start.6 = ((bf16[8,128,512]{2,1,0:T(8,128)(2,1)}), bf16[8,128,512]{2,1,0:T(8,128)(2,1)}, u32[]{:S(2)}, u32[]{:S(2)}) async-start(bf16[8,128,512]{2,1,0:T(8,128)(2,1)} %param.18), calls=%async_computation.6 | async-start | bytes 2097152 | tf_op jit(solution)/shard_map/all_to_all | solution.py:155
  72.3 272.1 %all-gather.13.cloned.1.call-start = ((), (), s32[]{:S(2)}) async-start(), calls=%async_computation.13 | async-start | bytes 34603008 | tf_op jit(solution)/shard_map/all_gather | solution.py:11
  72.5 91.1 %copy-start.19 = (f32[1,2,4,128]{3,1,2,0:T(2,128)}, f32[1,2,4,128]{3,1,2,0:T(2,128)S(1)}, u32[]{:S(2)}) copy-start(f32[1,2,4,128]{3,1,2,0:T(2,128)S(1)} %copy.163) | copy-start | bytes 12292
  133.3 94.9 %copy-start.6 = (bf16[4,2,128,256]{3,2,0,1:T(8,128)(2,1)}, bf16[4,2,128,256]{3,2,0,1:T(8,128)(2,1)S(1)}, u32[]{:S(2)}) copy-start(bf16[4,2,128,256]{3,2,0,1:T(8,128)(2,1)S(1)} %copy.77) | copy-start | bytes 1572868
  163.6 2.9 copy-start.14
  171.1 53.0 %copy-start.10 = (bf16[8,128,256]{2,1,0:T(8,128)(2,1)S(1)}, bf16[8,128,256]{2,1,0:T(8,128)(2,1)}, u32[]{:S(2)}) copy-start(bf16[8,128,256]{2,1,0:T(8,128)(2,1)} %copy-done.9) | copy-start | bytes 1572868
  228.2 1.0 copy-start.3
  256.9 2.4 copy-start.1
  259.3 2.6 copy-start.12
  259.3 1.6 copy-start.4
  259.3 1.7 copy-start.7
  259.4 1.7 copy-start.16
  261.9 9.0 %copy-start.8 = (bf16[4,2,128,256]{3,2,0,1:T(8,128)(2,1)S(1)}, bf16[4,2,128,256]{3,2,0,1:T(8,128)(2,1)}, u32[]{:S(2)}) copy-start(bf16[4,2,128,256]{3,2,0,1:T(8,128)(2,1)} %copy-done.6) | copy-start | bytes 1572868
  263.3 242.3 %all-to-all-start.7 = ((bf16[2,512,256]{2,0,1:T(2,128)(2,1)}), bf16[2,512,256]{2,0,1:T(2,128)(2,1)S(1)}, u32[]{:S(2)}, u32[]{:S(2)}) async-start(bf16[2,512,256]{2,0,1:T(2,128)(2,1)} %copy.96), calls=%async_computation.7 | async-start | bytes 1048576 | tf_op jit(solution)/shard_map/all_to_all | solution.py:211
  267.6 3.4 copy-start.13
  367.3 74.2 %copy-start.2 = (bf16[4,2,128,256]{3,2,0,1:T(8,128)(2,1)S(1)}, bf16[4,2,128,256]{3,2,0,1:T(8,128)(2,1)}, u32[]{:S(2)}) copy-start(bf16[4,2,128,256]{3,2,0,1:T(8,128)(2,1)} %copy-done) | copy-start | bytes 1572868
  444.2 65.9 %copy-start.15 = (f32[2]{0:T(128)S(1)}, f32[2]{0:T(128)}, u32[]{:S(2)}) copy-start(f32[2]{0:T(128)} %custom-call.4) | copy-start | bytes 28
  444.2 68.9 %copy-start.17 = (f32[1,2,4,128]{3,2,1,0:T(4,128)S(1)}, f32[1,2,4,128]{3,2,1,0:T(4,128)}, u32[]{:S(2)}) copy-start(f32[1,2,4,128]{3,2,1,0:T(4,128)} %fusion.46) | copy-start | bytes 12292
  505.6 37.3 %copy-start.5 = (bf16[2,512,512]{2,1,0:T(8,128)(2,1)S(1)}, bf16[2,512,512]{2,1,0:T(8,128)(2,1)}, u32[]{:S(2)}) copy-start(bf16[2,512,512]{2,1,0:T(8,128)(2,1)} %copy-done.3) | copy-start | bytes 3145732
  505.6 17.1 %all-to-all-start.5 = ((bf16[2,512,512]{2,0,1:T(2,128)(2,1)}), bf16[2,512,512]{2,0,1:T(2,128)(2,1)}, u32[]{:S(2)}, u32[]{:S(2)}) async-start(bf16[2,512,512]{2,0,1:T(2,128)(2,1)} %copy.87), calls=%async_computation.5 | async-start | bytes 2097152 | tf_op jit(solution)/shard_map/all_to_all | solution.py:210
  530.3 8.4 %all-to-all-start.10 = ((bf16[2,4,128]{2,0,1:T(2,128)(2,1)}), bf16[2,4,128]{2,0,1:T(2,128)(2,1)S(1)}, u32[]{:S(2)}, u32[]{:S(2)}) async-start(bf16[2,4,128]{2,0,1:T(2,128)(2,1)} %get-tuple-element.454), calls=%async_computation.10 | async-start | bytes 4096 | tf_op jit(solution)/shard_map/all_to_all | solution.py:214
  538.7 12.3 %all-to-all-start.8 = ((bf16[2,512,256]{2,0,1:T(2,128)(2,1)}), bf16[2,512,256]{2,0,1:T(2,128)(2,1)}, u32[]{:S(2)}, u32[]{:S(2)}) async-start(bf16[2,512,256]{2,0,1:T(2,128)(2,1)} %copy.104), calls=%async_computation.8 | async-start | bytes 1048576 | tf_op jit(solution)/shard_map/all_to_all | solution.py:212
  551.0 14.4 %all-to-all-start.9 = ((bf16[2,512,512]{2,0,1:T(2,128)(2,1)}), bf16[2,512,512]{2,0,1:T(2,128)(2,1)S(1)}, u32[]{:S(2)}, u32[]{:S(2)}) async-start(bf16[2,512,512]{2,0,1:T(2,128)(2,1)} %copy.108), calls=%async_computation.9 | async-start | bytes 2097152 | tf_op jit(solution)/shard_map/all_to_all | solution.py:213
Sparse Core Ops, SparseCore 0:
  56.6 114.3 all-gather.10
  231.0 113.3 all-gather.12
where the time goes:
time: 585 us; the launch traced here: 575 us
  blocking collectives  177 us (30%)
  waiting for transfers between devices  127 us (22%)
  other arithmetic  115 us (20%)
  local copies, waits for them, and re-layouts  74.1 us (13%)
  starting transfers between devices  42.1 us (7%)
  matrix products  21.7 us (4%)
  between operations  15.7 us (3%)
    unnamed x2, blocking collectives  120 us
    select_n x155, other arithmetic, hop(): jnp.where(position < mine, new, old)  105 us
    all_gather x2, waiting for transfers between devices, entering(): pieces = jax.tree.map(lambda part: lax.all_gather(part, axis), value)  74.3 us
    all_gather x2, blocking collectives, entering(): pieces = jax.tree.map(lambda part: lax.all_gather(part, axis), value)  49.5 us
    rev x4, local copies, waits for them, and re-layouts, entering(): pieces = jax.tree.map(lambda part: part[::-1], pieces)  23.5 us
    dot_general x12, matrix products, contract(): return jnp.einsum(form, left, right, preferred_element_type=jnp.float32)  21.7 us
    mul x62, local copies, waits for them, and re-layouts, combine_states(): latter[0][:, None, None] * earlier[1] + latter[1]  21.7 us
  transfers between devices with their start and end apart: 13, of which 11 were waited for; matrix products, arithmetic and copies ran while one was open for 25% of the time, Pallas kernels for 0%

commit v1 on v0

v1 whole, which is shorter than its diff:
```python
import functools

import jax
import jax.numpy as jnp
from jax import lax
from jax.experimental import pallas as pl
from jax.experimental.pallas import tpu as pltpu
from jax.sharding import PartitionSpec as P

f32, bf16 = jnp.float32, jnp.bfloat16
CHUNK, CHUNKS, TOKENS = 128, 4, 512
HEADS = 2
DK, DV = 256, 512
WIDE = DK + DV
EXTRA = 16
SLICES = 32
NEG = -1e30
SCALE = DK ** (-0.5)
ROWS = 256
VMEM = pltpu.VMEM
PARAMS = pltpu.CompilerParams(vmem_limit_bytes=56 * 1024 * 1024)


def dot(left, right, cl, cr, precision=None):
    return lax.dot_general(
        left, right, (((cl,), (cr,)), ((), ())), preferred_element_type=f32, precision=precision
    )


def exact(left, right):
    return dot(left, right, 1, 0, lax.Precision.HIGHEST)


def column(bundle, first):
    return jnp.concatenate([bundle[:, first + c : first + c + 1] for c in range(CHUNKS)], axis=0)


def line(bundle, first):
    return jnp.concatenate([bundle[first + c : first + c + 1, :] for c in range(CHUNKS)], axis=1)


def chunk_of(y, shift):
    return lax.rem(y + shift + CHUNKS, CHUNKS)


def smem():
    return pl.BlockSpec(memory_space=pltpu.SMEM)


def whole():
    return pl.BlockSpec(memory_space=VMEM)


def call(body, outs, ins, scratch=(), flops=0, grid_spec=None):
    size = lambda s: functools.reduce(lambda a, b: a * b, s.shape, 1) * s.dtype.itemsize
    args = dict(
        out_shape=outs,
        compiler_params=PARAMS,
        cost_estimate=pl.CostEstimate(
            flops=flops,
            bytes_accessed=sum(size(s) for s in list(ins) + list(outs)),
            transcendentals=0,
        ),
    )
    if grid_spec is not None:
        return pl.pallas_call(body, grid_spec=grid_spec, **args)(*ins)
    return pl.pallas_call(
        body,
        in_specs=[smem() if a.dtype == jnp.int32 and a.size <= 2 else whole() for a in ins],
        out_specs=tuple(whole() for _ in outs),
        scratch_shapes=scratch,
        **args,
    )(*ins)


def like(shape, dtype):
    return jax.ShapeDtypeStruct(shape, dtype)


def pack_body(gates, y_ref, a_ref, b_ref, *rest):
    outs = rest[-3:]
    y = y_ref[0]
    for shift, out in enumerate(outs, 1):
        dest = chunk_of(y, shift)
        for h in range(HEADS):
            out[h * CHUNK : (h + 1) * CHUNK, 0:DK] = a_ref[dest * HEADS + h]
            out[h * CHUNK : (h + 1) * CHUNK, DK:WIDE] = b_ref[dest * HEADS + h]
        if gates:
            both = jnp.concatenate([rest[0][...].astype(f32), rest[1][...].astype(f32)], axis=0)
            out[HEADS * CHUNK : HEADS * CHUNK + EXTRA, 0:CHUNK] = both.astype(bf16)


def pack(y, narrow, wide, gates=()):
    rows = HEADS * CHUNK + (EXTRA if gates else 0)
    return call(
        functools.partial(pack_body, bool(gates)),
        [like((rows, WIDE), bf16)] * 3,
        [y, narrow, wide, *gates],
    )


def assemble(all_ref, y, narrow_ref, wide_ref, received):
    for h in range(HEADS):
        all_ref[h, y, :, 0:DK] = narrow_ref[h]
        all_ref[h, y, :, DK:WIDE] = wide_ref[h]
    for shift, ref in enumerate(received, 1):
        source = chunk_of(y, -shift)
        for h in range(HEADS):
            all_ref[h, source] = ref[h * CHUNK : (h + 1) * CHUNK, :]


def update_body(
    y_ref, k_ref, v_ref, kv1, kv2, kv3, ig_ref, fg_ref, doc_ref, all_ref, line_ref, col_ref, pay_ref, gates, lines, extra
):
    y = y_ref[0]
    assemble(all_ref, y, k_ref, v_ref, (kv1, kv2, kv3))
    gates[y] = jnp.concatenate([ig_ref[...].astype(f32), fg_ref[...].astype(f32)], axis=0)
    for shift, ref in enumerate((kv1, kv2, kv3), 1):
        gates[chunk_of(y, -shift)] = ref[HEADS * CHUNK : HEADS * CHUNK + EXTRA, 0:CHUNK].astype(f32)
    row = lax.broadcasted_iota(jnp.int32, (16, CHUNK), 0)
    for c in range(CHUNKS):
        tile = gates[c]
        for h in range(HEADS):
            pick = y * HEADS + h
            lines[1, h * CHUNKS + c : h * CHUNKS + c + 1, :] = jnp.sum(
                jnp.where(row == pick, tile, 0.0), axis=0, keepdims=True
            )
            lines[0, h * CHUNKS + c : h * CHUNKS + c + 1, :] = jnp.sum(
                jnp.where(row == pick + 8, tile, 0.0), axis=0, keepdims=True
            )
    forget = lines[0, 0:8]
    fade = jnp.exp(-forget)
    lines[0, 0:8] = -jnp.log1p(fade)
    lines[0, 8:12] = doc_ref[...].astype(f32)
    lines[0, 12:16] = jnp.zeros((4, CHUNK), f32)
    closed = fade / (1.0 + fade)
    before = lax.broadcasted_iota(jnp.int32, (CHUNK, CHUNK), 0)
    after = lax.broadcasted_iota(jnp.int32, (CHUNK, CHUNK), 1)
    total = exact(lines[0], (before <= after).astype(f32))
    whole_lines = []
    for group in range(3):
        run = jnp.zeros((1, 1), f32)
        for c in range(CHUNKS):
            here = total[group * CHUNKS + c : group * CHUNKS + c + 1, :]
            whole_lines.append(here + run)
            run = run + here[:, CHUNK - 1 : CHUNK]
    segment = jnp.concatenate(whole_lines[8:12], axis=0)
    segment_end = segment[3:4, CHUNK - 1 : CHUNK]
    extra[...] = jnp.zeros_like(extra)
    for h in range(HEADS):
        cumulative = jnp.concatenate(whole_lines[h * CHUNKS : (h + 1) * CHUNKS], axis=0)
        end = cumulative[3:4, CHUNK - 1 : CHUNK]
        ingate = lines[1, h * CHUNKS : (h + 1) * CHUNKS]
        line_ref[h] = jnp.zeros((CHUNK, CHUNK), f32)
        line_ref[h, 0:4] = cumulative
        line_ref[h, 4:8] = ingate - cumulative
        line_ref[h, 8:12] = jnp.where(segment == segment_end, jnp.exp(end - cumulative + ingate), 0.0)
        line_ref[h, 12:16] = jnp.where(segment == 0.0, jnp.exp(cumulative), 0.0)
        line_ref[h, 16:20] = segment
        line_ref[h, 20:24] = closed[h * CHUNKS : (h + 1) * CHUNKS]
        col_ref[h] = line_ref[h].T
        decay = jnp.where(segment_end == 0.0, jnp.exp(end), 0.0)
        keys = all_ref[h, :, :, 0:DK].reshape(TOKENS, DK)
        values = all_ref[h, :, :, DK:WIDE].reshape(TOKENS, DV)
        keys_alpha = (column(col_ref[h], 8) * keys.astype(f32)).astype(bf16)
        update = dot(keys_alpha, values, 0, 0).astype(bf16)
        scatter(pay_ref, update, h)
        update_n = jnp.sum(keys_alpha.astype(f32), axis=0, keepdims=True)
        for half in range(2):
            extra[2 * h + half : 2 * h + half + 1, :] = update_n[:, half * CHUNK : (half + 1) * CHUNK]
            extra[4 + 2 * h + half : 5 + 2 * h + half, :] = jnp.broadcast_to(decay, (1, CHUNK))
    high = extra[...].astype(bf16)
    low = extra[...] - high.astype(f32)
    tile = jnp.concatenate([high.astype(f32), low], axis=0).astype(bf16)
    for i in range(SLICES):
        pay_ref[i, :, 2 * DK : 2 * DK + CHUNK] = tile


def scatter(pay_ref, matrix, h):
    for i in range(SLICES):
        r, c = i // 2, i % 2
        pay_ref[i, :, h * DK : (h + 1) * DK] = matrix[16 * r : 16 * (r + 1), DK * c : DK * (c + 1)]


def collect(matrix_ref, pay_ref, h):
    for i in range(SLICES):
        r, c = i // 2, i % 2
        matrix_ref[h, 16 * r : 16 * (r + 1), DK * c : DK * (c + 1)] = pay_ref[i, :, h * DK : (h + 1) * DK]


def spread(extra):
    return jnp.concatenate([extra[4 + r : 5 + r, :] for r in range(4)], axis=1)


def state_scan_body(n_ctx, me_ref, in_ref, out_ref, norm_ref, extra_ref):
    mine = SLICES // n_ctx
    me = me_ref[0]
    state = jnp.zeros((mine, 16, 2 * DK), f32)
    norm = jnp.zeros((4, CHUNK), f32)
    for j in range(n_ctx):
        block = in_ref[j * mine : (j + 1) * mine, :, 0 : 2 * DK]
        tile = in_ref[j * mine, :, 2 * DK : 2 * DK + CHUNK].astype(f32)
        extra = tile[0:8] + tile[8:16]
        extra_ref[j] = extra
        out_ref[j * mine : (j + 1) * mine] = state.astype(bf16)
        state = spread(extra) * state + block.astype(f32)
        norm = jnp.where(j < me, extra[4:8] * norm + extra[0:4], norm)
    norm_ref[...] = jnp.concatenate([norm, jnp.zeros((4, CHUNK), f32)], axis=0)


def back_scan_body(n_ctx, in_ref, extra_ref, out_ref):
    mine = SLICES // n_ctx
    back = jnp.zeros((mine, 16, 2 * DK), f32)
    for j in reversed(range(n_ctx)):
        block = in_ref[j * mine : (j + 1) * mine]
        out_ref[j * mine : (j + 1) * mine] = back.astype(bf16)
        back = spread(extra_ref[j]) * back + block.astype(f32)


def weights(line_ref, col_ref, h, r):
    last = (r + 1) * ROWS
    here = slice(r * ROWS, last)
    position = lax.broadcasted_iota(jnp.int32, (ROWS, last), 0) + r * ROWS
    source = lax.broadcasted_iota(jnp.int32, (ROWS, last), 1)
    log_weight = column(col_ref[h], 0)[here] + line(line_ref[h], 4)[:, 0:last]
    allowed = (position >= source) & (column(col_ref[h], 16)[here] == line(line_ref[h], 16)[:, 0:last])
    return jnp.exp(jnp.where(allowed, log_weight, NEG))


def put_column(ref, h, first, value):
    for c in range(CHUNKS):
        ref[h, :, first + c : first + c + 1] = value[c * CHUNK : (c + 1) * CHUNK]


def norm_line(norm_ref, h):
    both = [norm_ref[2 * h + half : 2 * h + half + 1, :] for half in range(2)]
    return jnp.concatenate(both, axis=1).astype(bf16).astype(f32)


def adjoint_body(
    y_ref, q_ref, g_ref, qg1, qg2, qg3, kv_ref, line_ref, col_ref, norm_ref, all_ref, pair_ref, num_ref, cols_ref, pay_ref
):
    assemble(all_ref, y_ref[0], q_ref, g_ref, (qg1, qg2, qg3))
    for h in range(HEADS):
        cols_ref[h] = jnp.zeros((CHUNK, CHUNK), f32)
        keys = kv_ref[h, :, :, 0:DK].reshape(TOKENS, DK)
        query = all_ref[h, :, :, 0:DK].reshape(TOKENS, DK)
        sums = []
        for r in range(TOKENS // ROWS):
            last = (r + 1) * ROWS
            scores = dot(query[r * ROWS : last], keys[0:last], 1, 1) * SCALE
            pair = (weights(line_ref, col_ref, h, r) * scores).astype(bf16)
            pair_ref[h, r * ROWS : last, 0:last] = pair
            if last < TOKENS:
                pair_ref[h, r * ROWS : last, last:TOKENS] = jnp.zeros((ROWS, TOKENS - last), bf16)
            sums.append(jnp.sum(pair.astype(f32), axis=1, keepdims=True))
        beta = column(col_ref[h], 12)
        wide_query = query.astype(f32)
        cross = jnp.sum(wide_query * norm_line(norm_ref, h), axis=1, keepdims=True)
        denominator = jnp.concatenate(sums, axis=0) + beta * cross * SCALE
        norm = jnp.sqrt(denominator * denominator + 1.0)
        put_column(cols_ref, h, 0, denominator)
        put_column(cols_ref, h, 4, norm)
        grad = all_ref[h, :, :, DK:WIDE].reshape(TOKENS, DV).astype(f32)
        num_grad = (grad / norm).astype(bf16)
        num_ref[h] = num_grad
        query_beta = (beta * wide_query * SCALE).astype(bf16)
        scatter(pay_ref, dot(query_beta, num_grad, 0, 0).astype(bf16), h)


def hidden_body(
    y_ref, kv_ref, qg_ref, pair_ref, num_ref, line_ref, col_ref, norm_ref, cols_ref, in_ref, o0, o1, o2, o3, score_ref, terms_ref, adjoint_ref, state, done
):
    y = y_ref[0]
    adjoint = []
    for h in range(HEADS):
        collect(state, in_ref, h)
        state_bf = state[h]
        terms_ref[h] = jnp.zeros((CHUNK, CHUNK), f32)
        keys = kv_ref[h, :, :, 0:DK].reshape(TOKENS, DK)
        values = kv_ref[h, :, :, DK:WIDE].reshape(TOKENS, DV)
        query = qg_ref[h, :, :, 0:DK].reshape(TOKENS, DK)
        grad = qg_ref[h, :, :, DK:WIDE].reshape(TOKENS, DV)
        beta = column(col_ref[h], 12)
        denominator = column(cols_ref[h], 0)
        norm = column(cols_ref[h], 4)
        norm_bf = norm_line(norm_ref, h)
        total = jnp.zeros((1, DK), f32)
        rows = []
        for r in range(TOKENS // ROWS):
            last = (r + 1) * ROWS
            here = slice(r * ROWS, last)
            cross = dot(query[here], state_bf, 1, 0)
            numerator = dot(pair_ref[h, here, 0:last], values[0:last], 1, 0) + beta[here] * cross * SCALE
            hidden = numerator / norm[here]
            done[here, 0:DV] = hidden.astype(bf16)
            inner = jnp.sum(grad[here].astype(f32) * hidden, axis=1, keepdims=True)
            den_grad = -inner * denominator[here] / (norm[here] * norm[here])
            wide_query = query[here].astype(f32)
            query_beta = (beta[here] * wide_query * SCALE).astype(bf16).astype(f32)
            total = total + jnp.sum(query_beta * den_grad, axis=0, keepdims=True)
            num_grad = num_ref[h, here]
            pair_grad = dot(num_grad, values[0:last], 1, 1) + den_grad
            score = (weights(line_ref, col_ref, h, r) * pair_grad).astype(bf16)
            score_ref[h, here, 0:last] = score
            if last < TOKENS:
                score_ref[h, here, last:TOKENS] = jnp.zeros((ROWS, TOKENS - last), bf16)
            from_state = dot(num_grad, state_bf, 1, 1) + den_grad * norm_bf
            query_grad = dot(score, keys[0:last], 1, 0) * SCALE + beta[here] * from_state * SCALE
            done[here, DV : DV + DK] = query_grad.astype(bf16)
            rows.append(jnp.sum(wide_query * query_grad, axis=1, keepdims=True))
        put_column(terms_ref, h, 0, jnp.concatenate(rows, axis=0))
        adjoint += [total[:, 0:CHUNK], total[:, CHUNK:DK]]
        send(done, y, h, (o0, o1, o2, o3))
    adjoint = jnp.concatenate(adjoint + [jnp.zeros((4, CHUNK), f32)], axis=0)
    for i in range(adjoint_ref.shape[0]):
        adjoint_ref[i] = adjoint


def send(done, y, h, outs):
    for shift, out in enumerate(outs):
        first = pl.multiple_of(chunk_of(y, shift) * CHUNK, CHUNK)
        out[h * CHUNK : (h + 1) * CHUNK, :] = done[pl.ds(first, CHUNK), :]


def local_body(qg_ref, pair_ref, num_ref, score_ref, key_ref, value_ref):
    for h in range(HEADS):
        query = qg_ref[h, :, :, 0:DK].reshape(TOKENS, DK)
        for s in range(TOKENS // ROWS):
            here = slice(s * ROWS, (s + 1) * ROWS)
            first = s * ROWS
            key_ref[h, here] = dot(score_ref[h, first:TOKENS, here], query[first:TOKENS], 0, 0) * SCALE
            value_ref[h, here] = dot(pair_ref[h, first:TOKENS, here], num_ref[h, first:TOKENS], 0, 0)


def grads_body(
    n_ctx, y_ref, me_ref, kv_ref, key_ref, value_ref, line_ref, col_ref, terms_ref, state_ref, pay_ref, back_ref, norm_ref, extra_ref, adjoint_ref, o0, o1, o2, o3, back, done, cols
):
    y, me = y_ref[0], me_ref[0]
    norm = jnp.zeros((4, CHUNK), f32)
    for j in reversed(range(n_ctx)):
        norm = jnp.where(j > me, extra_ref[j][4:8] * norm + adjoint_ref[j][0:4], norm)
    back_n = norm.astype(bf16).astype(f32)
    extra = extra_ref[me]
    state_n = norm_ref[0:4, :].astype(bf16).astype(f32)
    later_n = (extra[4:8] * state_n + extra[0:4]) * back_n
    decay = spread(extra)
    later = jnp.zeros((16, 2 * DK), f32)
    for i in range(SLICES):
        state = decay * state_ref[i].astype(f32) + pay_ref[i, :, 0 : 2 * DK].astype(f32)
        later = later + state * back_ref[i].astype(f32)
    cols[...] = jnp.zeros_like(cols)
    for h in range(HEADS):
        collect(back, back_ref, h)
        back_bf = back[h]
        keys = kv_ref[h, :, :, 0:DK].reshape(TOKENS, DK)
        values = kv_ref[h, :, :, DK:WIDE].reshape(TOKENS, DV)
        alpha = column(col_ref[h], 8)
        row = jnp.concatenate([back_n[2 * h : 2 * h + 1], back_n[2 * h + 1 : 2 * h + 2]], axis=1)
        key_grad = key_ref[h] + alpha * (dot(values, back_bf, 1, 1) + row)
        value_grad = value_ref[h] + alpha * dot(keys, back_bf, 1, 0)
        done[:, 0:DV] = value_grad.astype(bf16)
        done[:, DV : DV + DK] = key_grad.astype(bf16)
        send(done, y, h, (o0, o1, o2, o3))
        key_term = jnp.sum(keys.astype(f32) * key_grad, axis=1, keepdims=True)
        for c in range(CHUNKS):
            piece = key_term[c * CHUNK : (c + 1) * CHUNK]
            cols[:, h * 4 + c : h * 4 + c + 1] = terms_ref[h, :, c : c + 1] - piece
            cols[:, 8 + h * 4 + c : 9 + h * 4 + c] = piece
    lines = cols[...].T[0:16]
    before = lax.broadcasted_iota(jnp.int32, (CHUNK, CHUNK), 0)
    after = lax.broadcasted_iota(jnp.int32, (CHUNK, CHUNK), 1)
    suffix = exact(lines, (before >= after).astype(f32))
    tiles = [[None] * HEADS for _ in range(CHUNKS)]
    for h in range(HEADS):
        run = jnp.sum(later[:, h * DK : (h + 1) * DK], keepdims=True) + jnp.sum(
            later_n[2 * h : 2 * h + 2], keepdims=True
        )
        for c in reversed(range(CHUNKS)):
            here = suffix[h * 4 + c : h * 4 + c + 1]
            tiles[c][h] = (here + run) * line_ref[h, 20 + c : 21 + c]
            run = run + here[:, 0:1]
    gates = jnp.zeros((CHUNKS, 16, CHUNK), f32)
    for c in range(CHUNKS):
        rows = [lines[8 + h * 4 + c : 9 + h * 4 + c] for h in range(HEADS)] + tiles[c]
        cols[c * 16 : (c + 1) * 16, :] = jnp.concatenate(rows + [jnp.zeros((12, CHUNK), f32)], axis=0)
    for shift, out in enumerate((o0, o1, o2, o3)):
        first = pl.multiple_of(chunk_of(y, shift) * 16, 16)
        out[HEADS * CHUNK : HEADS * CHUNK + EXTRA, 0:CHUNK] = cols[pl.ds(first, 16), :].astype(bf16)


def unpack_body(gates, y_ref, r0, r1, r2, r3, wide_ref, narrow_ref, *gate_refs):
    y = y_ref[0]
    row = lax.broadcasted_iota(jnp.int32, (8, CHUNK), 0)
    sums = [jnp.zeros((8, CHUNK), f32)] * 2
    for shift, ref in enumerate((r0, r1, r2, r3)):
        source = chunk_of(y, -shift)
        for h in range(HEADS):
            wide_ref[source * HEADS + h] = ref[h * CHUNK : (h + 1) * CHUNK, 0:DV]
            narrow_ref[source * HEADS + h] = ref[h * CHUNK : (h + 1) * CHUNK, DV : DV + DK]
        if gates:
            tile = ref[HEADS * CHUNK : HEADS * CHUNK + EXTRA, 0:CHUNK].astype(f32)
            for k in range(2):
                for h in range(HEADS):
                    here = jnp.where(row == source * HEADS + h, tile[2 * k + h : 2 * k + h + 1], 0.0)
                    sums[k] = sums[k] + here
    if gates:
        gate_refs[0][...] = sums[0].astype(bf16)
        gate_refs[1][...] = sums[1].astype(bf16)


def unpack(y, parts, gates):
    outs = [like((CHUNKS * HEADS, CHUNK, DV), bf16), like((CHUNKS * HEADS, CHUNK, DK), bf16)]
    if gates:
        outs += [like((CHUNKS * HEADS, CHUNK), bf16)] * 2
    return call(functools.partial(unpack_body, gates), outs, [y, *parts])


def shift_all(parts):
    moved = []
    for shift, part in enumerate(parts, 1):
        pairs = [(i, (i + shift) % CHUNKS) for i in range(CHUNKS)]
        moved.append(lax.ppermute(part, "head", pairs))
    return moved


def own(narrow, wide, y):
    return [lax.dynamic_slice_in_dim(part, y * HEADS, HEADS, 0) for part in (narrow, wide)]


def exchange(part):
    return lax.all_to_all(part, "ctx", split_axis=0, concat_axis=0, tiled=True)


def shards(query, keys, values, igate, fgate, hidden_output_gradient, doc_start):
    n_ctx = lax.axis_size("ctx")
    pair_flops = TOKENS * TOKENS * HEADS * 2
    y_index = lax.axis_index("head").astype(jnp.int32)
    y = y_index.reshape(1)
    me = lax.axis_index("ctx").astype(jnp.int32).reshape(1)
    kv_sent = pack(y, keys, values, (igate, fgate))
    qg_sent = pack(y, query, hidden_output_gradient)
    kv_received = shift_all(kv_sent)
    qg_received = shift_all(qg_sent)
    tokens = (HEADS, CHUNKS, CHUNK, WIDE)
    bundle = like((HEADS, CHUNK, CHUNK), f32)
    kv, lines, cols, payload = call(
        update_body,
        [like(tokens, bf16), bundle, bundle, like((SLICES, 16, 2 * DK + CHUNK), bf16)],
        [y, *own(keys, values, y_index), *kv_received, igate, fgate, doc_start.reshape(CHUNKS, CHUNK)],
        [VMEM((CHUNKS, 16, CHUNK), f32), VMEM((2, 16, CHUNK), f32), VMEM((8, CHUNK), f32)],
        flops=TOKENS * DK * DV * HEADS * 2,
    )
    part = like((SLICES, 16, 2 * DK), bf16)
    state_part, norm, extra = call(
        functools.partial(state_scan_body, n_ctx),
        [part, like((8, CHUNK), f32), like((n_ctx, 8, CHUNK), f32)],
        [me, exchange(payload)],
    )
    state = exchange(state_part)
    square = like((HEADS, TOKENS, TOKENS), bf16)
    qg, pair, num_grad, norm_cols, adjoint = call(
        adjoint_body,
        [like(tokens, bf16), square, like((HEADS, TOKENS, DV), bf16), bundle, part],
        [y, *own(query, hidden_output_gradient, y_index), *qg_received, kv, lines, cols, norm],
        flops=pair_flops * DK + TOKENS * DK * DV * HEADS * 2,
    )
    (back_part,) = call(
        functools.partial(back_scan_body, n_ctx), [part], [exchange(adjoint), extra]
    )
    back = exchange(back_part)
    plain = like((HEADS * CHUNK, WIDE), bf16)
    *hidden_sent, score_grad, terms, adjoint_n = call(
        hidden_body,
        [plain] * 4 + [square, bundle, like((n_ctx, 8, CHUNK), f32)],
        [y, kv, qg, pair, num_grad, lines, cols, norm, norm_cols, state],
        [VMEM((HEADS, DK, DV), bf16), VMEM((TOKENS, WIDE), bf16)],
        flops=pair_flops * (DV + DV + DK) + 2 * TOKENS * DK * DV * HEADS * 2,
    )
    hidden_received = shift_all(hidden_sent[1:])
    adjoint_all = exchange(adjoint_n)
    key_grad, value_grad = call(
        local_body,
        [like((HEADS, TOKENS, DK), f32), like((HEADS, TOKENS, DV), f32)],
        [qg, pair, num_grad, score_grad],
        flops=pair_flops * (DK + DV),
    )
    grads_sent = call(
        functools.partial(grads_body, n_ctx),
        [like((HEADS * CHUNK + EXTRA, WIDE), bf16)] * 4,
        [y, me, kv, key_grad, value_grad, lines, cols, terms, state, payload, back, norm, extra, adjoint_all],
        [VMEM((HEADS, DK, DV), bf16), VMEM((TOKENS, WIDE), bf16), VMEM((CHUNK, CHUNK), f32)],
        flops=2 * TOKENS * DK * DV * HEADS * 2,
    )
    grads_received = shift_all(grads_sent[1:])
    hidden_home, query_home = unpack(y, [hidden_sent[0], *hidden_received], False)
    value_home, key_home, input_home, forget_home = unpack(y, [grads_sent[0], *grads_received], True)
    return (hidden_home, query_home, key_home, value_home, input_home, forget_home)


def solution(mesh):
    spec = P(None, ("ctx", "head"), None)
    flat = P(None, ("ctx", "head"))
    return jax.shard_map(
        shards,
        mesh=mesh,
        in_specs=(spec, spec, spec, flat, flat, spec, P("ctx")),
        out_specs=(spec, spec, spec, spec, flat, flat),
        check_vma=False,
    )
```

time: 585 us -> 192 us (0.33); the launches traced: 575 us -> 190 us
  blocking collectives: 177 us -> 0 us
  other arithmetic: 115 us -> 0 us
  local copies, waits for them, and re-layouts: 74.1 us -> 11.6 us
  waiting for transfers between devices: 127 us -> 80.1 us
  Pallas kernels: 0 us -> 44.1 us
  matrix products: 21.7 us -> 0 us
  between operations: 15.7 us -> 0.78 us
  starting transfers between devices: 42.1 us -> 53.9 us
    unnamed x2 -> x0, blocking collectives: 120 us -> none
    select_n x157 -> x0, other arithmetic: 106 us -> none  [the longest x155 105 us: hop(): jnp.where(position < mine, new, old)]
    all_gather x2 -> x0, waiting for transfers between devices: 74.3 us -> none  [entering(): pieces = jax.tree.map(lambda part: lax.all_gather(part, axis), value)]
    ppermute x0 -> x12, waiting for transfers between devices: none -> 58.2 us  [shift_all(): moved.append(lax.ppermute(part, 'head', pairs))]
    all_gather x2 -> x0, blocking collectives: 49.5 us -> none  [entering(): pieces = jax.tree.map(lambda part: lax.all_gather(part, axis), value)]
    pallas_call x0 -> x11, Pallas kernels: none -> 44.1 us  [call(): pl.pallas_call(body, in_specs=[smem() if a.dtype == jnp.int32 and a.size...]
    all_to_all x11 -> x5, waiting for transfers between devices: 53 us -> 21.9 us  [exchange(): return lax.all_to_all(part, 'ctx', split_axis=0, concat_axis=0, tiled=True)]
    rev x6 -> x0, local copies, waits for them, and re-layouts: 24.2 us -> none  [the longest x4 23.5 us: entering(): pieces = jax.tree.map(lambda part: part[::-1], pieces)]
  transfers between devices with their start and end apart: 13 -> 17, of which waited for: 11 -> 11; matrix products, arithmetic and copies ran while one was open for 25% -> 3% of each run, Pallas kernels for 0% -> 17%
where the time goes in v1:
time: 192 us; the launch traced here: 190 us
  waiting for transfers between devices  80.1 us (42%)
  starting transfers between devices  53.9 us (28%)
  Pallas kernels  44.1 us (23%)
  local copies, waits for them, and re-layouts  11.6 us (6%)
    ppermute x12, waiting for transfers between devices, shift_all(): moved.append(lax.ppermute(part, 'head', pairs))  58.2 us
    pallas_call x11, Pallas kernels, call(): pl.pallas_call(body, in_specs=[smem() if a.dtype == jnp.int32 and a.size...  44.1 us
    all_to_all x5, starting transfers between devices, exchange(): return lax.all_to_all(part, 'ctx', split_axis=0, concat_axis=0, tiled=True)  32.3 us
    all_to_all x5, waiting for transfers between devices, exchange(): return lax.all_to_all(part, 'ctx', split_axis=0, concat_axis=0, tiled=True)  21.9 us
    ppermute x12, starting transfers between devices, shift_all(): moved.append(lax.ppermute(part, 'head', pairs))  21.6 us
    dynamic_slice x4, local copies, waits for them, and re-layouts, own(): lax.dynamic_slice_in_dim(part, y * HEADS, HEADS, 0)  6.48 us
    unnamed x40, local copies, waits for them, and re-layouts  5.11 us
  transfers between devices with their start and end apart: 17, of which 11 were waited for; matrix products, arithmetic and copies ran while one was open for 3% of the time, Pallas kernels for 17%

profile of v1, /device:TPU:2, one launch (start us, length us, event | category | flops | bytes accessed | tf_op | source)
XLA Modules:
  0.0 190.5 jit_solution(375918826463010033)
XLA Ops:
  0.6 2.5 %shard_map.118 = (bf16[272,768]{1,0:T(8,128)(2,1)}, bf16[272,768]{1,0:T(8,128)(2,1)}, bf16[272,768]{1,0:T(8,128)(2,1)}) custom-call(s32[1]{0:T(128)} %bitcast.y_ref, bf16[8,128,256]{2,1,0:T(8,128)(2,1)} %a_ref.2, bf16[8,128,512]{2,1,0:T(8,128)(2,1)} %b_ref.2, bf16[8,128]{1,0:T(8,128)(2,1)} %ig_ref.1, bf16[8,128]{1,0:T(8,128)(2,1)} %fg_ref.1), custom_call_target="tpu_custom_call" | custom-call | bytes 2830340 | tf_op jit(solution)/shard_map/pallas_call | solution.py:67
  3.1 1.6 collective-permute-start
  4.7 2.9 %collective-permute-start.1 = (bf16[272,768]{1,0:T(8,128)(2,1)}, bf16[272,768]{1,0:T(8,128)(2,1)S(1)}, u32[]{:S(2)}, u32[]{:S(2)}) collective-permute-start(bf16[272,768]{1,0:T(8,128)(2,1)} %get-tuple-element.44), channel_id=1, source_target_pairs={{0,2},{1,3},{2,0},{3,1},{4,6},{5,7},{6,4},{7,5},{8,10},{9,11},{10,... | collective-permute-start | bytes 1253384 | tf_op jit(solution)/shard_map/ppermute | solution.py:423
  7.6 1.3 collective-permute-start.2
  8.9 1.6 constant_dynamic-slice_fusion.3.k_ref
  10.5 1.7 constant_dynamic-slice_fusion.2.v_ref
  12.2 3.8 %collective-permute-done.kv1 = bf16[272,768]{1,0:T(8,128)(2,1)S(1)} collective-permute-done((bf16[272,768]{1,0:T(8,128)(2,1)}, bf16[272,768]{1,0:T(8,128)(2,1)S(1)}, u32[]{:S(2)}, u32[]{:S(2)}) %collective-permute-start) | collective-permute-done | bytes 417824 | tf_op jit(solution)/shard_map/ppermute | solution.py:423
  16.0 10.1 %collective-permute-done.1.kv2 = bf16[272,768]{1,0:T(8,128)(2,1)S(1)} collective-permute-done((bf16[272,768]{1,0:T(8,128)(2,1)}, bf16[272,768]{1,0:T(8,128)(2,1)S(1)}, u32[]{:S(2)}, u32[]{:S(2)}) %collective-permute-start.1) | collective-permute-done | bytes 417824 | tf_op jit(solution)/shard_map/ppermute | solution.py:423
  26.1 0.0 collective-permute-done.2.kv3
  26.1 0.0 copy-done.8
  26.1 0.7 copy-done.9
  26.9 0.1 copy-done.10
  27.0 3.8 %shard_map.119 = (bf16[2,4,128,768]{3,2,1,0:T(8,128)(2,1)}, f32[2,128,128]{2,1,0:T(8,128)}, f32[2,128,128]{2,1,0:T(8,128)}, bf16[32,16,640]{2,1,0:T(8,128)(2,1)}) custom-call(s32[1]{0:T(128)} %bitcast.y_ref, bf16[2,128,256]{2,1,0:T(8,128)(2,1)} %constant_dynamic-slice_fusion.3.k_ref, bf16[2,128,512]{2,1,0:T(8,128)(2,1)} %constant_dynamic-slice_fusion.2.v_ref, ...), custom_call_target="tpu_custom_call" | custom-call | flops 268435456 | bytes 4143108 | tf_op jit(solution)/shard_map/pallas_call | solution.py:67
  30.8 8.5 %all-to-all-start = ((bf16[32,16,640]{2,1,0:T(8,128)(2,1)}), bf16[32,16,640]{2,1,0:T(8,128)(2,1)S(1)}, u32[]{:S(2)}, u32[]{:S(2)}) async-start(bf16[32,16,640]{2,1,0:T(8,128)(2,1)} %get-tuple-element.52.pay_ref), calls=%async_computation | async-start | bytes 1310720 | tf_op jit(solution)/shard_map/all_to_all | solution.py:432
  39.2 11.9 %all-to-all-done.in_ref = bf16[32,16,640]{2,1,0:T(8,128)(2,1)S(1)} async-done(((bf16[32,16,640]{2,1,0:T(8,128)(2,1)}), bf16[32,16,640]{2,1,0:T(8,128)(2,1)S(1)}, u32[]{:S(2)}, u32[]{:S(2)}) %all-to-all-start) | async-done | bytes 655392 | tf_op jit(solution)/shard_map/all_to_all | solution.py:432
  51.1 0.8 copy-done
  52.0 2.1 %shard_map.121 = (bf16[32,16,512]{2,1,0:T(8,128)(2,1)}, f32[8,128]{1,0:T(8,128)}, f32[32,8,128]{2,1,0:T(8,128)}) custom-call(s32[1]{0:T(128)} %bitcast.2.me_ref, bf16[32,16,640]{2,1,0:T(8,128)(2,1)} %copy-done), custom_call_target="tpu_custom_call" | custom-call | bytes 1314820 | tf_op jit(solution)/shard_map/pallas_call | solution.py:67
  54.0 5.1 %all-to-all-start.1 = ((bf16[32,16,512]{2,1,0:T(8,128)(2,1)}), bf16[32,16,512]{2,1,0:T(8,128)(2,1)S(1)}, u32[]{:S(2)}, u32[]{:S(2)}) async-start(bf16[32,16,512]{2,1,0:T(8,128)(2,1)} %get-tuple-element.58), calls=%async_computation.1 | async-start | bytes 1048576 | tf_op jit(solution)/shard_map/all_to_all | solution.py:432
  59.2 2.5 %shard_map.120 = (bf16[256,768]{1,0:T(8,128)(2,1)}, bf16[256,768]{1,0:T(8,128)(2,1)}, bf16[256,768]{1,0:T(8,128)(2,1)}) custom-call(s32[1]{0:T(128)} %bitcast.y_ref, bf16[8,128,256]{2,1,0:T(8,128)(2,1)} %a_ref.3, bf16[8,128,512]{2,1,0:T(8,128)(2,1)} %b_ref.3), custom_call_target="tpu_custom_call" | custom-call | bytes 2752516 | tf_op jit(solution)/shard_map/pallas_call | solution.py:67
  61.6 1.0 collective-permute-start.3
  62.6 2.4 %collective-permute-start.4 = (bf16[256,768]{1,0:T(8,128)(2,1)}, bf16[256,768]{1,0:T(8,128)(2,1)S(1)}, u32[]{:S(2)}, u32[]{:S(2)}) collective-permute-start(bf16[256,768]{1,0:T(8,128)(2,1)} %get-tuple-element.48), channel_id=1, source_target_pairs={{0,2},{1,3},{2,0},{3,1},{4,6},{5,7},{6,4},{7,5},{8,10},{9,11},{10,... | collective-permute-start | bytes 1179656 | tf_op jit(solution)/shard_map/ppermute | solution.py:423
  65.0 1.7 collective-permute-start.5
  66.7 1.6 constant_dynamic-slice_fusion.1.q_ref
  68.3 1.7 constant_dynamic-slice_fusion.g_ref
  69.9 4.9 %collective-permute-done.3.qg1 = bf16[256,768]{1,0:T(8,128)(2,1)S(1)} collective-permute-done((bf16[256,768]{1,0:T(8,128)(2,1)}, bf16[256,768]{1,0:T(8,128)(2,1)S(1)}, u32[]{:S(2)}, u32[]{:S(2)}) %collective-permute-start.3) | collective-permute-done | bytes 393248 | tf_op jit(solution)/shard_map/ppermute | solution.py:423
  74.8 8.0 %collective-permute-done.4.qg2 = bf16[256,768]{1,0:T(8,128)(2,1)S(1)} collective-permute-done((bf16[256,768]{1,0:T(8,128)(2,1)}, bf16[256,768]{1,0:T(8,128)(2,1)S(1)}, u32[]{:S(2)}, u32[]{:S(2)}) %collective-permute-start.4) | collective-permute-done | bytes 393248 | tf_op jit(solution)/shard_map/ppermute | solution.py:423
  82.8 0.5 collective-permute-done.5.qg3
  83.3 0.0 copy-done.14
  83.3 0.3 copy-done.15
  83.6 0.4 copy-done.16
  84.0 6.2 %shard_map.122 = (bf16[2,4,128,768]{3,2,1,0:T(8,128)(2,1)}, bf16[2,512,512]{2,1,0:T(8,128)(2,1)}, bf16[2,512,512]{2,1,0:T(8,128)(2,1)}, f32[2,128,128]{2,1,0:T(8,128)}, bf16[32,16,512]{2,1,0:T(8,128)(2,1)}) custom-call(s32[1]{0:T(128)} %bitcast.y_ref, bf16[2,128,256]{2,1,0:T(8,128)(2,1)} %constant_dynamic-slice_fusion.1.q_ref, ...), custom_call_target="tpu_custom_call" | custom-call | flops 536870912 | bytes 7737348 | tf_op jit(solution)/shard_map/pallas_call | solution.py:67
  90.2 0.0 all-to-all-done.1.in_ref.state_ref
  90.2 7.5 %all-to-all-start.2 = ((bf16[32,16,512]{2,1,0:T(8,128)(2,1)}), bf16[32,16,512]{2,1,0:T(8,128)(2,1)S(1)}, u32[]{:S(2)}, u32[]{:S(2)}) async-start(bf16[32,16,512]{2,1,0:T(8,128)(2,1)} %get-tuple-element.69), calls=%async_computation.2 | async-start | bytes 1048576 | tf_op jit(solution)/shard_map/all_to_all | solution.py:432
  97.7 0.0 copy-done.1
  97.7 9.1 %shard_map.123 = (bf16[256,768]{1,0:T(8,128)(2,1)}, bf16[256,768]{1,0:T(8,128)(2,1)}, bf16[256,768]{1,0:T(8,128)(2,1)}, bf16[256,768]{1,0:T(8,128)(2,1)}, bf16[2...) custom-call(s32[1]{0:T(128)} %bitcast.y_ref, ...), custom_call_target="tpu_custom_call" | custom-call | flops 1879048192 | bytes 9048068 | tf_op jit(solution)/shard_map/pallas_call | solution.py:67
  106.8 1.4 all-to-all-done.2.in_ref
  108.2 6.3 %all-to-all-start.4 = ((f32[32,8,128]{2,1,0:T(8,128)}), f32[32,8,128]{2,1,0:T(8,128)S(1)}, u32[]{:S(2)}, u32[]{:S(2)}) async-start(f32[32,8,128]{2,1,0:T(8,128)} %get-tuple-element.71), calls=%async_computation.4 | async-start | bytes 262144 | tf_op jit(solution)/shard_map/all_to_all | solution.py:432
  114.5 0.0 copy-done.3
  114.5 2.1 %shard_map.126 = bf16[32,16,512]{2,1,0:T(8,128)(2,1)} custom-call(bf16[32,16,512]{2,1,0:T(8,128)(2,1)} %copy-done.3, f32[32,8,128]{2,1,0:T(8,128)} %get-tuple-element.70.extra_ref), custom_call_target="tpu_custom_call" | custom-call | bytes 1179648 | tf_op jit(solution)/shard_map/pallas_call | solution.py:67
  116.6 4.5 %all-to-all-done.4.adjoint_ref = f32[32,8,128]{2,1,0:T(8,128)S(1)} async-done(((f32[32,8,128]{2,1,0:T(8,128)}), f32[32,8,128]{2,1,0:T(8,128)S(1)}, u32[]{:S(2)}, u32[]{:S(2)}) %all-to-all-start.4) | async-done | bytes 131104 | tf_op jit(solution)/shard_map/all_to_all | solution.py:432
  121.2 5.0 %all-to-all-start.3 = ((bf16[32,16,512]{2,1,0:T(8,128)(2,1)}), bf16[32,16,512]{2,1,0:T(8,128)(2,1)S(1)}, u32[]{:S(2)}, u32[]{:S(2)}) async-start(bf16[32,16,512]{2,1,0:T(8,128)(2,1)} %shard_map.126), calls=%async_computation.3 | async-start | bytes 1048576 | tf_op jit(solution)/shard_map/all_to_all | solution.py:432
  126.1 1.8 collective-permute-start.6
  127.9 4.7 %shard_map.125 = (f32[2,512,256]{2,1,0:T(8,128)}, f32[2,512,512]{2,1,0:T(8,128)}) custom-call(bf16[2,4,128,768]{3,2,1,0:T(8,128)(2,1)} %get-tuple-element.54.qg_ref, bf16[2,512,512]{2,1,0:T(8,128)(2,1)} %get-tuple-element.55.pair_ref, bf16[2,512,512]{2,1,0:T(8,128)(2,1)} %get-tuple-element.56.num_ref, bf16[2,512,512]{2,1,0:T(8,128)(2,1)} %get-tuple-element.65.score_ref), custom_call_target="tpu_custom_call" | custom-call | flops 805306368 | bytes 7864320 | tf_op jit(solution)/shard_map/pallas_call | solution.py:67
  132.7 4.1 %all-to-all-done.3.back_ref = bf16[32,16,512]{2,1,0:T(8,128)(2,1)S(1)} async-done(((bf16[32,16,512]{2,1,0:T(8,128)(2,1)}), bf16[32,16,512]{2,1,0:T(8,128)(2,1)S(1)}, u32[]{:S(2)}, u32[]{:S(2)}) %all-to-all-start.3) | async-done | bytes 524320 | tf_op jit(solution)/shard_map/all_to_all | solution.py:432
  136.7 0.8 copy-done.2
  137.5 6.0 %shard_map.127 = (bf16[272,768]{1,0:T(8,128)(2,1)}, bf16[272,768]{1,0:T(8,128)(2,1)}, bf16[272,768]{1,0:T(8,128)(2,1)}, bf16[272,768]{1,0:T(8,128)(2,1)}) custom-call(s32[1]{0:T(128)} %bitcast.y_ref, s32[1]{0:T(128)} %bitcast.2.me_ref, bf16[2,4,128,768]{3,2,1,0:T(8,128)(2,1)} %get-tuple-element.46.kv_ref, f32[2,512,256]{2,1,0:T(8,128)} %get-tuple-element.66.key_ref, ...), custom_call_target="tpu_custom_call" | custom-call | flops 536870912 | bytes 8753160 | tf_op jit(solution)/shard_map/pallas_call | solution.py:67
  143.6 1.7 collective-permute-start.9
  145.3 2.4 %collective-permute-start.10 = (bf16[272,768]{1,0:T(8,128)(2,1)}, bf16[272,768]{1,0:T(8,128)(2,1)S(1)}, u32[]{:S(2)}, u32[]{:S(2)}) collective-permute-start(bf16[272,768]{1,0:T(8,128)(2,1)} %get-tuple-element.74), channel_id=1, source_target_pairs={{0,2},{1,3},{2,0},{3,1},{4,6},{5,7},{6,4},{7,5},{8,10},{9,11},{10,... | collective-permute-start | bytes 1253384 | tf_op jit(solution)/shard_map/ppermute | solution.py:423
  147.7 1.0 collective-permute-start.11
  148.7 1.1 collective-permute-start.7
  149.8 0.0 collective-permute-done.6.r1
  149.8 0.0 copy-done.17
  149.8 2.7 %collective-permute-start.8 = (bf16[256,768]{1,0:T(8,128)(2,1)S(1)}, bf16[256,768]{1,0:T(8,128)(2,1)S(1)}, u32[]{:S(2)}, u32[]{:S(2)}) collective-permute-start(bf16[256,768]{1,0:T(8,128)(2,1)S(1)} %copy-done.17), channel_id=1, source_target_pairs={{0,3},{1,0},{2,1},{3,2},{4,7},{5,4},{6,5},{7,6},{8,11},{9,8},{10,9... | collective-permute-start | bytes 1179656 | tf_op jit(solution)/shard_map/ppermute | solution.py:423
  152.5 22.7 %collective-permute-done.7.r2 = bf16[256,768]{1,0:T(8,128)(2,1)S(1)} collective-permute-done((bf16[256,768]{1,0:T(8,128)(2,1)S(1)}, bf16[256,768]{1,0:T(8,128)(2,1)S(1)}, u32[]{:S(2)}, u32[]{:S(2)}) %collective-permute-start.7) | collective-permute-done | bytes 393248 | tf_op jit(solution)/shard_map/ppermute | solution.py:423
  175.2 8.2 %collective-permute-done.8.r3 = bf16[256,768]{1,0:T(8,128)(2,1)S(1)} collective-permute-done((bf16[256,768]{1,0:T(8,128)(2,1)S(1)}, bf16[256,768]{1,0:T(8,128)(2,1)S(1)}, u32[]{:S(2)}, u32[]{:S(2)}) %collective-permute-start.8) | collective-permute-done | bytes 393248 | tf_op jit(solution)/shard_map/ppermute | solution.py:423
  183.4 0.8 copy-done.13
  184.2 2.6 %shard_map.124 = (bf16[8,128,512]{2,1,0:T(8,128)(2,1)}, bf16[8,128,256]{2,1,0:T(8,128)(2,1)}) custom-call(s32[1]{0:T(128)} %bitcast.y_ref, bf16[256,768]{1,0:T(8,128)(2,1)} %get-tuple-element.59.r0, bf16[256,768]{1,0:T(8,128)(2,1)} %copy-done.11, bf16[256,768]{1,0:T(8,128)(2,1)} %copy-done.12, bf16[256,768]{1,0:T(8,128)(2,1)} %copy-done.13), custom_call_target="tpu_custom_call" | custom-call | bytes 3145732 | tf_op jit(solution)/shard_map/pallas_call | solution.py:67
  186.8 0.0 collective-permute-done.9.r1
  186.8 0.0 collective-permute-done.10.r2
  186.8 0.0 collective-permute-done.11.r3
  186.8 0.7 copy-done.5
  187.5 0.2 copy-done.6
  187.7 0.1 copy-done.7
  187.8 2.6 %shard_map.128 = (bf16[8,128,512]{2,1,0:T(8,128)(2,1)}, bf16[8,128,256]{2,1,0:T(8,128)(2,1)}, bf16[8,128]{1,0:T(8,128)(2,1)}, bf16[8,128]{1,0:T(8,128)(2,1)}) custom-call(s32[1]{0:T(128)} %bitcast.y_ref, bf16[272,768]{1,0:T(8,128)(2,1)} %get-tuple-element.72.r0, bf16[272,768]{1,0:T(8,128)(2,1)} %copy-done.5, bf16[272,768]{1,0:T(8,128)(2,1)} %copy-done.6, ...), custom_call_target="tpu_custom_call" | custom-call | bytes 3248132 | tf_op jit(solution)/shard_map/pallas_call | solution.py:67
  (25 shorter events, 0.0 us)
Async XLA Ops:
  3.1 12.9 %collective-permute-start = (bf16[272,768]{1,0:T(8,128)(2,1)}, bf16[272,768]{1,0:T(8,128)(2,1)S(1)}, u32[]{:S(2)}, u32[]{:S(2)}) collective-permute-start(bf16[272,768]{1,0:T(8,128)(2,1)} %get-tuple-element.43), channel_id=1, source_target_pairs={{0,1},{1,2},{2,3},{3,0},{4,5},{5,6},{6,7},{7,4},{8,9},{9,10},{10,1... | collective-permute-start | bytes 1253384 | tf_op jit(solution)/shard_map/ppermute | solution.py:423
  4.7 21.4 %collective-permute-start.1 = (bf16[272,768]{1,0:T(8,128)(2,1)}, bf16[272,768]{1,0:T(8,128)(2,1)S(1)}, u32[]{:S(2)}, u32[]{:S(2)}) collective-permute-start(bf16[272,768]{1,0:T(8,128)(2,1)} %get-tuple-element.44), channel_id=1, source_target_pairs={{0,2},{1,3},{2,0},{3,1},{4,6},{5,7},{6,4},{7,5},{8,10},{9,11},{10,... | collective-permute-start | bytes 1253384 | tf_op jit(solution)/shard_map/ppermute | solution.py:423
  7.6 18.5 %collective-permute-start.2 = (bf16[272,768]{1,0:T(8,128)(2,1)}, bf16[272,768]{1,0:T(8,128)(2,1)S(1)}, u32[]{:S(2)}, u32[]{:S(2)}) collective-permute-start(bf16[272,768]{1,0:T(8,128)(2,1)} %get-tuple-element.45), channel_id=1, source_target_pairs={{0,3},{1,0},{2,1},{3,2},{4,7},{5,4},{6,5},{7,6},{8,11},{9,8},{10,9... | collective-permute-start | bytes 1253384 | tf_op jit(solution)/shard_map/ppermute | solution.py:423
  16.0 10.1 %copy-start.8 = (bf16[272,768]{1,0:T(8,128)(2,1)}, bf16[272,768]{1,0:T(8,128)(2,1)S(1)}, u32[]{:S(2)}) copy-start(bf16[272,768]{1,0:T(8,128)(2,1)S(1)} %collective-permute-done.kv1) | copy-start | bytes 1253380
  26.1 0.8 copy-start.9
  26.1 0.9 copy-start.10
  30.8 20.4 %all-to-all-start = ((bf16[32,16,640]{2,1,0:T(8,128)(2,1)}), bf16[32,16,640]{2,1,0:T(8,128)(2,1)S(1)}, u32[]{:S(2)}, u32[]{:S(2)}) async-start(bf16[32,16,640]{2,1,0:T(8,128)(2,1)} %get-tuple-element.52.pay_ref), calls=%async_computation | async-start | bytes 1310720 | tf_op jit(solution)/shard_map/all_to_all | solution.py:432
  51.1 0.8 copy-start
  54.0 36.2 %all-to-all-start.1 = ((bf16[32,16,512]{2,1,0:T(8,128)(2,1)}), bf16[32,16,512]{2,1,0:T(8,128)(2,1)S(1)}, u32[]{:S(2)}, u32[]{:S(2)}) async-start(bf16[32,16,512]{2,1,0:T(8,128)(2,1)} %get-tuple-element.58), calls=%async_computation.1 | async-start | bytes 1048576 | tf_op jit(solution)/shard_map/all_to_all | solution.py:432
  61.6 13.2 %collective-permute-start.3 = (bf16[256,768]{1,0:T(8,128)(2,1)}, bf16[256,768]{1,0:T(8,128)(2,1)S(1)}, u32[]{:S(2)}, u32[]{:S(2)}) collective-permute-start(bf16[256,768]{1,0:T(8,128)(2,1)} %get-tuple-element.47), channel_id=1, source_target_pairs={{0,1},{1,2},{2,3},{3,0},{4,5},{5,6},{6,7},{7,4},{8,9},{9,10},{10,1... | collective-permute-start | bytes 1179656 | tf_op jit(solution)/shard_map/ppermute | solution.py:423
  62.6 20.2 %collective-permute-start.4 = (bf16[256,768]{1,0:T(8,128)(2,1)}, bf16[256,768]{1,0:T(8,128)(2,1)S(1)}, u32[]{:S(2)}, u32[]{:S(2)}) collective-permute-start(bf16[256,768]{1,0:T(8,128)(2,1)} %get-tuple-element.48), channel_id=1, source_target_pairs={{0,2},{1,3},{2,0},{3,1},{4,6},{5,7},{6,4},{7,5},{8,10},{9,11},{10,... | collective-permute-start | bytes 1179656 | tf_op jit(solution)/shard_map/ppermute | solution.py:423
  65.0 18.2 %collective-permute-start.5 = (bf16[256,768]{1,0:T(8,128)(2,1)}, bf16[256,768]{1,0:T(8,128)(2,1)S(1)}, u32[]{:S(2)}, u32[]{:S(2)}) collective-permute-start(bf16[256,768]{1,0:T(8,128)(2,1)} %get-tuple-element.49), channel_id=1, source_target_pairs={{0,3},{1,0},{2,1},{3,2},{4,7},{5,4},{6,5},{7,6},{8,11},{9,8},{10,9... | collective-permute-start | bytes 1179656 | tf_op jit(solution)/shard_map/ppermute | solution.py:423
  74.8 8.4 %copy-start.14 = (bf16[256,768]{1,0:T(8,128)(2,1)}, bf16[256,768]{1,0:T(8,128)(2,1)S(1)}, u32[]{:S(2)}) copy-start(bf16[256,768]{1,0:T(8,128)(2,1)S(1)} %collective-permute-done.3.qg1) | copy-start | bytes 1179652
  82.8 0.8 copy-start.15
  83.3 0.7 copy-start.16
  90.2 7.5 %copy-start.1 = (bf16[32,16,512]{2,1,0:T(8,128)(2,1)}, bf16[32,16,512]{2,1,0:T(8,128)(2,1)S(1)}, u32[]{:S(2)}) copy-start(bf16[32,16,512]{2,1,0:T(8,128)(2,1)S(1)} %all-to-all-done.1.in_ref.state_ref) | copy-start | bytes 1572868
  90.2 18.0 %all-to-all-start.2 = ((bf16[32,16,512]{2,1,0:T(8,128)(2,1)}), bf16[32,16,512]{2,1,0:T(8,128)(2,1)S(1)}, u32[]{:S(2)}, u32[]{:S(2)}) async-start(bf16[32,16,512]{2,1,0:T(8,128)(2,1)} %get-tuple-element.69), calls=%async_computation.2 | async-start | bytes 1048576 | tf_op jit(solution)/shard_map/all_to_all | solution.py:432
  106.8 19.3 %copy-start.19 = (bf16[256,768]{1,0:T(8,128)(2,1)S(1)}, bf16[256,768]{1,0:T(8,128)(2,1)}, u32[]{:S(2)}) copy-start(bf16[256,768]{1,0:T(8,128)(2,1)} %get-tuple-element.60) | copy-start | bytes 1179652
  108.2 6.3 %copy-start.3 = (bf16[32,16,512]{2,1,0:T(8,128)(2,1)}, bf16[32,16,512]{2,1,0:T(8,128)(2,1)S(1)}, u32[]{:S(2)}) copy-start(bf16[32,16,512]{2,1,0:T(8,128)(2,1)S(1)} %all-to-all-done.2.in_ref) | copy-start | bytes 1572868
  108.2 12.9 %all-to-all-start.4 = ((f32[32,8,128]{2,1,0:T(8,128)}), f32[32,8,128]{2,1,0:T(8,128)S(1)}, u32[]{:S(2)}, u32[]{:S(2)}) async-start(f32[32,8,128]{2,1,0:T(8,128)} %get-tuple-element.71), calls=%async_computation.4 | async-start | bytes 262144 | tf_op jit(solution)/shard_map/all_to_all | solution.py:432
  121.2 11.5 %copy-start.4 = (f32[32,8,128]{2,1,0:T(8,128)}, f32[32,8,128]{2,1,0:T(8,128)S(1)}, u32[]{:S(2)}) copy-start(f32[32,8,128]{2,1,0:T(8,128)S(1)} %all-to-all-done.4.adjoint_ref) | copy-start | bytes 393220
  121.2 15.6 %all-to-all-start.3 = ((bf16[32,16,512]{2,1,0:T(8,128)(2,1)}), bf16[32,16,512]{2,1,0:T(8,128)(2,1)S(1)}, u32[]{:S(2)}, u32[]{:S(2)}) async-start(bf16[32,16,512]{2,1,0:T(8,128)(2,1)} %shard_map.126), calls=%async_computation.3 | async-start | bytes 1048576 | tf_op jit(solution)/shard_map/all_to_all | solution.py:432
  126.1 23.6 %collective-permute-start.6 = (bf16[256,768]{1,0:T(8,128)(2,1)S(1)}, bf16[256,768]{1,0:T(8,128)(2,1)S(1)}, u32[]{:S(2)}, u32[]{:S(2)}) collective-permute-start(bf16[256,768]{1,0:T(8,128)(2,1)S(1)} %copy-done.19), channel_id=1, source_target_pairs={{0,1},{1,2},{2,3},{3,0},{4,5},{5,6},{6,7},{7,4},{8,9},{9,10},{10,1... | collective-permute-start | bytes 1179656 | tf_op jit(solution)/shard_map/ppermute | solution.py:423
  136.7 0.8 copy-start.2
  137.5 11.2 %copy-start.18 = (bf16[256,768]{1,0:T(8,128)(2,1)S(1)}, bf16[256,768]{1,0:T(8,128)(2,1)}, u32[]{:S(2)}) copy-start(bf16[256,768]{1,0:T(8,128)(2,1)} %get-tuple-element.61) | copy-start | bytes 1179652
  137.5 12.2 %copy-start.17 = (bf16[256,768]{1,0:T(8,128)(2,1)S(1)}, bf16[256,768]{1,0:T(8,128)(2,1)}, u32[]{:S(2)}) copy-start(bf16[256,768]{1,0:T(8,128)(2,1)} %get-tuple-element.62) | copy-start | bytes 1179652
  143.6 43.2 %collective-permute-start.9 = (bf16[272,768]{1,0:T(8,128)(2,1)}, bf16[272,768]{1,0:T(8,128)(2,1)S(1)}, u32[]{:S(2)}, u32[]{:S(2)}) collective-permute-start(bf16[272,768]{1,0:T(8,128)(2,1)} %get-tuple-element.73), channel_id=1, source_target_pairs={{0,1},{1,2},{2,3},{3,0},{4,5},{5,6},{6,7},{7,4},{8,9},{9,10},{10,1... | collective-permute-start | bytes 1253384 | tf_op jit(solution)/shard_map/ppermute | solution.py:423
  145.3 41.5 %collective-permute-start.10 = (bf16[272,768]{1,0:T(8,128)(2,1)}, bf16[272,768]{1,0:T(8,128)(2,1)S(1)}, u32[]{:S(2)}, u32[]{:S(2)}) collective-permute-start(bf16[272,768]{1,0:T(8,128)(2,1)} %get-tuple-element.74), channel_id=1, source_target_pairs={{0,2},{1,3},{2,0},{3,1},{4,6},{5,7},{6,4},{7,5},{8,10},{9,11},{10,... | collective-permute-start | bytes 1253384 | tf_op jit(solution)/shard_map/ppermute | solution.py:423
  147.7 39.1 %collective-permute-start.11 = (bf16[272,768]{1,0:T(8,128)(2,1)}, bf16[272,768]{1,0:T(8,128)(2,1)S(1)}, u32[]{:S(2)}, u32[]{:S(2)}) collective-permute-start(bf16[272,768]{1,0:T(8,128)(2,1)} %get-tuple-element.75), channel_id=1, source_target_pairs={{0,3},{1,0},{2,1},{3,2},{4,7},{5,4},{6,5},{7,6},{8,11},{9,8},{10,9... | collective-permute-start | bytes 1253384 | tf_op jit(solution)/shard_map/ppermute | solution.py:423
  148.7 26.5 %collective-permute-start.7 = (bf16[256,768]{1,0:T(8,128)(2,1)S(1)}, bf16[256,768]{1,0:T(8,128)(2,1)S(1)}, u32[]{:S(2)}, u32[]{:S(2)}) collective-permute-start(bf16[256,768]{1,0:T(8,128)(2,1)S(1)} %copy-done.18), channel_id=1, source_target_pairs={{0,2},{1,3},{2,0},{3,1},{4,6},{5,7},{6,4},{7,5},{8,10},{9,11},{10,... | collective-permute-start | bytes 1179656 | tf_op jit(solution)/shard_map/ppermute | solution.py:423
  149.8 33.6 %copy-start.11 = (bf16[256,768]{1,0:T(8,128)(2,1)}, bf16[256,768]{1,0:T(8,128)(2,1)S(1)}, u32[]{:S(2)}) copy-start(bf16[256,768]{1,0:T(8,128)(2,1)S(1)} %collective-permute-done.6.r1) | copy-start | bytes 1179652
  149.8 33.6 %collective-permute-start.8 = (bf16[256,768]{1,0:T(8,128)(2,1)S(1)}, bf16[256,768]{1,0:T(8,128)(2,1)S(1)}, u32[]{:S(2)}, u32[]{:S(2)}) collective-permute-start(bf16[256,768]{1,0:T(8,128)(2,1)S(1)} %copy-done.17), channel_id=1, source_target_pairs={{0,3},{1,0},{2,1},{3,2},{4,7},{5,4},{6,5},{7,6},{8,11},{9,8},{10,9... | collective-permute-start | bytes 1179656 | tf_op jit(solution)/shard_map/ppermute | solution.py:423
  175.2 8.2 %copy-start.12 = (bf16[256,768]{1,0:T(8,128)(2,1)}, bf16[256,768]{1,0:T(8,128)(2,1)S(1)}, u32[]{:S(2)}) copy-start(bf16[256,768]{1,0:T(8,128)(2,1)S(1)} %collective-permute-done.7.r2) | copy-start | bytes 1179652
  183.4 0.8 copy-start.13
  186.8 0.8 copy-start.5
  186.8 0.9 copy-start.6
  186.8 1.0 copy-start.7

commit v2 on v1

v2 whole, which is shorter than its diff:
```python
import functools

import jax
import jax.numpy as jnp
from jax import lax
from jax.experimental import pallas as pl
from jax.experimental.pallas import tpu as pltpu
from jax.sharding import PartitionSpec as P

f32, bf16 = jnp.float32, jnp.bfloat16
CHUNK, CHUNKS, TOKENS = 128, 4, 512
HEADS = 2
DK, DV = 256, 512
WIDE = DK + DV
EXTRA = 16
SLICES = 32
NEG = -1e30
BIG = 10**8
SCALE = DK ** (-0.5)
ROWS = 256
VMEM = pltpu.VMEM
PARAMS = pltpu.CompilerParams(vmem_limit_bytes=16 * 1024 * 1024)


def dot(left, right, cl, cr, precision=None):
    return lax.dot_general(
        left, right, (((cl,), (cr,)), ((), ())), preferred_element_type=f32, precision=precision
    )


def exact(left, right):
    return dot(left, right, 1, 0, lax.Precision.HIGHEST)


def column(bundle, first):
    return jnp.concatenate([bundle[:, first + c : first + c + 1] for c in range(CHUNKS)], axis=0)


def line(bundle, first):
    return jnp.concatenate([bundle[first + c : first + c + 1, :] for c in range(CHUNKS)], axis=1)


def chunk_of(y, shift):
    return lax.rem(y + shift + CHUNKS, CHUNKS)


def smem():
    return pl.BlockSpec(memory_space=pltpu.SMEM)


def whole():
    return pl.BlockSpec(memory_space=VMEM)


def call(body, outs, ins, scratch=(), cost=1, after=()):
    def run(*refs):
        body(*refs[: len(ins)], *refs[len(ins) + len(after) :])

    in_specs = [smem() if a.dtype == jnp.int32 and a.size <= 2 else whole() for a in ins]
    return pl.pallas_call(
        run,
        out_shape=outs,
        in_specs=in_specs + [pl.BlockSpec(memory_space=pl.ANY) for _ in after],
        out_specs=tuple(whole() for _ in outs),
        scratch_shapes=scratch,
        compiler_params=PARAMS,
        cost_estimate=pl.CostEstimate(flops=cost, bytes_accessed=cost, transcendentals=0),
    )(*ins, *after)


def like(shape, dtype):
    return jax.ShapeDtypeStruct(shape, dtype)


def pack_body(gates, y_ref, a_ref, b_ref, *rest):
    outs = rest[-4:]
    y = y_ref[0]
    for shift, out in enumerate(outs):
        dest = chunk_of(y, shift)
        for h in range(HEADS):
            out[h * CHUNK : (h + 1) * CHUNK, 0:DK] = a_ref[dest * HEADS + h]
            out[h * CHUNK : (h + 1) * CHUNK, DK:WIDE] = b_ref[dest * HEADS + h]
        if gates:
            both = jnp.concatenate([rest[0][...].astype(f32), rest[1][...].astype(f32)], axis=0)
            out[HEADS * CHUNK : HEADS * CHUNK + EXTRA, 0:CHUNK] = both.astype(bf16)


def pack(y, narrow, wide, gates=()):
    rows = HEADS * CHUNK + (EXTRA if gates else 0)
    return call(
        functools.partial(pack_body, bool(gates)),
        [like((rows, WIDE), bf16)] * 4,
        [y, narrow, wide, *gates],
    )


def assemble(all_ref, y, received):
    for shift, ref in enumerate(received):
        source = chunk_of(y, -shift)
        for h in range(HEADS):
            all_ref[h, source] = ref[h * CHUNK : (h + 1) * CHUNK, :]


def update_body(
    y_ref, kv0, kv1, kv2, kv3, doc_ref, all_ref, line_ref, col_ref, pay_ref, gates, lines, extra
):
    y = y_ref[0]
    received = (kv0, kv1, kv2, kv3)
    assemble(all_ref, y, received)
    for shift, ref in enumerate(received):
        gates[chunk_of(y, -shift)] = ref[HEADS * CHUNK : HEADS * CHUNK + EXTRA, 0:CHUNK].astype(f32)
    row = lax.broadcasted_iota(jnp.int32, (16, CHUNK), 0)
    for c in range(CHUNKS):
        tile = gates[c]
        for h in range(HEADS):
            pick = y * HEADS + h
            lines[1, h * CHUNKS + c : h * CHUNKS + c + 1, :] = jnp.sum(
                jnp.where(row == pick, tile, 0.0), axis=0, keepdims=True
            )
            lines[0, h * CHUNKS + c : h * CHUNKS + c + 1, :] = jnp.sum(
                jnp.where(row == pick + 8, tile, 0.0), axis=0, keepdims=True
            )
    forget = lines[0, 0:8]
    fade = jnp.exp(-forget)
    lines[0, 0:8] = -jnp.log1p(fade)
    lines[0, 8:12] = doc_ref[...].astype(f32)
    lines[0, 12:16] = jnp.zeros((4, CHUNK), f32)
    closed = fade / (1.0 + fade)
    before = lax.broadcasted_iota(jnp.int32, (CHUNK, CHUNK), 0)
    after = lax.broadcasted_iota(jnp.int32, (CHUNK, CHUNK), 1)
    total = exact(lines[0], (before <= after).astype(f32))
    whole_lines = []
    for group in range(3):
        run = jnp.zeros((1, 1), f32)
        for c in range(CHUNKS):
            here = total[group * CHUNKS + c : group * CHUNKS + c + 1, :]
            whole_lines.append(here + run)
            run = run + here[:, CHUNK - 1 : CHUNK]
    segment = jnp.concatenate(whole_lines[8:12], axis=0)
    segment_end = segment[3:4, CHUNK - 1 : CHUNK]
    extra[...] = jnp.zeros_like(extra)
    for h in range(HEADS):
        cumulative = jnp.concatenate(whole_lines[h * CHUNKS : (h + 1) * CHUNKS], axis=0)
        end = cumulative[3:4, CHUNK - 1 : CHUNK]
        ingate = lines[1, h * CHUNKS : (h + 1) * CHUNKS]
        line_ref[h] = jnp.zeros((CHUNK, CHUNK), f32)
        line_ref[h, 0:4] = cumulative
        line_ref[h, 4:8] = ingate - cumulative
        line_ref[h, 8:12] = jnp.where(segment == segment_end, jnp.exp(end - cumulative + ingate), 0.0)
        line_ref[h, 12:16] = jnp.where(segment == 0.0, jnp.exp(cumulative), 0.0)
        line_ref[h, 16:20] = segment
        line_ref[h, 20:24] = closed[h * CHUNKS : (h + 1) * CHUNKS]
        col_ref[h] = line_ref[h].T
        decay = jnp.where(segment_end == 0.0, jnp.exp(end), 0.0)
        keys = all_ref[h, :, :, 0:DK].reshape(TOKENS, DK)
        values = all_ref[h, :, :, DK:WIDE].reshape(TOKENS, DV)
        keys_alpha = (column(col_ref[h], 8) * keys.astype(f32)).astype(bf16)
        update = dot(keys_alpha, values, 0, 0).astype(bf16)
        scatter(pay_ref, update, h)
        update_n = jnp.sum(keys_alpha.astype(f32), axis=0, keepdims=True)
        for half in range(2):
            extra[2 * h + half : 2 * h + half + 1, :] = update_n[:, half * CHUNK : (half + 1) * CHUNK]
            extra[4 + 2 * h + half : 5 + 2 * h + half, :] = jnp.broadcast_to(decay, (1, CHUNK))
    share(pay_ref, extra[...])


def share(pay_ref, lines):
    high = lines.astype(bf16).astype(f32)
    tile = jnp.concatenate([high, lines - high], axis=0).astype(bf16)
    for i in range(SLICES):
        pay_ref[i, :, 2 * DK : 2 * DK + CHUNK] = tile


def shared(pay_ref, index):
    tile = pay_ref[index, :, 2 * DK : 2 * DK + CHUNK].astype(f32)
    return tile[0:8] + tile[8:16]


def scatter(pay_ref, matrix, h, first=0):
    for i in range(SLICES):
        r, c = i // 2, i % 2
        here = slice(first + h * DK, first + (h + 1) * DK)
        pay_ref[i, :, here] = matrix[16 * r : 16 * (r + 1), DK * c : DK * (c + 1)]


def collect(matrix_ref, pay_ref, h):
    for i in range(SLICES):
        r, c = i // 2, i % 2
        matrix_ref[h, 16 * r : 16 * (r + 1), DK * c : DK * (c + 1)] = pay_ref[i, :, h * DK : (h + 1) * DK]


def pair_body(y_ref, qg0, qg1, qg2, qg3, kv_ref, line_ref, col_ref, all_ref, pair_ref, weight_ref, sum_ref):
    assemble(all_ref, y_ref[0], (qg0, qg1, qg2, qg3))
    for h in range(HEADS):
        sum_ref[h] = jnp.zeros((CHUNK, CHUNK), f32)
        keys = kv_ref[h, :, :, 0:DK].reshape(TOKENS, DK)
        query = all_ref[h, :, :, 0:DK].reshape(TOKENS, DK)
        for r in range(TOKENS // ROWS):
            last = (r + 1) * ROWS
            here = slice(r * ROWS, last)
            scores = dot(query[here], keys[0:last], 1, 1) * SCALE
            weight = weights(line_ref, col_ref, h, r)
            weight_ref[h, here, 0:last] = weight
            pair = (weight * scores).astype(bf16)
            pair_ref[h, here, 0:last] = pair
            put_column(sum_ref, h, 0, jnp.sum(pair.astype(f32), axis=1, keepdims=True), r)


def weights(line_ref, col_ref, h, r):
    last = (r + 1) * ROWS
    here = slice(r * ROWS, last)
    position = lax.broadcasted_iota(jnp.int32, (ROWS, last), 0) + r * ROWS
    source = lax.broadcasted_iota(jnp.int32, (ROWS, last), 1)
    log_weight = column(col_ref[h], 0)[here] + line(line_ref[h], 4)[:, 0:last]
    allowed = (position >= source) & (column(col_ref[h], 16)[here] == line(line_ref[h], 16)[:, 0:last])
    return jnp.exp(jnp.where(allowed, log_weight, NEG))


def put_column(ref, h, first, value, r=0):
    first += r * (ROWS // CHUNK)
    for c in range(value.shape[0] // CHUNK):
        ref[h, :, first + c : first + c + 1] = value[c * CHUNK : (c + 1) * CHUNK]


def norm_line(norm_ref, h):
    both = [norm_ref[2 * h + half : 2 * h + half + 1, :] for half in range(2)]
    return jnp.concatenate(both, axis=1).astype(bf16).astype(f32)


def spread(extra):
    return jnp.concatenate([extra[4 + r : 5 + r, :] for r in range(4)], axis=1)


def adjoint_body(n_ctx, me_ref, in_ref, qg_ref, col_ref, sum_ref, pay_ref, norm_ref, extra_ref, num_ref, cols_ref):
    mine = SLICES // n_ctx
    me = me_ref[0]
    norm = jnp.zeros((4, CHUNK), f32)
    for j in range(n_ctx):
        extra = shared(in_ref, j * mine)
        extra_ref[j] = extra
        norm = jnp.where(j < me, extra[4:8] * norm + extra[0:4], norm)
    norm_ref[...] = jnp.concatenate([norm, jnp.zeros((4, CHUNK), f32)], axis=0)
    for h in range(HEADS):
        cols_ref[h] = jnp.zeros((CHUNK, CHUNK), f32)
        query = qg_ref[h, :, :, 0:DK].reshape(TOKENS, DK).astype(f32)
        beta = column(col_ref[h], 12)
        cross = jnp.sum(query * norm_line(norm_ref, h), axis=1, keepdims=True)
        denominator = column(sum_ref[h], 0) + beta * cross * SCALE
        norm = jnp.sqrt(denominator * denominator + 1.0)
        put_column(cols_ref, h, 0, denominator)
        put_column(cols_ref, h, 4, norm)
        grad = qg_ref[h, :, :, DK:WIDE].reshape(TOKENS, DV).astype(f32)
        num_grad = (grad / norm).astype(bf16)
        num_ref[h] = num_grad
        query_beta = (beta * query * SCALE).astype(bf16)
        scatter(pay_ref, dot(query_beta, num_grad, 0, 0).astype(bf16), h, 2 * DK)
    state = jnp.zeros((mine, 16, 2 * DK), f32)
    for j in range(n_ctx):
        here = slice(j * mine, (j + 1) * mine)
        pay_ref[here, :, 0 : 2 * DK] = state.astype(bf16)
        state = spread(extra_ref[j]) * state + in_ref[here, :, 0 : 2 * DK].astype(f32)


def local_body(kv_ref, pair_ref, num_ref, weight_ref, inner_ref, score_ref, value_ref):
    for h in range(HEADS):
        values = kv_ref[h, :, :, DK:WIDE].reshape(TOKENS, DV)
        for r in range(TOKENS // ROWS):
            last = (r + 1) * ROWS
            here = slice(r * ROWS, last)
            inner_ref[h, here] = dot(pair_ref[h, here, 0:last], values[0:last], 1, 0)
            score_ref[h, here, 0:last] = weight_ref[h, here, 0:last] * dot(num_ref[h, here], values[0:last], 1, 1)
        for s in range(TOKENS // ROWS):
            first = s * ROWS
            here = slice(first, first + ROWS)
            value_ref[h, here] = dot(pair_ref[h, first:TOKENS, here], num_ref[h, first:TOKENS], 0, 0)


def hidden_body(
    n_ctx, y_ref, in_ref, extra_ref, qg_ref, inner_ref, col_ref, cols_ref, o0, o1, o2, o3, pay_ref, state_ref, den_ref, done, lines
):
    mine = SLICES // n_ctx
    lines[...] = jnp.zeros_like(lines)
    for h in range(HEADS):
        collect(state_ref, in_ref, h)
        state = state_ref[h]
        den_ref[h] = jnp.zeros((CHUNK, CHUNK), f32)
        beta = column(col_ref[h], 12) * SCALE
        denominator = column(cols_ref[h], 0)
        inverse = 1.0 / column(cols_ref[h], 4)
        factor = -denominator * inverse * inverse
        for r in range(TOKENS // ROWS):
            here = slice(r * ROWS, (r + 1) * ROWS)
            chunks = slice(r * ROWS // CHUNK, (r + 1) * ROWS // CHUNK)
            query = qg_ref[h, chunks, :, 0:DK].reshape(ROWS, DK)
            grad = qg_ref[h, chunks, :, DK:WIDE].reshape(ROWS, DV)
            hidden = (inner_ref[h, here] + beta[here] * dot(query, state, 1, 0)) * inverse[here]
            done[here, :] = hidden.astype(bf16)
            product = jnp.sum(grad.astype(f32) * hidden, axis=1, keepdims=True)
            den_grad = product * factor[here]
            put_column(den_ref, h, 0, den_grad, r)
            query_beta = (beta[here] * query.astype(f32)).astype(bf16).astype(f32)
            total = jnp.sum(query_beta * den_grad, axis=0, keepdims=True)
            for half in range(2):
                lines[2 * h + half : 2 * h + half + 1, :] += total[:, half * CHUNK : (half + 1) * CHUNK]
        send(done, y_ref[0], h, (o0, o1, o2, o3))
    share(pay_ref, lines[...])
    back = jnp.zeros((mine, 16, 2 * DK), f32)
    for j in reversed(range(n_ctx)):
        here = slice(j * mine, (j + 1) * mine)
        pay_ref[here, :, 0 : 2 * DK] = back.astype(bf16)
        back = spread(extra_ref[j]) * back + in_ref[here, :, 2 * DK : 4 * DK].astype(f32)


def send(done, y, h, outs):
    for shift, out in enumerate(outs):
        first = pl.multiple_of(chunk_of(y, shift) * CHUNK, CHUNK)
        out[h * CHUNK : (h + 1) * CHUNK, :] = done[pl.ds(first, CHUNK), :]


def score_body(
    y_ref, kv_ref, qg_ref, num_ref, weight_ref, inner_ref, state_ref, norm_ref, col_ref, den_ref, o0, o1, o2, o3, terms_ref, key_ref, score, done
):
    for h in range(HEADS):
        terms_ref[h] = jnp.zeros((CHUNK, CHUNK), f32)
        keys = kv_ref[h, :, :, 0:DK].reshape(TOKENS, DK)
        query = qg_ref[h, :, :, 0:DK].reshape(TOKENS, DK)
        beta = column(col_ref[h], 12) * SCALE
        den_grad = column(den_ref[h], 0)
        norm_bf = norm_line(norm_ref, h)
        state = state_ref[h]
        for r in range(TOKENS // ROWS):
            last = (r + 1) * ROWS
            here = slice(r * ROWS, last)
            score[here, 0:last] = (
                inner_ref[h, here, 0:last] + weight_ref[h, here, 0:last] * den_grad[here]
            ).astype(bf16)
            from_state = dot(num_ref[h, here], state, 1, 1) + den_grad[here] * norm_bf
            query_grad = dot(score[here, 0:last], keys[0:last], 1, 0) * SCALE + beta[here] * from_state
            done[here, :] = query_grad.astype(bf16)
            term = jnp.sum(query[here].astype(f32) * query_grad, axis=1, keepdims=True)
            put_column(terms_ref, h, 0, term, r)
        send(done, y_ref[0], h, (o0, o1, o2, o3))
        for s in range(TOKENS // ROWS):
            first = s * ROWS
            here = slice(first, first + ROWS)
            key_ref[h, here] = dot(score[first:TOKENS, here], query[first:TOKENS], 0, 0) * SCALE


def grads_body(
    n_ctx, y_ref, me_ref, in_ref, kv_ref, key_ref, value_ref, line_ref, col_ref, terms_ref, state_ref, pay_ref, norm_ref, extra_ref, o0, o1, o2, o3, back, done, cols
):
    mine = SLICES // n_ctx
    y, me = y_ref[0], me_ref[0]
    norm = jnp.zeros((4, CHUNK), f32)
    for j in reversed(range(n_ctx)):
        norm = jnp.where(j > me, extra_ref[j][4:8] * norm + shared(in_ref, j * mine)[0:4], norm)
    back_n = norm.astype(bf16).astype(f32)
    extra = extra_ref[me]
    state_n = norm_ref[0:4, :].astype(bf16).astype(f32)
    later_n = (extra[4:8] * state_n + extra[0:4]) * back_n
    decay = spread(extra)
    later = jnp.zeros((16, 2 * DK), f32)
    for i in range(SLICES):
        state = decay * state_ref[i, :, 0 : 2 * DK].astype(f32) + pay_ref[i, :, 0 : 2 * DK].astype(f32)
        later = later + state * in_ref[i, :, 0 : 2 * DK].astype(f32)
    cols[...] = jnp.zeros_like(cols)
    for h in range(HEADS):
        collect(back, in_ref, h)
        back_bf = back[h]
        keys = kv_ref[h, :, :, 0:DK].reshape(TOKENS, DK)
        values = kv_ref[h, :, :, DK:WIDE].reshape(TOKENS, DV)
        alpha = column(col_ref[h], 8)
        row = jnp.concatenate([back_n[2 * h : 2 * h + 1], back_n[2 * h + 1 : 2 * h + 2]], axis=1)
        for r in range(TOKENS // ROWS):
            here = slice(r * ROWS, (r + 1) * ROWS)
            key_grad = key_ref[h, here] + alpha[here] * (dot(values[here], back_bf, 1, 1) + row)
            value_grad = value_ref[h, here] + alpha[here] * dot(keys[here], back_bf, 1, 0)
            done[here, 0:DV] = value_grad.astype(bf16)
            done[here, DV : DV + DK] = key_grad.astype(bf16)
            key_term = jnp.sum(keys[here].astype(f32) * key_grad, axis=1, keepdims=True)
            for c in range(ROWS // CHUNK):
                piece = key_term[c * CHUNK : (c + 1) * CHUNK]
                k = r * (ROWS // CHUNK) + c
                cols[:, h * 4 + k : h * 4 + k + 1] = terms_ref[h, :, k : k + 1] - piece
                cols[:, 8 + h * 4 + k : 9 + h * 4 + k] = piece
        send(done, y, h, (o0, o1, o2, o3))
    lines = cols[...].T[0:16]
    before = lax.broadcasted_iota(jnp.int32, (CHUNK, CHUNK), 0)
    after = lax.broadcasted_iota(jnp.int32, (CHUNK, CHUNK), 1)
    suffix = exact(lines, (before >= after).astype(f32))
    tiles = [[None] * HEADS for _ in range(CHUNKS)]
    for h in range(HEADS):
        run = jnp.sum(later[:, h * DK : (h + 1) * DK], keepdims=True) + jnp.sum(
            later_n[2 * h : 2 * h + 2], keepdims=True
        )
        for c in reversed(range(CHUNKS)):
            here = suffix[h * 4 + c : h * 4 + c + 1]
            tiles[c][h] = (here + run) * line_ref[h, 20 + c : 21 + c]
            run = run + here[:, 0:1]
    for c in range(CHUNKS):
        rows = [lines[8 + h * 4 + c : 9 + h * 4 + c] for h in range(HEADS)] + tiles[c]
        cols[c * 16 : (c + 1) * 16, :] = jnp.concatenate(rows + [jnp.zeros((12, CHUNK), f32)], axis=0)
    for shift, out in enumerate((o0, o1, o2, o3)):
        first = pl.multiple_of(chunk_of(y, shift) * 16, 16)
        out[HEADS * CHUNK : HEADS * CHUNK + EXTRA, 0:CHUNK] = cols[pl.ds(first, 16), :].astype(bf16)


def unpack_plain_body(y_ref, r0, r1, r2, r3, out_ref):
    for shift, ref in enumerate((r0, r1, r2, r3)):
        source = chunk_of(y_ref[0], -shift)
        for h in range(HEADS):
            out_ref[source * HEADS + h] = ref[h * CHUNK : (h + 1) * CHUNK, :]


def unpack_body(y_ref, r0, r1, r2, r3, wide_ref, narrow_ref, input_ref, forget_ref):
    y = y_ref[0]
    row = lax.broadcasted_iota(jnp.int32, (8, CHUNK), 0)
    sums = [jnp.zeros((8, CHUNK), f32)] * 2
    for shift, ref in enumerate((r0, r1, r2, r3)):
        source = chunk_of(y, -shift)
        tile = ref[HEADS * CHUNK : HEADS * CHUNK + EXTRA, 0:CHUNK].astype(f32)
        for h in range(HEADS):
            wide_ref[source * HEADS + h] = ref[h * CHUNK : (h + 1) * CHUNK, 0:DV]
            narrow_ref[source * HEADS + h] = ref[h * CHUNK : (h + 1) * CHUNK, DV : DV + DK]
            for k in range(2):
                here = jnp.where(row == source * HEADS + h, tile[2 * k + h : 2 * k + h + 1], 0.0)
                sums[k] = sums[k] + here
    input_ref[...] = sums[0].astype(bf16)
    forget_ref[...] = sums[1].astype(bf16)


def shift_all(parts):
    moved = [parts[0]]
    for shift, part in enumerate(parts[1:], 1):
        pairs = [(i, (i + shift) % CHUNKS) for i in range(CHUNKS)]
        moved.append(lax.ppermute(part, "head", pairs))
    return moved


def exchange(part):
    return lax.all_to_all(part, "ctx", split_axis=0, concat_axis=0, tiled=True)


def shards(query, keys, values, igate, fgate, hidden_output_gradient, doc_start):
    n_ctx = lax.axis_size("ctx")
    y = lax.axis_index("head").astype(jnp.int32).reshape(1)
    me = lax.axis_index("ctx").astype(jnp.int32).reshape(1)
    kv_received = shift_all(pack(y, keys, values, (igate, fgate)))
    qg_received = shift_all(pack(y, query, hidden_output_gradient))
    tokens = like((HEADS, CHUNKS, CHUNK, WIDE), bf16)
    bundle = like((HEADS, CHUNK, CHUNK), f32)
    square = like((HEADS, TOKENS, TOKENS), f32)
    square_bf = like((HEADS, TOKENS, TOKENS), bf16)
    carried = like((SLICES, 16, 2 * DK + CHUNK), bf16)
    kv, lines, cols, payload = call(
        update_body,
        [tokens, bundle, bundle, carried],
        [y, *kv_received, doc_start.reshape(CHUNKS, CHUNK)],
        [VMEM((CHUNKS, 16, CHUNK), f32), VMEM((2, 16, CHUNK), f32), VMEM((8, CHUNK), f32)],
    )
    updates = exchange(payload)
    qg, pair, weight, sums = call(
        pair_body, [tokens, square_bf, square, bundle], [y, *qg_received, kv, lines, cols], cost=BIG
    )
    both, norm, extra, num_grad, norm_cols = call(
        functools.partial(adjoint_body, n_ctx),
        [
            like((SLICES, 16, 4 * DK), bf16),
            like((8, CHUNK), f32),
            like((n_ctx, 8, CHUNK), f32),
            like((HEADS, TOKENS, DV), bf16),
            bundle,
        ],
        [me, updates, qg, cols, sums],
    )
    states = exchange(both)
    wide = like((HEADS, TOKENS, DV), f32)
    inner, inner_score, value_grad = call(
        local_body, [wide, square, wide], [kv, pair, num_grad, weight], cost=BIG
    )
    hidden_part = like((HEADS * CHUNK, DV), bf16)
    *hidden_sent, back_part, state, den_grad = call(
        functools.partial(hidden_body, n_ctx),
        [hidden_part] * 4 + [carried, like((HEADS, DK, DV), bf16), bundle],
        [y, states, extra, qg, inner, cols, norm_cols],
        [VMEM((TOKENS, DV), bf16), VMEM((8, CHUNK), f32)],
    )
    backs = exchange(back_part)
    hidden_received = shift_all(hidden_sent)
    *query_sent, terms, key_grad = call(
        score_body,
        [like((HEADS * CHUNK, DK), bf16)] * 4 + [bundle, like((HEADS, TOKENS, DK), f32)],
        [y, kv, qg, num_grad, weight, inner_score, state, norm, cols, den_grad],
        [VMEM((TOKENS, TOKENS), bf16), VMEM((TOKENS, DK), bf16)],
        cost=BIG,
    )
    query_received = shift_all(query_sent)
    home = lambda width: like((CHUNKS * HEADS, CHUNK, width), bf16)
    (hidden_home,) = call(unpack_plain_body, [home(DV)], [y, *hidden_received])
    grads_sent = call(
        functools.partial(grads_body, n_ctx),
        [like((HEADS * CHUNK + EXTRA, WIDE), bf16)] * 4,
        [y, me, backs, kv, key_grad, value_grad, lines, cols, terms, states, payload, norm, extra],
        [VMEM((HEADS, DK, DV), bf16), VMEM((TOKENS, WIDE), bf16), VMEM((CHUNK, CHUNK), f32)],
        after=[hidden_home],
    )
    grads_received = shift_all(grads_sent)
    (query_home,) = call(unpack_plain_body, [home(DK)], [y, *query_received], cost=BIG)
    gate = like((CHUNKS * HEADS, CHUNK), bf16)
    value_home, key_home, input_home, forget_home = call(
        unpack_body, [home(DV), home(DK), gate, gate], [y, *grads_received], after=[query_home]
    )
    return (hidden_home, query_home, key_home, value_home, input_home, forget_home)


def solution(mesh):
    spec = P(None, ("ctx", "head"), None)
    flat = P(None, ("ctx", "head"))
    return jax.shard_map(
        shards,
        mesh=mesh,
        in_specs=(spec, spec, spec, flat, flat, spec, P("ctx")),
        out_specs=(spec, spec, spec, spec, flat, flat),
        check_vma=False,
    )
```

time: 192 us -> 178 us (0.927)
  local copies, waits for them, and re-layouts: 11.6 us -> 48.5 us
  Pallas kernels: 44.1 us -> 21 us
  waiting for transfers between devices: 80.1 us -> 61.5 us
  starting transfers between devices: 53.9 us -> 44.8 us
    unnamed x40 -> x116, local copies, waits for them, and re-layouts: 5.11 us -> 48.5 us
    pallas_call x11 -> x12, Pallas kernels: 44.1 us -> 21 us  [call(): pl.pallas_call(run, out_shape=outs, in_specs=in_specs + [pl.BlockSpec(mem...]
    all_to_all x5 -> x3, waiting for transfers between devices: 21.9 us -> 6.69 us  [exchange(): return lax.all_to_all(part, 'ctx', split_axis=0, concat_axis=0, tiled=True)]
    all_to_all x5 -> x3, starting transfers between devices: 32.3 us -> 21.6 us  [exchange(): return lax.all_to_all(part, 'ctx', split_axis=0, concat_axis=0, tiled=True)]
    dynamic_slice x4 -> x0, local copies, waits for them, and re-layouts: 6.48 us -> none  [own(): lax.dynamic_slice_in_dim(part, y * HEADS, HEADS, 0)]
    ppermute x12 -> x15, waiting for transfers between devices: 58.2 us -> 54.9 us  [shift_all(): moved.append(lax.ppermute(part, 'head', pairs))]
    ppermute x12 -> x15, starting transfers between devices: 21.6 us -> 23.1 us  [shift_all(): moved.append(lax.ppermute(part, 'head', pairs))]
  transfers between devices with their start and end apart: 17 -> 18, of which waited for: 11 -> 8; matrix products, arithmetic and copies ran while one was open for 3% -> 0% of each run, Pallas kernels for 17% -> 4%
where the time goes in v2:
time: 178 us; the launch traced here: 177 us
  waiting for transfers between devices  61.5 us (35%)
  local copies, waits for them, and re-layouts  48.5 us (27%)
  starting transfers between devices  44.8 us (25%)
  Pallas kernels  21 us (12%)
    ppermute x15, waiting for transfers between devices, shift_all(): moved.append(lax.ppermute(part, 'head', pairs))  54.9 us
    unnamed x116, local copies, waits for them, and re-layouts  48.5 us
    ppermute x15, starting transfers between devices, shift_all(): moved.append(lax.ppermute(part, 'head', pairs))  23.1 us
    all_to_all x3, starting transfers between devices, exchange(): return lax.all_to_all(part, 'ctx', split_axis=0, concat_axis=0, tiled=True)  21.6 us
    pallas_call x12, Pallas kernels, call(): pl.pallas_call(run, out_shape=outs, in_specs=in_specs + [pl.BlockSpec(mem...  21 us
    all_to_all x3, waiting for transfers between devices, exchange(): return lax.all_to_all(part, 'ctx', split_axis=0, concat_axis=0, tiled=True)  6.69 us
  transfers between devices with their start and end apart: 18, of which 8 were waited for; matrix products, arithmetic and copies ran while one was open for 0% of the time, Pallas kernels for 4%

profile of v2, /device:TPU:2, one launch (start us, length us, event | category | flops | bytes accessed | tf_op | source)
XLA Modules:
  0.0 176.7 jit_solution(104452779668652842)
XLA Ops:
  0.6 1.2 copy-done.14
  1.9 1.0 copy-done.24
  4.4 1.6 collective-permute-start
  6.0 2.9 %collective-permute-start.1 = (bf16[272,768]{1,0:T(8,128)(2,1)S(1)}, bf16[272,768]{1,0:T(8,128)(2,1)S(1)}, u32[]{:S(2)}, u32[]{:S(2)}) collective-permute-start(bf16[272,768]{1,0:T(8,128)(2,1)S(1)} %get-tuple-element.53), channel_id=1, source_target_pairs={{0,2},{1,3},{2,0},{3,1},{4,6},{5,7},{6,4},{7,5},{8,10},{9,11},{10,... | collective-permute-start | bytes 1253384 | tf_op jit(solution)/shard_map/ppermute | solution.py:436
  8.9 1.3 collective-permute-start.2
  10.3 6.8 %collective-permute-done.refs_2_ = bf16[272,768]{1,0:T(8,128)(2,1)S(1)} collective-permute-done((bf16[272,768]{1,0:T(8,128)(2,1)S(1)}, bf16[272,768]{1,0:T(8,128)(2,1)S(1)}, u32[]{:S(2)}, u32[]{:S(2)}) %collective-permute-start) | collective-permute-done | bytes 417824 | tf_op jit(solution)/shard_map/ppermute | solution.py:436
  17.1 10.1 %collective-permute-done.1.refs_3_ = bf16[272,768]{1,0:T(8,128)(2,1)S(1)} collective-permute-done((bf16[272,768]{1,0:T(8,128)(2,1)S(1)}, bf16[272,768]{1,0:T(8,128)(2,1)S(1)}, u32[]{:S(2)}, u32[]{:S(2)}) %collective-permute-start.1) | collective-permute-done | bytes 417824 | tf_op jit(solution)/shard_map/ppermute | solution.py:436
  27.9 2.3 %shard_map.119 = (bf16[2,4,128,768]{3,2,1,0:T(8,128)(2,1)S(1)}, f32[2,128,128]{2,1,0:T(8,128)S(1)}, f32[2,128,128]{2,1,0:T(8,128)S(1)}, bf16[32,16,640]{2,1,0:T(8,128)(2,1)}) custom-call(s32[1]{0:T(128)} %bitcast.refs_0_, bf16[272,768]{1,0:T(8,128)(2,1)S(1)} %get-tuple-element.51.refs_1_, bf16[272,768]{1,0:T(8,128)(2,1)S(1)} %collective-permute-done.refs_2_, ...), custom_call_target="tpu_custom_call" | custom-call | flops 1 | bytes 1 | tf_op jit(solution)/shard_map/pallas_call | solution.py:60
  30.3 8.5 %all-to-all-start = ((bf16[32,16,640]{2,1,0:T(8,128)(2,1)}), bf16[32,16,640]{2,1,0:T(8,128)(2,1)}, u32[]{:S(2)}, u32[]{:S(2)}) async-start(bf16[32,16,640]{2,1,0:T(8,128)(2,1)} %get-tuple-element.55.refs_10_), calls=%async_computation | async-start | bytes 1310720 | tf_op jit(solution)/shard_map/all_to_all | solution.py:441
  38.8 1.1 shard_map.120
  40.6 1.2 collective-permute-start.3
  41.9 2.4 %collective-permute-start.4 = (bf16[256,768]{1,0:T(8,128)(2,1)}, bf16[256,768]{1,0:T(8,128)(2,1)S(1)}, u32[]{:S(2)}, u32[]{:S(2)}) collective-permute-start(bf16[256,768]{1,0:T(8,128)(2,1)} %get-tuple-element.58), channel_id=1, source_target_pairs={{0,2},{1,3},{2,0},{3,1},{4,6},{5,7},{6,4},{7,5},{8,10},{9,11},{10,... | collective-permute-start | bytes 1179656 | tf_op jit(solution)/shard_map/ppermute | solution.py:436
  44.3 1.6 collective-permute-start.5
  45.8 7.8 %collective-permute-done.3.refs_2_ = bf16[256,768]{1,0:T(8,128)(2,1)S(1)} collective-permute-done((bf16[256,768]{1,0:T(8,128)(2,1)}, bf16[256,768]{1,0:T(8,128)(2,1)S(1)}, u32[]{:S(2)}, u32[]{:S(2)}) %collective-permute-start.3) | collective-permute-done | bytes 393248 | tf_op jit(solution)/shard_map/ppermute | solution.py:436
  54.4 7.7 %collective-permute-done.4.refs_3_ = bf16[256,768]{1,0:T(8,128)(2,1)S(1)} collective-permute-done((bf16[256,768]{1,0:T(8,128)(2,1)}, bf16[256,768]{1,0:T(8,128)(2,1)S(1)}, u32[]{:S(2)}, u32[]{:S(2)}) %collective-permute-start.4) | collective-permute-done | bytes 393248 | tf_op jit(solution)/shard_map/ppermute | solution.py:436
  63.5 1.0 copy-done.27
  64.5 1.0 copy-done.29
  65.5 1.0 copy-done.31
  66.5 1.0 copy-done.33
  67.5 1.6 shard_map.121
  69.1 1.4 copy-done
  70.5 1.0 copy-done.17
  72.1 0.9 copy-done.43
  73.0 3.0 %shard_map.122 = (bf16[32,16,1024]{2,1,0:T(8,128)(2,1)S(1)}, f32[8,128]{1,0:T(8,128)S(1)}, f32[32,8,128]{2,1,0:T(8,128)S(1)}, bf16[2,512,512]{2,1,0:T(8,128)(2,1)S(1)}, f32[2,128,128]{2,1,0:T(8,128)S(1)}) custom-call(s32[1]{0:T(128)} %bitcast.1.refs_0_.refs_1_, bf16[32,16,640]{2,1,0:T(8,128)(2,1)} %all-to-all-done.refs_1_, ...), custom_call_target="tpu_custom_call" | custom-call | flops 1 | bytes 1 | tf_op jit(solution)/shard_map/pallas_call | solution.py:60
  76.1 1.0 copy-done.3
  77.0 1.0 copy-done.16
  78.7 7.4 %all-to-all-start.1 = ((bf16[32,16,1024]{2,1,0:T(8,128)(2,1)}), bf16[32,16,1024]{2,1,0:T(8,128)(2,1)}, u32[]{:S(2)}, u32[]{:S(2)}) async-start(bf16[32,16,1024]{2,1,0:T(8,128)(2,1)} %copy-done.16), calls=%async_computation.1 | async-start | bytes 2097152 | tf_op jit(solution)/shard_map/all_to_all | solution.py:441
  86.1 1.6 copy-done.1
  87.7 1.2 copy-done.4
  88.9 1.2 copy-done.18
  90.2 1.4 shard_map.123
  91.6 1.3 copy-done.8
  92.9 1.3 copy-done.10
  94.2 1.4 copy-done.12
  95.6 6.7 %all-to-all-done.1.refs_1_.refs_9_ = bf16[32,16,1024]{2,1,0:T(8,128)(2,1)} async-done(((bf16[32,16,1024]{2,1,0:T(8,128)(2,1)}), bf16[32,16,1024]{2,1,0:T(8,128)(2,1)}, u32[]{:S(2)}, u32[]{:S(2)}) %all-to-all-start.1) | async-done | bytes 1048608 | tf_op jit(solution)/shard_map/all_to_all | solution.py:441
  102.3 1.6 copy-done.13
  103.9 0.9 copy-done.45
  104.8 3.2 %shard_map.124 = (bf16[256,512]{1,0:T(8,128)(2,1)S(1)}, bf16[256,512]{1,0:T(8,128)(2,1)S(1)}, bf16[256,512]{1,0:T(8,128)(2,1)S(1)}, bf16[256,512]{1,0:T(8,128)(2...) custom-call(s32[1]{0:T(128)} %bitcast.refs_0_, ...), custom_call_target="tpu_custom_call" | custom-call | flops 1 | bytes 1 | tf_op jit(solution)/shard_map/pallas_call | solution.py:60
  108.0 0.9 copy-done.21
  113.2 5.7 %all-to-all-start.2 = ((bf16[32,16,640]{2,1,0:T(8,128)(2,1)}), bf16[32,16,640]{2,1,0:T(8,128)(2,1)}, u32[]{:S(2)}, u32[]{:S(2)}) async-start(bf16[32,16,640]{2,1,0:T(8,128)(2,1)} %copy-done.21), calls=%async_computation.2 | async-start | bytes 1310720 | tf_op jit(solution)/shard_map/all_to_all | solution.py:441
  118.9 1.3 collective-permute-start.6
  120.1 2.4 %collective-permute-start.7 = (bf16[256,512]{1,0:T(8,128)(2,1)}, bf16[256,512]{1,0:T(8,128)(2,1)S(1)}, u32[]{:S(2)}, u32[]{:S(2)}) collective-permute-start(bf16[256,512]{1,0:T(8,128)(2,1)} %copy-done.50), channel_id=1, source_target_pairs={{0,2},{1,3},{2,0},{3,1},{4,6},{5,7},{6,4},{7,5},{8,10},{9,11},{10,... | collective-permute-start | bytes 786440 | tf_op jit(solution)/shard_map/ppermute | solution.py:436
  122.5 1.1 collective-permute-start.8
  123.7 1.6 copy-done.2
  125.2 1.2 copy-done.5
  126.5 1.6 copy-done.11
  128.1 1.0 copy-done.23
  129.1 0.9 copy-done.39
  130.0 1.7 shard_map.126
  131.7 1.0 copy-done.19
  136.0 1.0 shard_map.125.refs_13_
  137.6 1.2 copy-done.6
  138.8 1.6 copy-done.9
  140.4 3.4 %shard_map.128 = (bf16[272,768]{1,0:T(8,128)(2,1)S(1)}, bf16[272,768]{1,0:T(8,128)(2,1)S(1)}, bf16[272,768]{1,0:T(8,128)(2,1)S(1)}, bf16[272,768]{1,0:T(8,128)(2,1)S(1)}) custom-call(s32[1]{0:T(128)} %bitcast.refs_0_, s32[1]{0:T(128)} %bitcast.1.refs_0_.refs_1_, bf16[32,16,640]{2,1,0:T(8,128)(2,1)} %all-to-all-done.2.refs_2_, ...), custom_call_target="tpu_custom_call" | custom-call | flops 1 | bytes 1 | tf_op jit(solution)/shard_map/pallas_call | solution.py:60
  143.8 1.0 collective-permute-start.12
  144.8 1.7 collective-permute-start.13
  146.5 1.5 collective-permute-start.14
  148.5 1.9 %collective-permute-start.10 = (bf16[256,256]{1,0:T(8,128)(2,1)S(1)}, bf16[256,256]{1,0:T(8,128)(2,1)S(1)}, u32[]{:S(2)}, u32[]{:S(2)}) collective-permute-start(bf16[256,256]{1,0:T(8,128)(2,1)S(1)} %copy-done.55), channel_id=1, source_target_pairs={{0,2},{1,3},{2,0},{3,1},{4,6},{5,7},{6,4},{7,5},{8,10},{9,11},{10,... | collective-permute-start | bytes 393224 | tf_op jit(solution)/shard_map/ppermute | solution.py:436
  150.4 18.2 %collective-permute-done.9.refs_2_ = bf16[256,256]{1,0:T(8,128)(2,1)S(1)} collective-permute-done((bf16[256,256]{1,0:T(8,128)(2,1)S(1)}, bf16[256,256]{1,0:T(8,128)(2,1)S(1)}, u32[]{:S(2)}, u32[]{:S(2)}) %collective-permute-start.9) | collective-permute-done | bytes 131104 | tf_op jit(solution)/shard_map/ppermute | solution.py:436
  169.3 1.3 collective-permute-done.10.refs_3_
  170.6 2.9 %collective-permute-done.11.refs_4_ = bf16[256,256]{1,0:T(8,128)(2,1)S(1)} collective-permute-done((bf16[256,256]{1,0:T(8,128)(2,1)S(1)}, bf16[256,256]{1,0:T(8,128)(2,1)S(1)}, u32[]{:S(2)}, u32[]{:S(2)}) %collective-permute-start.11) | collective-permute-done | bytes 131104 | tf_op jit(solution)/shard_map/ppermute | solution.py:436
  173.5 0.8 shard_map.127.refs_5_
  174.4 1.0 copy-done.7
  175.4 1.3 shard_map.129
  (100 shorter events, 15.9 us)
Async XLA Ops:
  0.6 1.2 copy-start.14
  1.9 1.0 copy-start.24
  4.3 34.5 %copy-start.15 = (bf16[8,128,512]{2,1,0:T(8,128)(2,1)S(1)}, bf16[8,128,512]{2,1,0:T(8,128)(2,1)}, u32[]{:S(2)}) copy-start(bf16[8,128,512]{2,1,0:T(8,128)(2,1)} %refs_2_.3) | copy-start | bytes 3145732
  4.3 34.5 %copy-start.25 = (bf16[8,128,256]{2,1,0:T(8,128)(2,1)S(1)}, bf16[8,128,256]{2,1,0:T(8,128)(2,1)}, u32[]{:S(2)}) copy-start(bf16[8,128,256]{2,1,0:T(8,128)(2,1)} %refs_1_.3) | copy-start | bytes 1572868
  4.4 12.7 %collective-permute-start = (bf16[272,768]{1,0:T(8,128)(2,1)S(1)}, bf16[272,768]{1,0:T(8,128)(2,1)S(1)}, u32[]{:S(2)}, u32[]{:S(2)}) collective-permute-start(bf16[272,768]{1,0:T(8,128)(2,1)S(1)} %get-tuple-element.52), channel_id=1, source_target_pairs={{0,1},{1,2},{2,3},{3,0},{4,5},{5,6},{6,7},{7,4},{8,9},{9,10},{10,1... | collective-permute-start | bytes 1253384 | tf_op jit(solution)/shard_map/ppermute | solution.py:436
  6.0 21.2 %collective-permute-start.1 = (bf16[272,768]{1,0:T(8,128)(2,1)S(1)}, bf16[272,768]{1,0:T(8,128)(2,1)S(1)}, u32[]{:S(2)}, u32[]{:S(2)}) collective-permute-start(bf16[272,768]{1,0:T(8,128)(2,1)S(1)} %get-tuple-element.53), channel_id=1, source_target_pairs={{0,2},{1,3},{2,0},{3,1},{4,6},{5,7},{6,4},{7,5},{8,10},{9,11},{10,... | collective-permute-start | bytes 1253384 | tf_op jit(solution)/shard_map/ppermute | solution.py:436
  8.9 18.3 %collective-permute-start.2 = (bf16[272,768]{1,0:T(8,128)(2,1)S(1)}, bf16[272,768]{1,0:T(8,128)(2,1)S(1)}, u32[]{:S(2)}, u32[]{:S(2)}) collective-permute-start(bf16[272,768]{1,0:T(8,128)(2,1)S(1)} %get-tuple-element.54), channel_id=1, source_target_pairs={{0,3},{1,0},{2,1},{3,2},{4,7},{5,4},{6,5},{7,6},{8,11},{9,8},{10,9... | collective-permute-start | bytes 1253384 | tf_op jit(solution)/shard_map/ppermute | solution.py:436
  30.3 41.9 %all-to-all-start = ((bf16[32,16,640]{2,1,0:T(8,128)(2,1)}), bf16[32,16,640]{2,1,0:T(8,128)(2,1)}, u32[]{:S(2)}, u32[]{:S(2)}) async-start(bf16[32,16,640]{2,1,0:T(8,128)(2,1)} %get-tuple-element.55.refs_10_), calls=%async_computation | async-start | bytes 1310720 | tf_op jit(solution)/shard_map/all_to_all | solution.py:441
  39.9 0.7 copy-start.26
  40.6 13.0 %collective-permute-start.3 = (bf16[256,768]{1,0:T(8,128)(2,1)}, bf16[256,768]{1,0:T(8,128)(2,1)S(1)}, u32[]{:S(2)}, u32[]{:S(2)}) collective-permute-start(bf16[256,768]{1,0:T(8,128)(2,1)} %get-tuple-element.57), channel_id=1, source_target_pairs={{0,1},{1,2},{2,3},{3,0},{4,5},{5,6},{6,7},{7,4},{8,9},{9,10},{10,1... | collective-permute-start | bytes 1179656 | tf_op jit(solution)/shard_map/ppermute | solution.py:436
  41.9 20.2 %collective-permute-start.4 = (bf16[256,768]{1,0:T(8,128)(2,1)}, bf16[256,768]{1,0:T(8,128)(2,1)S(1)}, u32[]{:S(2)}, u32[]{:S(2)}) collective-permute-start(bf16[256,768]{1,0:T(8,128)(2,1)} %get-tuple-element.58), channel_id=1, source_target_pairs={{0,2},{1,3},{2,0},{3,1},{4,6},{5,7},{6,4},{7,5},{8,10},{9,11},{10,... | collective-permute-start | bytes 1179656 | tf_op jit(solution)/shard_map/ppermute | solution.py:436
  44.3 18.5 %collective-permute-start.5 = (bf16[256,768]{1,0:T(8,128)(2,1)}, bf16[256,768]{1,0:T(8,128)(2,1)S(1)}, u32[]{:S(2)}, u32[]{:S(2)}) collective-permute-start(bf16[256,768]{1,0:T(8,128)(2,1)} %get-tuple-element.59), channel_id=1, source_target_pairs={{0,3},{1,0},{2,1},{3,2},{4,7},{5,4},{6,5},{7,6},{8,11},{9,8},{10,9... | collective-permute-start | bytes 1179656 | tf_op jit(solution)/shard_map/ppermute | solution.py:436
  53.6 0.7 copy-start.28
  62.0 0.7 copy-start.30
  62.8 0.7 copy-start.32
  63.5 1.0 copy-start.27
  64.5 1.0 copy-start.29
  65.5 1.0 copy-start.31
  66.5 1.0 copy-start.33
  69.1 1.4 copy-start
  70.5 1.0 copy-start.17
  72.1 0.9 copy-start.43
  76.1 1.0 copy-start.3
  77.0 1.0 copy-start.16
  78.7 23.6 %all-to-all-start.1 = ((bf16[32,16,1024]{2,1,0:T(8,128)(2,1)}), bf16[32,16,1024]{2,1,0:T(8,128)(2,1)}, u32[]{:S(2)}, u32[]{:S(2)}) async-start(bf16[32,16,1024]{2,1,0:T(8,128)(2,1)} %copy-done.16), calls=%async_computation.1 | async-start | bytes 2097152 | tf_op jit(solution)/shard_map/all_to_all | solution.py:441
  86.1 1.6 copy-start.1
  87.7 1.2 copy-start.4
  88.9 1.2 copy-start.18
  91.6 1.3 copy-start.8
  92.9 1.3 copy-start.10
  94.2 1.4 copy-start.12
  102.3 1.6 copy-start.13
  103.9 0.9 copy-start.45
  108.0 0.9 copy-start.21
  108.9 0.8 copy-start.22
  109.7 0.7 copy-start.34
  111.0 0.7 copy-start.49
  111.8 0.7 copy-start.50
  113.2 23.8 %all-to-all-start.2 = ((bf16[32,16,640]{2,1,0:T(8,128)(2,1)}), bf16[32,16,640]{2,1,0:T(8,128)(2,1)}, u32[]{:S(2)}, u32[]{:S(2)}) async-start(bf16[32,16,640]{2,1,0:T(8,128)(2,1)} %copy-done.21), calls=%async_computation.2 | async-start | bytes 1310720 | tf_op jit(solution)/shard_map/all_to_all | solution.py:441
  118.9 17.1 %collective-permute-start.6 = (bf16[256,512]{1,0:T(8,128)(2,1)}, bf16[256,512]{1,0:T(8,128)(2,1)S(1)}, u32[]{:S(2)}, u32[]{:S(2)}) collective-permute-start(bf16[256,512]{1,0:T(8,128)(2,1)} %copy-done.51), channel_id=1, source_target_pairs={{0,1},{1,2},{2,3},{3,0},{4,5},{5,6},{6,7},{7,4},{8,9},{9,10},{10,1... | collective-permute-start | bytes 786440 | tf_op jit(solution)/shard_map/ppermute | solution.py:436
  120.1 15.8 %collective-permute-start.7 = (bf16[256,512]{1,0:T(8,128)(2,1)}, bf16[256,512]{1,0:T(8,128)(2,1)S(1)}, u32[]{:S(2)}, u32[]{:S(2)}) collective-permute-start(bf16[256,512]{1,0:T(8,128)(2,1)} %copy-done.50), channel_id=1, source_target_pairs={{0,2},{1,3},{2,0},{3,1},{4,6},{5,7},{6,4},{7,5},{8,10},{9,11},{10,... | collective-permute-start | bytes 786440 | tf_op jit(solution)/shard_map/ppermute | solution.py:436
  122.5 13.4 %collective-permute-start.8 = (bf16[256,512]{1,0:T(8,128)(2,1)}, bf16[256,512]{1,0:T(8,128)(2,1)S(1)}, u32[]{:S(2)}, u32[]{:S(2)}) collective-permute-start(bf16[256,512]{1,0:T(8,128)(2,1)} %copy-done.49), channel_id=1, source_target_pairs={{0,3},{1,0},{2,1},{3,2},{4,7},{5,4},{6,5},{7,6},{8,11},{9,8},{10,9... | collective-permute-start | bytes 786440 | tf_op jit(solution)/shard_map/ppermute | solution.py:436
  123.7 1.6 copy-start.2
  125.2 1.2 copy-start.5
  126.5 1.6 copy-start.11
  128.1 1.0 copy-start.23
  129.1 0.9 copy-start.39
  130.0 6.0 %copy-start.35 = (bf16[256,512]{1,0:T(8,128)(2,1)S(1)}, bf16[256,512]{1,0:T(8,128)(2,1)}, u32[]{:S(2)}) copy-start(bf16[256,512]{1,0:T(8,128)(2,1)} %copy-done.34) | copy-start | bytes 786436
  131.7 1.0 copy-start.19
  135.9 1.6 copy-start.20
  135.9 1.6 copy-start.37
  137.6 1.2 copy-start.6
  138.8 1.6 copy-start.9
  140.4 7.6 %copy-start.57 = (bf16[256,256]{1,0:T(8,128)(2,1)S(1)}, bf16[256,256]{1,0:T(8,128)(2,1)}, u32[]{:S(2)}) copy-start(bf16[256,256]{1,0:T(8,128)(2,1)} %copy-done.56) | copy-start | bytes 393220
  140.4 8.1 %copy-start.55 = (bf16[256,256]{1,0:T(8,128)(2,1)S(1)}, bf16[256,256]{1,0:T(8,128)(2,1)}, u32[]{:S(2)}) copy-start(bf16[256,256]{1,0:T(8,128)(2,1)} %copy-done.54) | copy-start | bytes 393220
  140.4 28.2 %copy-start.53 = (bf16[256,256]{1,0:T(8,128)(2,1)S(1)}, bf16[256,256]{1,0:T(8,128)(2,1)}, u32[]{:S(2)}) copy-start(bf16[256,256]{1,0:T(8,128)(2,1)} %copy-done.52) | copy-start | bytes 393220
  140.4 33.2 %copy-start.41 = (bf16[256,256]{1,0:T(8,128)(2,1)S(1)}, bf16[256,256]{1,0:T(8,128)(2,1)}, u32[]{:S(2)}) copy-start(bf16[256,256]{1,0:T(8,128)(2,1)} %copy-done.40) | copy-start | bytes 393220
  143.8 30.6 %collective-permute-start.12 = (bf16[272,768]{1,0:T(8,128)(2,1)S(1)}, bf16[272,768]{1,0:T(8,128)(2,1)S(1)}, u32[]{:S(2)}, u32[]{:S(2)}) collective-permute-start(bf16[272,768]{1,0:T(8,128)(2,1)S(1)} %get-tuple-element.89), channel_id=1, source_target_pairs={{0,1},{1,2},{2,3},{3,0},{4,5},{5,6},{6,7},{7,4},{8,9},{9,10},{10,1... | collective-permute-start | bytes 1253384 | tf_op jit(solution)/shard_map/ppermute | solution.py:436
  144.8 29.6 %collective-permute-start.13 = (bf16[272,768]{1,0:T(8,128)(2,1)S(1)}, bf16[272,768]{1,0:T(8,128)(2,1)S(1)}, u32[]{:S(2)}, u32[]{:S(2)}) collective-permute-start(bf16[272,768]{1,0:T(8,128)(2,1)S(1)} %get-tuple-element.90), channel_id=1, source_target_pairs={{0,2},{1,3},{2,0},{3,1},{4,6},{5,7},{6,4},{7,5},{8,10},{9,11},{10,... | collective-permute-start | bytes 1253384 | tf_op jit(solution)/shard_map/ppermute | solution.py:436
  146.5 27.9 %collective-permute-start.14 = (bf16[272,768]{1,0:T(8,128)(2,1)S(1)}, bf16[272,768]{1,0:T(8,128)(2,1)S(1)}, u32[]{:S(2)}, u32[]{:S(2)}) collective-permute-start(bf16[272,768]{1,0:T(8,128)(2,1)S(1)} %get-tuple-element.91), channel_id=1, source_target_pairs={{0,3},{1,0},{2,1},{3,2},{4,7},{5,4},{6,5},{7,6},{8,11},{9,8},{10,9... | collective-permute-start | bytes 1253384 | tf_op jit(solution)/shard_map/ppermute | solution.py:436
  148.0 20.6 %collective-permute-start.9 = (bf16[256,256]{1,0:T(8,128)(2,1)S(1)}, bf16[256,256]{1,0:T(8,128)(2,1)S(1)}, u32[]{:S(2)}, u32[]{:S(2)}) collective-permute-start(bf16[256,256]{1,0:T(8,128)(2,1)S(1)} %copy-done.57), channel_id=1, source_target_pairs={{0,1},{1,2},{2,3},{3,0},{4,5},{5,6},{6,7},{7,4},{8,9},{9,10},{10,1... | collective-permute-start | bytes 393224 | tf_op jit(solution)/shard_map/ppermute | solution.py:436
  148.5 22.1 %collective-permute-start.10 = (bf16[256,256]{1,0:T(8,128)(2,1)S(1)}, bf16[256,256]{1,0:T(8,128)(2,1)S(1)}, u32[]{:S(2)}, u32[]{:S(2)}) collective-permute-start(bf16[256,256]{1,0:T(8,128)(2,1)S(1)} %copy-done.55), channel_id=1, source_target_pairs={{0,2},{1,3},{2,0},{3,1},{4,6},{5,7},{6,4},{7,5},{8,10},{9,11},{10,... | collective-permute-start | bytes 393224 | tf_op jit(solution)/shard_map/ppermute | solution.py:436
  168.6 5.0 %collective-permute-start.11 = (bf16[256,256]{1,0:T(8,128)(2,1)S(1)}, bf16[256,256]{1,0:T(8,128)(2,1)S(1)}, u32[]{:S(2)}, u32[]{:S(2)}) collective-permute-start(bf16[256,256]{1,0:T(8,128)(2,1)S(1)} %copy-done.53), channel_id=1, source_target_pairs={{0,3},{1,0},{2,1},{3,2},{4,7},{5,4},{6,5},{7,6},{8,11},{9,8},{10,9... | collective-permute-start | bytes 393224 | tf_op jit(solution)/shard_map/ppermute | solution.py:436
  174.4 1.0 copy-start.7
  (12 other events, 8.0 us)

commit v3 on v2

--- a/solution.py
+++ b/solution.py
@@ -15,11 +15,11 @@
 EXTRA = 16
 SLICES = 32
 NEG = -1e30
-BIG = 10**8
+BIG = 10**10
 SCALE = DK ** (-0.5)
 ROWS = 256
 VMEM = pltpu.VMEM
-PARAMS = pltpu.CompilerParams(vmem_limit_bytes=16 * 1024 * 1024)
+PARAMS = pltpu.CompilerParams(vmem_limit_bytes=28 * 1024 * 1024)
 
 
 def dot(left, right, cl, cr, precision=None):
@@ -52,53 +52,159 @@
     return pl.BlockSpec(memory_space=VMEM)
 
 
-def call(body, outs, ins, scratch=(), cost=1, after=()):
+def pieces(source, target, sem, lanes=None):
+    count = HEADS if source.shape[0] == HEADS else 1
+    copies = []
+    for h in range(count):
+        pick = (h,) if count > 1 else (slice(None),)
+        at = lambda ref, cut: ref.at[pick + cut] if cut or count > 1 else ref
+        cut = (slice(None),) * (len(source.shape) - 2) + (pl.ds(0, lanes),) if lanes else ()
+        copies.append(pltpu.make_async_copy(at(source, cut), at(target, ()), sem.at[h]))
+    return copies
+
+
+class Far:
+    def __init__(self, ref, held, sem, lanes):
+        self.ref, self.copies = held, dict(enumerate(pieces(ref, held, sem, lanes)))
+        self.shape = held.shape
+
+    def start(self, h):
+        if h in self.copies:
+            self.copies[h].start()
+
+    def finish(self):
+        for h in list(self.copies):
+            self.copies.pop(h).wait()
+
+    def __getitem__(self, index):
+        first = index[0] if isinstance(index, tuple) else index
+        if isinstance(first, int) and self.shape[0] == HEADS:
+            if first in self.copies:
+                self.copies.pop(first).wait()
+        else:
+            self.finish()
+        return self.ref[index]
+
+
+class FarOut:
+    def __init__(self, ref, held, sem):
+        self.ref, self.copies = held, pieces(held, ref, sem)
+        self.shape, self.sent = held.shape, 0
+
+    def send(self, upto):
+        while self.sent < upto:
+            self.copies[self.sent].start()
+            self.sent += 1
+
+    def finish(self):
+        for copy in self.copies:
+            copy.wait()
+
+    def __getitem__(self, index):
+        return self.ref[index]
+
+    def __setitem__(self, index, value):
+        first = index[0] if isinstance(index, tuple) else index
+        if isinstance(first, int) and len(self.copies) > 1:
+            self.send(first)
+        self.ref[index] = value
+
+
+def call(body, outs, ins, scratch=(), cost=1, after=(), far=(), raw=(), loose=(), far_outs=(), raw_outs=()):
+    far = dict(far) if isinstance(far, dict) else {i: None for i in far}
+    hbm = pl.BlockSpec(memory_space=pltpu.HBM)
+    free = pl.BlockSpec(memory_space=pl.ANY)
+    buffers = [VMEM(ins[i].shape[:-1] + (n or ins[i].shape[-1],), ins[i].dtype) for i, n in far.items()]
+    buffers += [VMEM(outs[i].shape, outs[i].dtype) for i in far_outs]
+
     def run(*refs):
-        body(*refs[: len(ins)], *refs[len(ins) + len(after) :])
-
-    in_specs = [smem() if a.dtype == jnp.int32 and a.size <= 2 else whole() for a in ins]
+        in_refs = list(refs[: len(ins)])
+        refs = refs[len(ins) + len(after) :]
+        out_refs, refs = list(refs[: len(outs)]), refs[len(outs) :]
+        own, held, sems = refs[: len(scratch)], refs[len(scratch) :], refs[-1]
+        for k, (i, lanes) in enumerate(far.items()):
+            in_refs[i] = Far(in_refs[i], held[k], sems.at[k], lanes)
+        for h in range(HEADS):
+            for i in far:
+                in_refs[i].start(h)
+        for k, i in enumerate(far_outs, len(far)):
+            out_refs[i] = FarOut(out_refs[i], held[k], sems.at[k])
+        body(*in_refs, *out_refs, *own)
+        for i in far_outs:
+            out_refs[i].send(len(out_refs[i].copies))
+        for i in far:
+            in_refs[i].finish()
+        for i in far_outs:
+            out_refs[i].finish()
+
+    def place(i, a):
+        if a.dtype == jnp.int32 and a.size <= 2:
+            return smem()
+        return free if i in loose else hbm if i in far or i in raw else whole()
+
+    def pin(i, a):
+        held = (i in far or i in raw) and i not in loose
+        return pltpu.with_memory_space_constraint(a, pltpu.HBM) if held else a
+
+    far_all = set(far_outs) | set(raw_outs)
     return pl.pallas_call(
         run,
-        out_shape=outs,
-        in_specs=in_specs + [pl.BlockSpec(memory_space=pl.ANY) for _ in after],
-        out_specs=tuple(whole() for _ in outs),
-        scratch_shapes=scratch,
+        out_shape=[pltpu.HBM(o.shape, o.dtype) if i in far_all else o for i, o in enumerate(outs)],
+        in_specs=[place(i, a) for i, a in enumerate(ins)] + [hbm if a.ndim == 3 else free for a in after],
+        out_specs=tuple(hbm if i in far_all else whole() for i in range(len(outs))),
+        scratch_shapes=[*scratch, *buffers, pltpu.SemaphoreType.DMA((max(1, len(buffers)), HEADS))],
         compiler_params=PARAMS,
         cost_estimate=pl.CostEstimate(flops=cost, bytes_accessed=cost, transcendentals=0),
-    )(*ins, *after)
+    )(*[pin(i, a) for i, a in enumerate(ins)], *(pltpu.with_memory_space_constraint(a, pltpu.HBM) if a.ndim == 3 else a for a in after))
 
 
 def like(shape, dtype):
     return jax.ShapeDtypeStruct(shape, dtype)
 
 
+def run_copies(pairs, sems):
+    copies = [pltpu.make_async_copy(a, b, sems.at[k]) for k, (a, b) in enumerate(pairs)]
+    for copy in copies:
+        copy.start()
+    return copies
+
+
 def pack_body(gates, y_ref, a_ref, b_ref, *rest):
-    outs = rest[-4:]
-    y = y_ref[0]
-    for shift, out in enumerate(outs):
-        dest = chunk_of(y, shift)
+    *rest, sems = rest
+    outs = rest[-CHUNKS:]
+    pairs = []
+    for shift in (1, 3, 2, 0):
+        dest = chunk_of(y_ref[0], shift)
         for h in range(HEADS):
-            out[h * CHUNK : (h + 1) * CHUNK, 0:DK] = a_ref[dest * HEADS + h]
-            out[h * CHUNK : (h + 1) * CHUNK, DK:WIDE] = b_ref[dest * HEADS + h]
-        if gates:
-            both = jnp.concatenate([rest[0][...].astype(f32), rest[1][...].astype(f32)], axis=0)
+            rows = pl.ds(h * CHUNK, CHUNK)
+            pairs.append((a_ref.at[dest * HEADS + h], outs[shift].at[rows, pl.ds(0, DK)]))
+            pairs.append((b_ref.at[dest * HEADS + h], outs[shift].at[rows, pl.ds(DK, DV)]))
+    copies = run_copies(pairs, sems)
+    if gates:
+        both = jnp.concatenate([rest[0][...].astype(f32), rest[1][...].astype(f32)], axis=0)
+        for out in outs:
             out[HEADS * CHUNK : HEADS * CHUNK + EXTRA, 0:CHUNK] = both.astype(bf16)
-
-
-def pack(y, narrow, wide, gates=()):
+    for copy in copies:
+        copy.wait()
+
+
+def pack(y, narrow, wide, gates=(), after=()):
     rows = HEADS * CHUNK + (EXTRA if gates else 0)
     return call(
         functools.partial(pack_body, bool(gates)),
-        [like((rows, WIDE), bf16)] * 4,
+        [like((rows, WIDE), bf16)] * CHUNKS,
         [y, narrow, wide, *gates],
+        [pltpu.SemaphoreType.DMA((4 * CHUNKS,))],
+        after=after,
+        far=(3, 4) if gates else (),
+        raw=(1, 2),
     )
 
 
 def assemble(all_ref, y, received):
-    for shift, ref in enumerate(received):
-        source = chunk_of(y, -shift)
-        for h in range(HEADS):
-            all_ref[h, source] = ref[h * CHUNK : (h + 1) * CHUNK, :]
+    for h in range(HEADS):
+        for shift, ref in enumerate(received):
+            all_ref[h, chunk_of(y, -shift)] = ref[h * CHUNK : (h + 1) * CHUNK, :]
 
 
 def update_body(
@@ -200,7 +306,7 @@
             here = slice(r * ROWS, last)
             scores = dot(query[here], keys[0:last], 1, 1) * SCALE
             weight = weights(line_ref, col_ref, h, r)
-            weight_ref[h, here, 0:last] = weight
+            weight_ref[h, here, 0:last] = weight.astype(bf16)
             pair = (weight * scores).astype(bf16)
             pair_ref[h, here, 0:last] = pair
             put_column(sum_ref, h, 0, jnp.sum(pair.astype(f32), axis=1, keepdims=True), r)
@@ -267,12 +373,14 @@
         for r in range(TOKENS // ROWS):
             last = (r + 1) * ROWS
             here = slice(r * ROWS, last)
-            inner_ref[h, here] = dot(pair_ref[h, here, 0:last], values[0:last], 1, 0)
-            score_ref[h, here, 0:last] = weight_ref[h, here, 0:last] * dot(num_ref[h, here], values[0:last], 1, 1)
+            inner_ref[h, here] = dot(pair_ref[h, here, 0:last], values[0:last], 1, 0).astype(bf16)
+            inner = dot(num_ref[h, here], values[0:last], 1, 1)
+            score_ref[h, here, 0:last] = (weight_ref[h, here, 0:last].astype(f32) * inner).astype(bf16)
         for s in range(TOKENS // ROWS):
             first = s * ROWS
             here = slice(first, first + ROWS)
-            value_ref[h, here] = dot(pair_ref[h, first:TOKENS, here], num_ref[h, first:TOKENS], 0, 0)
+            inner = dot(pair_ref[h, first:TOKENS, here], num_ref[h, first:TOKENS], 0, 0)
+            value_ref[h, here] = inner.astype(bf16)
 
 
 def hidden_body(
@@ -293,7 +401,8 @@
             chunks = slice(r * ROWS // CHUNK, (r + 1) * ROWS // CHUNK)
             query = qg_ref[h, chunks, :, 0:DK].reshape(ROWS, DK)
             grad = qg_ref[h, chunks, :, DK:WIDE].reshape(ROWS, DV)
-            hidden = (inner_ref[h, here] + beta[here] * dot(query, state, 1, 0)) * inverse[here]
+            cross = beta[here] * dot(query, state, 1, 0)
+            hidden = (inner_ref[h, here].astype(f32) + cross) * inverse[here]
             done[here, :] = hidden.astype(bf16)
             product = jnp.sum(grad.astype(f32) * hidden, axis=1, keepdims=True)
             den_grad = product * factor[here]
@@ -331,9 +440,9 @@
         for r in range(TOKENS // ROWS):
             last = (r + 1) * ROWS
             here = slice(r * ROWS, last)
-            score[here, 0:last] = (
-                inner_ref[h, here, 0:last] + weight_ref[h, here, 0:last] * den_grad[here]
-            ).astype(bf16)
+            weight = weight_ref[h, here, 0:last].astype(f32)
+            inner = inner_ref[h, here, 0:last].astype(f32)
+            score[here, 0:last] = (inner + weight * den_grad[here]).astype(bf16)
             from_state = dot(num_ref[h, here], state, 1, 1) + den_grad[here] * norm_bf
             query_grad = dot(score[here, 0:last], keys[0:last], 1, 0) * SCALE + beta[here] * from_state
             done[here, :] = query_grad.astype(bf16)
@@ -343,7 +452,8 @@
         for s in range(TOKENS // ROWS):
             first = s * ROWS
             here = slice(first, first + ROWS)
-            key_ref[h, here] = dot(score[first:TOKENS, here], query[first:TOKENS], 0, 0) * SCALE
+            inner = dot(score[first:TOKENS, here], query[first:TOKENS], 0, 0) * SCALE
+            key_ref[h, here] = inner.astype(bf16)
 
 
 def grads_body(
@@ -373,8 +483,8 @@
         row = jnp.concatenate([back_n[2 * h : 2 * h + 1], back_n[2 * h + 1 : 2 * h + 2]], axis=1)
         for r in range(TOKENS // ROWS):
             here = slice(r * ROWS, (r + 1) * ROWS)
-            key_grad = key_ref[h, here] + alpha[here] * (dot(values[here], back_bf, 1, 1) + row)
-            value_grad = value_ref[h, here] + alpha[here] * dot(keys[here], back_bf, 1, 0)
+            key_grad = key_ref[h, here].astype(f32) + alpha[here] * (dot(values[here], back_bf, 1, 1) + row)
+            value_grad = value_ref[h, here].astype(f32) + alpha[here] * dot(keys[here], back_bf, 1, 0)
             done[here, 0:DV] = value_grad.astype(bf16)
             done[here, DV : DV + DK] = key_grad.astype(bf16)
             key_term = jnp.sum(keys[here].astype(f32) * key_grad, axis=1, keepdims=True)
@@ -405,28 +515,45 @@
         out[HEADS * CHUNK : HEADS * CHUNK + EXTRA, 0:CHUNK] = cols[pl.ds(first, 16), :].astype(bf16)
 
 
-def unpack_plain_body(y_ref, r0, r1, r2, r3, out_ref):
+def unpack_plain_body(y_ref, r0, r1, r2, r3, out_ref, sems):
+    pairs = []
+    for shift, ref in ((1, r1), (2, r2), (3, r3), (0, r0)):
+        source = chunk_of(y_ref[0], -shift)
+        if shift == 0:
+            copies = run_copies(pairs, sems)
+            r0.finish()
+            pairs, ref = [], r0.ref
+        for h in range(HEADS):
+            pairs.append((ref.at[pl.ds(h * CHUNK, CHUNK), :], out_ref.at[source * HEADS + h]))
+    for copy in copies + run_copies(pairs, sems.at[pl.ds(6, 2)]):
+        copy.wait()
+
+
+def unpack_body(y_ref, r0, r1, r2, r3, wide_ref, narrow_ref, input_ref, forget_ref, tiles, sems):
+    y = y_ref[0]
+    pairs = []
     for shift, ref in enumerate((r0, r1, r2, r3)):
-        source = chunk_of(y_ref[0], -shift)
+        pairs.append((ref.at[pl.ds(HEADS * CHUNK, EXTRA), pl.ds(0, CHUNK)], tiles.at[shift]))
+    for shift, ref in enumerate((r0, r1, r2, r3)):
+        source = chunk_of(y, -shift)
         for h in range(HEADS):
-            out_ref[source * HEADS + h] = ref[h * CHUNK : (h + 1) * CHUNK, :]
-
-
-def unpack_body(y_ref, r0, r1, r2, r3, wide_ref, narrow_ref, input_ref, forget_ref):
-    y = y_ref[0]
+            rows = pl.ds(h * CHUNK, CHUNK)
+            pairs.append((ref.at[rows, pl.ds(0, DV)], wide_ref.at[source * HEADS + h]))
+            pairs.append((ref.at[rows, pl.ds(DV, DK)], narrow_ref.at[source * HEADS + h]))
+    copies = run_copies(pairs, sems)
     row = lax.broadcasted_iota(jnp.int32, (8, CHUNK), 0)
     sums = [jnp.zeros((8, CHUNK), f32)] * 2
-    for shift, ref in enumerate((r0, r1, r2, r3)):
-        source = chunk_of(y, -shift)
-        tile = ref[HEADS * CHUNK : HEADS * CHUNK + EXTRA, 0:CHUNK].astype(f32)
+    for shift in range(CHUNKS):
+        copies[shift].wait()
+        tile = tiles[shift].astype(f32)
         for h in range(HEADS):
-            wide_ref[source * HEADS + h] = ref[h * CHUNK : (h + 1) * CHUNK, 0:DV]
-            narrow_ref[source * HEADS + h] = ref[h * CHUNK : (h + 1) * CHUNK, DV : DV + DK]
             for k in range(2):
-                here = jnp.where(row == source * HEADS + h, tile[2 * k + h : 2 * k + h + 1], 0.0)
-                sums[k] = sums[k] + here
+                here = row == chunk_of(y, -shift) * HEADS + h
+                sums[k] = sums[k] + jnp.where(here, tile[2 * k + h : 2 * k + h + 1], 0.0)
     input_ref[...] = sums[0].astype(bf16)
     forget_ref[...] = sums[1].astype(bf16)
+    for copy in copies[CHUNKS:]:
+        copy.wait()
 
 
 def shift_all(parts):
@@ -437,6 +564,24 @@
     return moved
 
 
+def home(width):
+    return like((CHUNKS * HEADS, CHUNK, width), bf16)
+
+
+def unpack(y, received, width, cost=1):
+    return call(
+        unpack_plain_body,
+        [home(width)],
+        [y, *received],
+        [pltpu.SemaphoreType.DMA((2 * CHUNKS,))],
+        cost=cost,
+        far=(1,),
+        raw=(2, 3, 4),
+        loose=(2, 3, 4),
+        raw_outs=(0,),
+    )
+
+
 def exchange(part):
     return lax.all_to_all(part, "ctx", split_axis=0, concat_axis=0, tiled=True)
 
@@ -446,10 +591,9 @@
     y = lax.axis_index("head").astype(jnp.int32).reshape(1)
     me = lax.axis_index("ctx").astype(jnp.int32).reshape(1)
     kv_received = shift_all(pack(y, keys, values, (igate, fgate)))
-    qg_received = shift_all(pack(y, query, hidden_output_gradient))
+    qg_received = shift_all(pack(y, query, hidden_output_gradient, after=[kv_received[1]]))
     tokens = like((HEADS, CHUNKS, CHUNK, WIDE), bf16)
     bundle = like((HEADS, CHUNK, CHUNK), f32)
-    square = like((HEADS, TOKENS, TOKENS), f32)
     square_bf = like((HEADS, TOKENS, TOKENS), bf16)
     carried = like((SLICES, 16, 2 * DK + CHUNK), bf16)
     kv, lines, cols, payload = call(
@@ -457,10 +601,18 @@
         [tokens, bundle, bundle, carried],
         [y, *kv_received, doc_start.reshape(CHUNKS, CHUNK)],
         [VMEM((CHUNKS, 16, CHUNK), f32), VMEM((2, 16, CHUNK), f32), VMEM((8, CHUNK), f32)],
+        far=(5,),
+        far_outs=(0, 3),
     )
     updates = exchange(payload)
     qg, pair, weight, sums = call(
-        pair_body, [tokens, square_bf, square, bundle], [y, *qg_received, kv, lines, cols], cost=BIG
+        pair_body,
+        [tokens, square_bf, square_bf, bundle],
+        [y, *qg_received, kv, lines, cols],
+        cost=BIG,
+        far={5: DK, 1: None, 2: None, 3: None, 4: None},
+        loose=(1, 2, 3, 4),
+        far_outs=(1, 2, 3),
     )
     both, norm, extra, num_grad, norm_cols = call(
         functools.partial(adjoint_body, n_ctx),
@@ -472,11 +624,19 @@
             bundle,
         ],
         [me, updates, qg, cols, sums],
+        far=(1, 4),
+        loose=(1,),
+        far_outs=(0, 3, 4),
     )
     states = exchange(both)
-    wide = like((HEADS, TOKENS, DV), f32)
+    wide = like((HEADS, TOKENS, DV), bf16)
     inner, inner_score, value_grad = call(
-        local_body, [wide, square, wide], [kv, pair, num_grad, weight], cost=BIG
+        local_body,
+        [wide, square_bf, wide],
+        [kv, pair, num_grad, weight],
+        cost=BIG,
+        far=(0, 1, 2, 3),
+        far_outs=(0, 1, 2),
     )
     hidden_part = like((HEADS * CHUNK, DV), bf16)
     *hidden_sent, back_part, state, den_grad = call(
@@ -484,31 +644,44 @@
         [hidden_part] * 4 + [carried, like((HEADS, DK, DV), bf16), bundle],
         [y, states, extra, qg, inner, cols, norm_cols],
         [VMEM((TOKENS, DV), bf16), VMEM((8, CHUNK), f32)],
+        far=(1, 6, 4),
+        loose=(1,),
+        far_outs=(0, 1, 2, 3, 4, 5, 6),
     )
     backs = exchange(back_part)
     hidden_received = shift_all(hidden_sent)
     *query_sent, terms, key_grad = call(
         score_body,
-        [like((HEADS * CHUNK, DK), bf16)] * 4 + [bundle, like((HEADS, TOKENS, DK), f32)],
+        [like((HEADS * CHUNK, DK), bf16)] * 4 + [bundle, like((HEADS, TOKENS, DK), bf16)],
         [y, kv, qg, num_grad, weight, inner_score, state, norm, cols, den_grad],
         [VMEM((TOKENS, TOKENS), bf16), VMEM((TOKENS, DK), bf16)],
         cost=BIG,
+        far={9: None, 5: None, 4: None, 3: None, 6: None, 1: DK},
+        far_outs=(0, 1, 2, 3, 4, 5),
     )
     query_received = shift_all(query_sent)
-    home = lambda width: like((CHUNKS * HEADS, CHUNK, width), bf16)
-    (hidden_home,) = call(unpack_plain_body, [home(DV)], [y, *hidden_received])
+    (hidden_home,) = unpack(y, hidden_received, DV)
     grads_sent = call(
         functools.partial(grads_body, n_ctx),
         [like((HEADS * CHUNK + EXTRA, WIDE), bf16)] * 4,
         [y, me, backs, kv, key_grad, value_grad, lines, cols, terms, states, payload, norm, extra],
         [VMEM((HEADS, DK, DV), bf16), VMEM((TOKENS, WIDE), bf16), VMEM((CHUNK, CHUNK), f32)],
         after=[hidden_home],
+        far={2: None, 3: None, 4: None, 5: None, 8: None, 9: 2 * DK, 10: 2 * DK},
+        loose=(2, 9),
     )
     grads_received = shift_all(grads_sent)
-    (query_home,) = call(unpack_plain_body, [home(DK)], [y, *query_received], cost=BIG)
+    (query_home,) = unpack(y, query_received, DK, BIG)
     gate = like((CHUNKS * HEADS, CHUNK), bf16)
     value_home, key_home, input_home, forget_home = call(
-        unpack_body, [home(DV), home(DK), gate, gate], [y, *grads_received], after=[query_home]
+        unpack_body,
+        [home(DV), home(DK), gate, gate],
+        [y, *grads_received],
+        [VMEM((CHUNKS, EXTRA, CHUNK), bf16), pltpu.SemaphoreType.DMA((5 * CHUNKS,))],
+        after=[query_home],
+        raw=(1, 2, 3, 4),
+        loose=(1, 2, 3, 4),
+        raw_outs=(0, 1),
     )
     return (hidden_home, query_home, key_home, value_home, input_home, forget_home)
 

time: 178 us -> 138 us (0.78)
  local copies, waits for them, and re-layouts: 48.5 us -> 0.01 us
  Pallas kernels: 21 us -> 39.8 us
  waiting for transfers between devices: 61.5 us -> 47.8 us
  starting transfers between devices: 44.8 us -> 48.6 us
    unnamed x116 -> x4, local copies, waits for them, and re-layouts: 48.5 us -> 0.01 us
    ppermute x15, waiting for transfers between devices: 54.9 us -> 29.2 us  [shift_all(): moved.append(lax.ppermute(part, 'head', pairs))]
    pallas_call x12, Pallas kernels: 21 us -> 39.8 us  [call(): pl.pallas_call(run, out_shape=[pltpu.HBM(o.shape, o.dtype) if i in far_al...]
    all_to_all x3, waiting for transfers between devices: 6.69 us -> 18.6 us  [exchange(): return lax.all_to_all(part, 'ctx', split_axis=0, concat_axis=0, tiled=True)]
    ppermute x15, starting transfers between devices: 23.1 us -> 30 us  [shift_all(): moved.append(lax.ppermute(part, 'head', pairs))]
    all_to_all x3, starting transfers between devices: 21.6 us -> 18.6 us  [exchange(): return lax.all_to_all(part, 'ctx', split_axis=0, concat_axis=0, tiled=True)]
  transfers between devices with their start and end apart: 18 -> 18, of which waited for: 8 -> 8; matrix products, arithmetic and copies ran while one was open for 0% -> 0% of each run, Pallas kernels for 4% -> 20%
where the time goes in v3:
time: 138 us; the launch traced here: 137 us
  starting transfers between devices  48.6 us (35%)
  waiting for transfers between devices  47.8 us (35%)
  Pallas kernels  39.8 us (29%)
    pallas_call x12, Pallas kernels, call(): pl.pallas_call(run, out_shape=[pltpu.HBM(o.shape, o.dtype) if i in far_al...  39.8 us
    ppermute x15, starting transfers between devices, shift_all(): moved.append(lax.ppermute(part, 'head', pairs))  30 us
    ppermute x15, waiting for transfers between devices, shift_all(): moved.append(lax.ppermute(part, 'head', pairs))  29.2 us
    all_to_all x3, starting transfers between devices, exchange(): return lax.all_to_all(part, 'ctx', split_axis=0, concat_axis=0, tiled=True)  18.6 us
    all_to_all x3, waiting for transfers between devices, exchange(): return lax.all_to_all(part, 'ctx', split_axis=0, concat_axis=0, tiled=True)  18.6 us
  transfers between devices with their start and end apart: 18, of which 8 were waited for; matrix products, arithmetic and copies ran while one was open for 0% of the time, Pallas kernels for 20%

profile of v3, /device:TPU:2, one launch (start us, length us, event | category | flops | bytes accessed | tf_op | source)
XLA Modules:
  0.0 137.2 jit_solution(6065977298982276249)
XLA Ops:
  0.6 1.6 %shard_map.118 = (bf16[272,768]{1,0:T(8,128)(2,1)S(1)}, bf16[272,768]{1,0:T(8,128)(2,1)S(1)}, bf16[272,768]{1,0:T(8,128)(2,1)S(1)}, bf16[272,768]{1,0:T(8,128)(2,1)S(1)}) custom-call(s32[1]{0:T(128)} %bitcast.refs_0_, bf16[8,128,256]{2,1,0:T(8,128)(2,1)} %refs_1_.2, bf16[8,128,512]{2,1,0:T(8,128)(2,1)} %refs_2_.2, bf16[8,128]{1,0:T(8,128)(2,1)} %refs_3_.1, ...), custom_call_target="tpu_custom_call" | custom-call | flops 1 | bytes 1 | tf_op jit(solution)/shard_map/pallas_call | solution.py:150
  2.3 1.6 %collective-permute-start = (bf16[272,768]{1,0:T(8,128)(2,1)S(1)}, bf16[272,768]{1,0:T(8,128)(2,1)S(1)}, u32[]{:S(2)}, u32[]{:S(2)}) collective-permute-start(bf16[272,768]{1,0:T(8,128)(2,1)S(1)} %get-tuple-element.52), channel_id=1, source_target_pairs={{0,1},{1,2},{2,3},{3,0},{4,5},{5,6},{6,7},{7,4},{8,9},{9,10},{10,1... | collective-permute-start | bytes 1253384 | tf_op jit(solution)/shard_map/ppermute | solution.py:563
  3.9 2.9 %collective-permute-start.1 = (bf16[272,768]{1,0:T(8,128)(2,1)S(1)}, bf16[272,768]{1,0:T(8,128)(2,1)S(1)}, u32[]{:S(2)}, u32[]{:S(2)}) collective-permute-start(bf16[272,768]{1,0:T(8,128)(2,1)S(1)} %get-tuple-element.53), channel_id=1, source_target_pairs={{0,2},{1,3},{2,0},{3,1},{4,6},{5,7},{6,4},{7,5},{8,10},{9,11},{10,... | collective-permute-start | bytes 1253384 | tf_op jit(solution)/shard_map/ppermute | solution.py:563
  6.8 1.3 collective-permute-start.2
  8.2 6.8 %collective-permute-done.refs_2_.refs_3_ = bf16[272,768]{1,0:T(8,128)(2,1)S(1)} collective-permute-done((bf16[272,768]{1,0:T(8,128)(2,1)S(1)}, bf16[272,768]{1,0:T(8,128)(2,1)S(1)}, u32[]{:S(2)}, u32[]{:S(2)}) %collective-permute-start) | collective-permute-done | bytes 417824 | tf_op jit(solution)/shard_map/ppermute | solution.py:563
  15.0 2.6 %shard_map.120 = (bf16[256,768]{1,0:T(8,128)(2,1)S(1)}, bf16[256,768]{1,0:T(8,128)(2,1)}, bf16[256,768]{1,0:T(8,128)(2,1)}, bf16[256,768]{1,0:T(8,128)(2,1)}) custom-call(s32[1]{0:T(128)} %bitcast.refs_0_, bf16[8,128,256]{2,1,0:T(8,128)(2,1)} %refs_1_.3, bf16[8,128,512]{2,1,0:T(8,128)(2,1)} %refs_2_.3, bf16[272,768]{1,0:T(8,128)(2,1)S(1)} %collective-permute-done.refs_2_.refs_3_), custom_call_target="tpu_custom_call" | custom-call | flops 1 | bytes 1 | tf_op jit(solution)/shard_map/pallas_call | solution.py:150
  17.6 1.5 %collective-permute-start.3 = (bf16[256,768]{1,0:T(8,128)(2,1)}, bf16[256,768]{1,0:T(8,128)(2,1)}, u32[]{:S(2)}, u32[]{:S(2)}) collective-permute-start(bf16[256,768]{1,0:T(8,128)(2,1)} %get-tuple-element.57), channel_id=1, source_target_pairs={{0,1},{1,2},{2,3},{3,0},{4,5},{5,6},{6,7},{7,4},{8,9},{9,10},{10,1... | collective-permute-start | bytes 1179656 | tf_op jit(solution)/shard_map/ppermute | solution.py:563
  19.1 8.4 %collective-permute-start.4 = (bf16[256,768]{1,0:T(8,128)(2,1)}, bf16[256,768]{1,0:T(8,128)(2,1)}, u32[]{:S(2)}, u32[]{:S(2)}) collective-permute-start(bf16[256,768]{1,0:T(8,128)(2,1)} %get-tuple-element.58), channel_id=1, source_target_pairs={{0,2},{1,3},{2,0},{3,1},{4,6},{5,7},{6,4},{7,5},{8,10},{9,11},{10,... | collective-permute-start | bytes 1179656 | tf_op jit(solution)/shard_map/ppermute | solution.py:563
  27.6 2.5 %collective-permute-start.5 = (bf16[256,768]{1,0:T(8,128)(2,1)}, bf16[256,768]{1,0:T(8,128)(2,1)}, u32[]{:S(2)}, u32[]{:S(2)}) collective-permute-start(bf16[256,768]{1,0:T(8,128)(2,1)} %get-tuple-element.59), channel_id=1, source_target_pairs={{0,3},{1,0},{2,1},{3,2},{4,7},{5,4},{6,5},{7,6},{8,11},{9,8},{10,9... | collective-permute-start | bytes 1179656 | tf_op jit(solution)/shard_map/ppermute | solution.py:563
  30.1 0.0 collective-permute-done.1.refs_3_
  30.1 0.0 collective-permute-done.2.refs_4_
  30.1 2.9 %shard_map.119 = (bf16[2,4,128,768]{3,2,1,0:T(8,128)(2,1)}, f32[2,128,128]{2,1,0:T(8,128)S(1)}, f32[2,128,128]{2,1,0:T(8,128)S(1)}, bf16[32,16,640]{2,1,0:T(8,128)(2,1)}) custom-call(s32[1]{0:T(128)} %bitcast.refs_0_, bf16[272,768]{1,0:T(8,128)(2,1)S(1)} %get-tuple-element.51.refs_1_, bf16[272,768]{1,0:T(8,128)(2,1)S(1)} %collective-permute-done.refs_2_.refs_3_, ...), custom_call_target="tpu_custom_call" | custom-call | flops 1 | bytes 1 | tf_op jit(solution)/shard_map/pallas_call | solution.py:150
  33.0 0.0 copy-start
  33.1 8.5 %all-to-all-start = ((bf16[32,16,640]{2,1,0:T(8,128)(2,1)}), bf16[32,16,640]{2,1,0:T(8,128)(2,1)S(1)}, u32[]{:S(2)}, u32[]{:S(2)}) async-start(bf16[32,16,640]{2,1,0:T(8,128)(2,1)} %get-tuple-element.55.refs_10_), calls=%async_computation | async-start | bytes 1310720 | tf_op jit(solution)/shard_map/all_to_all | solution.py:586
  41.5 0.0 collective-permute-done.3.refs_2_
  41.5 0.6 collective-permute-done.4.refs_3_
  42.1 0.0 collective-permute-done.5.refs_4_
  42.1 4.1 %shard_map.121 = (bf16[2,4,128,768]{3,2,1,0:T(8,128)(2,1)S(1)}, bf16[2,512,512]{2,1,0:T(8,128)(2,1)}, bf16[2,512,512]{2,1,0:T(8,128)(2,1)}, f32[2,128,128]{2,1,0:T(8,128)}) custom-call(s32[1]{0:T(128)} %bitcast.refs_0_, bf16[256,768]{1,0:T(8,128)(2,1)S(1)} %get-tuple-element.56.refs_1_, bf16[256,768]{1,0:T(8,128)(2,1)} %collective-permute-done.3.refs_2_, ...), custom_call_target="tpu_custom_call" | custom-call | flops 10000000000 | bytes 10000000000 | tf_op jit(solution)/shard_map/pallas_call | solution.py:150
  46.3 0.0 copy-done
  46.3 7.1 %all-to-all-done.refs_1_ = bf16[32,16,640]{2,1,0:T(8,128)(2,1)S(1)} async-done(((bf16[32,16,640]{2,1,0:T(8,128)(2,1)}), bf16[32,16,640]{2,1,0:T(8,128)(2,1)S(1)}, u32[]{:S(2)}, u32[]{:S(2)}) %all-to-all-start) | async-done | bytes 655392 | tf_op jit(solution)/shard_map/all_to_all | solution.py:586
  53.4 4.1 %shard_map.122 = (bf16[32,16,1024]{2,1,0:T(8,128)(2,1)}, f32[8,128]{1,0:T(8,128)S(1)}, f32[32,8,128]{2,1,0:T(8,128)S(1)}, bf16[2,512,512]{2,1,0:T(8,128)(2,1)}, f32[2,128,128]{2,1,0:T(8,128)}) custom-call(s32[1]{0:T(128)} %bitcast.1.refs_0_.refs_1_, bf16[32,16,640]{2,1,0:T(8,128)(2,1)S(1)} %all-to-all-done.refs_1_, ...), custom_call_target="tpu_custom_call" | custom-call | flops 1 | bytes 1 | tf_op jit(solution)/shard_map/pallas_call | solution.py:150
  57.6 5.1 %all-to-all-start.1 = ((bf16[32,16,1024]{2,1,0:T(8,128)(2,1)}), bf16[32,16,1024]{2,1,0:T(8,128)(2,1)S(1)}, u32[]{:S(2)}, u32[]{:S(2)}) async-start(bf16[32,16,1024]{2,1,0:T(8,128)(2,1)} %get-tuple-element.65), calls=%async_computation.1 | async-start | bytes 2097152 | tf_op jit(solution)/shard_map/all_to_all | solution.py:586
  62.7 4.8 %shard_map.123 = (bf16[2,512,512]{2,1,0:T(8,128)(2,1)}, bf16[2,512,512]{2,1,0:T(8,128)(2,1)}, bf16[2,512,512]{2,1,0:T(8,128)(2,1)}) custom-call(bf16[2,4,128,768]{3,2,1,0:T(8,128)(2,1)} %get-tuple-element.60.refs_5_.refs_0_.refs_1_.refs_3_, bf16[2,512,512]{2,1,0:T(8,128)(2,1)} %get-tuple-element.67.refs_1_, ...), custom_call_target="tpu_custom_call" | custom-call | flops 10000000000 | bytes 10000000000 | tf_op jit(solution)/shard_map/pallas_call | solution.py:150
  67.5 11.4 %all-to-all-done.1.refs_1_.refs_9_ = bf16[32,16,1024]{2,1,0:T(8,128)(2,1)S(1)} async-done(((bf16[32,16,1024]{2,1,0:T(8,128)(2,1)}), bf16[32,16,1024]{2,1,0:T(8,128)(2,1)S(1)}, u32[]{:S(2)}, u32[]{:S(2)}) %all-to-all-start.1) | async-done | bytes 1048608 | tf_op jit(solution)/shard_map/all_to_all | solution.py:586
  79.0 4.2 %shard_map.124 = (bf16[256,512]{1,0:T(8,128)(2,1)}, bf16[256,512]{1,0:T(8,128)(2,1)}, bf16[256,512]{1,0:T(8,128)(2,1)}, bf16[256,512]{1,0:T(8,128)(2,1)}, bf16[3...) custom-call(s32[1]{0:T(128)} %bitcast.refs_0_, ...), custom_call_target="tpu_custom_call" | custom-call | flops 1 | bytes 1 | tf_op jit(solution)/shard_map/pallas_call | solution.py:150
  83.1 5.0 %all-to-all-start.2 = ((bf16[32,16,640]{2,1,0:T(8,128)(2,1)}), bf16[32,16,640]{2,1,0:T(8,128)(2,1)S(1)}, u32[]{:S(2)}, u32[]{:S(2)}) async-start(bf16[32,16,640]{2,1,0:T(8,128)(2,1)} %get-tuple-element.84), calls=%async_computation.2 | async-start | bytes 1310720 | tf_op jit(solution)/shard_map/all_to_all | solution.py:586
  88.2 1.6 %collective-permute-start.6 = (bf16[256,512]{1,0:T(8,128)(2,1)}, bf16[256,512]{1,0:T(8,128)(2,1)S(1)}, u32[]{:S(2)}, u32[]{:S(2)}) collective-permute-start(bf16[256,512]{1,0:T(8,128)(2,1)} %get-tuple-element.73), channel_id=1, source_target_pairs={{0,1},{1,2},{2,3},{3,0},{4,5},{5,6},{6,7},{7,4},{8,9},{9,10},{10,1... | collective-permute-start | bytes 786440 | tf_op jit(solution)/shard_map/ppermute | solution.py:563
  89.8 0.1 collective-permute-start.7
  89.9 2.6 %collective-permute-start.8 = (bf16[256,512]{1,0:T(8,128)(2,1)}, bf16[256,512]{1,0:T(8,128)(2,1)S(1)}, u32[]{:S(2)}, u32[]{:S(2)}) collective-permute-start(bf16[256,512]{1,0:T(8,128)(2,1)} %get-tuple-element.75), channel_id=1, source_target_pairs={{0,3},{1,0},{2,1},{3,2},{4,7},{5,4},{6,5},{7,6},{8,11},{9,8},{10,9... | collective-permute-start | bytes 786440 | tf_op jit(solution)/shard_map/ppermute | solution.py:563
  92.5 4.7 %shard_map.126 = (bf16[256,256]{1,0:T(8,128)(2,1)}, bf16[256,256]{1,0:T(8,128)(2,1)}, bf16[256,256]{1,0:T(8,128)(2,1)}, bf16[256,256]{1,0:T(8,128)(2,1)}, f32[2,...) custom-call(s32[1]{0:T(128)} %bitcast.refs_0_, ...), custom_call_target="tpu_custom_call" | custom-call | flops 10000000000 | bytes 10000000000 | tf_op jit(solution)/shard_map/pallas_call | solution.py:150
  97.2 0.0 copy-start.1
  97.2 0.1 collective-permute-start.9
  97.3 2.8 %collective-permute-start.10 = (bf16[256,256]{1,0:T(8,128)(2,1)}, bf16[256,256]{1,0:T(8,128)(2,1)S(1)}, u32[]{:S(2)}, u32[]{:S(2)}) collective-permute-start(bf16[256,256]{1,0:T(8,128)(2,1)} %get-tuple-element.82), channel_id=1, source_target_pairs={{0,2},{1,3},{2,0},{3,1},{4,6},{5,7},{6,4},{7,5},{8,10},{9,11},{10,... | collective-permute-start | bytes 393224 | tf_op jit(solution)/shard_map/ppermute | solution.py:563
  100.1 5.0 %collective-permute-done.6.refs_2_ = bf16[256,512]{1,0:T(8,128)(2,1)S(1)} collective-permute-done((bf16[256,512]{1,0:T(8,128)(2,1)}, bf16[256,512]{1,0:T(8,128)(2,1)S(1)}, u32[]{:S(2)}, u32[]{:S(2)}) %collective-permute-start.6) | collective-permute-done | bytes 262176 | tf_op jit(solution)/shard_map/ppermute | solution.py:563
  105.1 0.0 collective-permute-start.11
  105.1 0.0 collective-permute-done.7.refs_3_
  105.1 0.4 collective-permute-done.8.refs_4_
  105.5 1.9 %shard_map.125.refs_13_ = bf16[8,128,512]{2,1,0:T(8,128)(2,1)} custom-call(s32[1]{0:T(128)} %bitcast.refs_0_, bf16[256,512]{1,0:T(8,128)(2,1)} %get-tuple-element.72.refs_1_, bf16[256,512]{1,0:T(8,128)(2,1)S(1)} %collective-permute-done.6.refs_2_, bf16[256,512]{1,0:T(8,128)(2,1)S(1)} %collective-permute-done.7.refs_3_, ...), custom_call_target="tpu_custom_call" | custom-call | flops 1 | bytes 1 | tf_op jit(solution)/shard_map/pallas_call | solution.py:150
  107.5 0.0 all-to-all-done.2.refs_2_
  107.5 0.0 copy-done.1
  107.5 5.1 %shard_map.128 = (bf16[272,768]{1,0:T(8,128)(2,1)S(1)}, bf16[272,768]{1,0:T(8,128)(2,1)S(1)}, bf16[272,768]{1,0:T(8,128)(2,1)S(1)}, bf16[272,768]{1,0:T(8,128)(2,1)S(1)}) custom-call(s32[1]{0:T(128)} %bitcast.refs_0_, s32[1]{0:T(128)} %bitcast.1.refs_0_.refs_1_, bf16[32,16,640]{2,1,0:T(8,128)(2,1)S(1)} %all-to-all-done.2.refs_2_, ...), custom_call_target="tpu_custom_call" | custom-call | flops 1 | bytes 1 | tf_op jit(solution)/shard_map/pallas_call | solution.py:150
  112.6 1.6 %collective-permute-start.12 = (bf16[272,768]{1,0:T(8,128)(2,1)S(1)}, bf16[272,768]{1,0:T(8,128)(2,1)S(1)}, u32[]{:S(2)}, u32[]{:S(2)}) collective-permute-start(bf16[272,768]{1,0:T(8,128)(2,1)S(1)} %get-tuple-element.89), channel_id=1, source_target_pairs={{0,1},{1,2},{2,3},{3,0},{4,5},{5,6},{6,7},{7,4},{8,9},{9,10},{10,1... | collective-permute-start | bytes 1253384 | tf_op jit(solution)/shard_map/ppermute | solution.py:563
  114.3 2.6 %collective-permute-start.13 = (bf16[272,768]{1,0:T(8,128)(2,1)S(1)}, bf16[272,768]{1,0:T(8,128)(2,1)S(1)}, u32[]{:S(2)}, u32[]{:S(2)}) collective-permute-start(bf16[272,768]{1,0:T(8,128)(2,1)S(1)} %get-tuple-element.90), channel_id=1, source_target_pairs={{0,2},{1,3},{2,0},{3,1},{4,6},{5,7},{6,4},{7,5},{8,10},{9,11},{10,... | collective-permute-start | bytes 1253384 | tf_op jit(solution)/shard_map/ppermute | solution.py:563
  116.9 0.0 collective-permute-done.9.refs_2_
  116.9 0.1 collective-permute-start.14
  117.0 0.0 collective-permute-done.10.refs_3_
  117.0 0.0 collective-permute-done.11.refs_4_
  117.0 1.8 %shard_map.127.refs_5_ = bf16[8,128,256]{2,1,0:T(8,128)(2,1)} custom-call(s32[1]{0:T(128)} %bitcast.refs_0_, bf16[256,256]{1,0:T(8,128)(2,1)} %get-tuple-element.80.refs_1_, bf16[256,256]{1,0:T(8,128)(2,1)S(1)} %collective-permute-done.9.refs_2_, bf16[256,256]{1,0:T(8,128)(2,1)S(1)} %collective-permute-done.10.refs_3_, ...), custom_call_target="tpu_custom_call" | custom-call | flops 10000000000 | bytes 10000000000 | tf_op jit(solution)/shard_map/pallas_call | solution.py:150
  118.8 6.2 %collective-permute-done.12.refs_2_ = bf16[272,768]{1,0:T(8,128)(2,1)S(1)} collective-permute-done((bf16[272,768]{1,0:T(8,128)(2,1)S(1)}, bf16[272,768]{1,0:T(8,128)(2,1)S(1)}, u32[]{:S(2)}, u32[]{:S(2)}) %collective-permute-start.12) | collective-permute-done | bytes 417824 | tf_op jit(solution)/shard_map/ppermute | solution.py:563
  125.1 10.1 %collective-permute-done.13.refs_3_ = bf16[272,768]{1,0:T(8,128)(2,1)S(1)} collective-permute-done((bf16[272,768]{1,0:T(8,128)(2,1)S(1)}, bf16[272,768]{1,0:T(8,128)(2,1)S(1)}, u32[]{:S(2)}, u32[]{:S(2)}) %collective-permute-start.13) | collective-permute-done | bytes 417824 | tf_op jit(solution)/shard_map/ppermute | solution.py:563
  135.1 0.0 collective-permute-done.14.refs_4_
  135.1 1.9 %shard_map.129 = (bf16[8,128,512]{2,1,0:T(8,128)(2,1)}, bf16[8,128,256]{2,1,0:T(8,128)(2,1)}, bf16[8,128]{1,0:T(8,128)(2,1)}, bf16[8,128]{1,0:T(8,128)(2,1)}) custom-call(s32[1]{0:T(128)} %bitcast.refs_0_, bf16[272,768]{1,0:T(8,128)(2,1)S(1)} %get-tuple-element.88.refs_1_, bf16[272,768]{1,0:T(8,128)(2,1)S(1)} %collective-permute-done.12.refs_2_, ...), custom_call_target="tpu_custom_call" | custom-call | flops 1 | bytes 1 | tf_op jit(solution)/shard_map/pallas_call | solution.py:150
Async XLA Ops:
  2.3 12.7 %collective-permute-start = (bf16[272,768]{1,0:T(8,128)(2,1)S(1)}, bf16[272,768]{1,0:T(8,128)(2,1)S(1)}, u32[]{:S(2)}, u32[]{:S(2)}) collective-permute-start(bf16[272,768]{1,0:T(8,128)(2,1)S(1)} %get-tuple-element.52), channel_id=1, source_target_pairs={{0,1},{1,2},{2,3},{3,0},{4,5},{5,6},{6,7},{7,4},{8,9},{9,10},{10,1... | collective-permute-start | bytes 1253384 | tf_op jit(solution)/shard_map/ppermute | solution.py:563
  3.9 26.2 %collective-permute-start.1 = (bf16[272,768]{1,0:T(8,128)(2,1)S(1)}, bf16[272,768]{1,0:T(8,128)(2,1)S(1)}, u32[]{:S(2)}, u32[]{:S(2)}) collective-permute-start(bf16[272,768]{1,0:T(8,128)(2,1)S(1)} %get-tuple-element.53), channel_id=1, source_target_pairs={{0,2},{1,3},{2,0},{3,1},{4,6},{5,7},{6,4},{7,5},{8,10},{9,11},{10,... | collective-permute-start | bytes 1253384 | tf_op jit(solution)/shard_map/ppermute | solution.py:563
  6.8 23.3 %collective-permute-start.2 = (bf16[272,768]{1,0:T(8,128)(2,1)S(1)}, bf16[272,768]{1,0:T(8,128)(2,1)S(1)}, u32[]{:S(2)}, u32[]{:S(2)}) collective-permute-start(bf16[272,768]{1,0:T(8,128)(2,1)S(1)} %get-tuple-element.54), channel_id=1, source_target_pairs={{0,3},{1,0},{2,1},{3,2},{4,7},{5,4},{6,5},{7,6},{8,11},{9,8},{10,9... | collective-permute-start | bytes 1253384 | tf_op jit(solution)/shard_map/ppermute | solution.py:563
  17.6 23.9 %collective-permute-start.3 = (bf16[256,768]{1,0:T(8,128)(2,1)}, bf16[256,768]{1,0:T(8,128)(2,1)}, u32[]{:S(2)}, u32[]{:S(2)}) collective-permute-start(bf16[256,768]{1,0:T(8,128)(2,1)} %get-tuple-element.57), channel_id=1, source_target_pairs={{0,1},{1,2},{2,3},{3,0},{4,5},{5,6},{6,7},{7,4},{8,9},{9,10},{10,1... | collective-permute-start | bytes 1179656 | tf_op jit(solution)/shard_map/ppermute | solution.py:563
  19.1 23.0 %collective-permute-start.4 = (bf16[256,768]{1,0:T(8,128)(2,1)}, bf16[256,768]{1,0:T(8,128)(2,1)}, u32[]{:S(2)}, u32[]{:S(2)}) collective-permute-start(bf16[256,768]{1,0:T(8,128)(2,1)} %get-tuple-element.58), channel_id=1, source_target_pairs={{0,2},{1,3},{2,0},{3,1},{4,6},{5,7},{6,4},{7,5},{8,10},{9,11},{10,... | collective-permute-start | bytes 1179656 | tf_op jit(solution)/shard_map/ppermute | solution.py:563
  27.6 14.6 %collective-permute-start.5 = (bf16[256,768]{1,0:T(8,128)(2,1)}, bf16[256,768]{1,0:T(8,128)(2,1)}, u32[]{:S(2)}, u32[]{:S(2)}) collective-permute-start(bf16[256,768]{1,0:T(8,128)(2,1)} %get-tuple-element.59), channel_id=1, source_target_pairs={{0,3},{1,0},{2,1},{3,2},{4,7},{5,4},{6,5},{7,6},{8,11},{9,8},{10,9... | collective-permute-start | bytes 1179656 | tf_op jit(solution)/shard_map/ppermute | solution.py:563
  33.0 13.2 %copy-start = (f32[2,128,128]{2,1,0:T(8,128)}, f32[2,128,128]{2,1,0:T(8,128)S(1)}, u32[]{:S(2)}) copy-start(f32[2,128,128]{2,1,0:T(8,128)S(1)} %get-tuple-element.61.refs_6_) | copy-start | bytes 393220
  33.1 20.4 %all-to-all-start = ((bf16[32,16,640]{2,1,0:T(8,128)(2,1)}), bf16[32,16,640]{2,1,0:T(8,128)(2,1)S(1)}, u32[]{:S(2)}, u32[]{:S(2)}) async-start(bf16[32,16,640]{2,1,0:T(8,128)(2,1)} %get-tuple-element.55.refs_10_), calls=%async_computation | async-start | bytes 1310720 | tf_op jit(solution)/shard_map/all_to_all | solution.py:586
  57.6 21.4 %all-to-all-start.1 = ((bf16[32,16,1024]{2,1,0:T(8,128)(2,1)}), bf16[32,16,1024]{2,1,0:T(8,128)(2,1)S(1)}, u32[]{:S(2)}, u32[]{:S(2)}) async-start(bf16[32,16,1024]{2,1,0:T(8,128)(2,1)} %get-tuple-element.65), calls=%async_computation.1 | async-start | bytes 2097152 | tf_op jit(solution)/shard_map/all_to_all | solution.py:586
  83.1 24.3 %all-to-all-start.2 = ((bf16[32,16,640]{2,1,0:T(8,128)(2,1)}), bf16[32,16,640]{2,1,0:T(8,128)(2,1)S(1)}, u32[]{:S(2)}, u32[]{:S(2)}) async-start(bf16[32,16,640]{2,1,0:T(8,128)(2,1)} %get-tuple-element.84), calls=%async_computation.2 | async-start | bytes 1310720 | tf_op jit(solution)/shard_map/all_to_all | solution.py:586
  88.2 16.9 %collective-permute-start.6 = (bf16[256,512]{1,0:T(8,128)(2,1)}, bf16[256,512]{1,0:T(8,128)(2,1)S(1)}, u32[]{:S(2)}, u32[]{:S(2)}) collective-permute-start(bf16[256,512]{1,0:T(8,128)(2,1)} %get-tuple-element.73), channel_id=1, source_target_pairs={{0,1},{1,2},{2,3},{3,0},{4,5},{5,6},{6,7},{7,4},{8,9},{9,10},{10,1... | collective-permute-start | bytes 786440 | tf_op jit(solution)/shard_map/ppermute | solution.py:563
  89.8 15.3 %collective-permute-start.7 = (bf16[256,512]{1,0:T(8,128)(2,1)}, bf16[256,512]{1,0:T(8,128)(2,1)S(1)}, u32[]{:S(2)}, u32[]{:S(2)}) collective-permute-start(bf16[256,512]{1,0:T(8,128)(2,1)} %get-tuple-element.74), channel_id=1, source_target_pairs={{0,2},{1,3},{2,0},{3,1},{4,6},{5,7},{6,4},{7,5},{8,10},{9,11},{10,... | collective-permute-start | bytes 786440 | tf_op jit(solution)/shard_map/ppermute | solution.py:563
  89.9 15.6 %collective-permute-start.8 = (bf16[256,512]{1,0:T(8,128)(2,1)}, bf16[256,512]{1,0:T(8,128)(2,1)S(1)}, u32[]{:S(2)}, u32[]{:S(2)}) collective-permute-start(bf16[256,512]{1,0:T(8,128)(2,1)} %get-tuple-element.75), channel_id=1, source_target_pairs={{0,3},{1,0},{2,1},{3,2},{4,7},{5,4},{6,5},{7,6},{8,11},{9,8},{10,9... | collective-permute-start | bytes 786440 | tf_op jit(solution)/shard_map/ppermute | solution.py:563
  97.2 10.2 %copy-start.1 = (f32[2,128,128]{2,1,0:T(8,128)S(1)}, f32[2,128,128]{2,1,0:T(8,128)}, u32[]{:S(2)}) copy-start(f32[2,128,128]{2,1,0:T(8,128)} %copy-done) | copy-start | bytes 393220
  97.2 19.7 %collective-permute-start.9 = (bf16[256,256]{1,0:T(8,128)(2,1)}, bf16[256,256]{1,0:T(8,128)(2,1)S(1)}, u32[]{:S(2)}, u32[]{:S(2)}) collective-permute-start(bf16[256,256]{1,0:T(8,128)(2,1)} %get-tuple-element.81), channel_id=1, source_target_pairs={{0,1},{1,2},{2,3},{3,0},{4,5},{5,6},{6,7},{7,4},{8,9},{9,10},{10,1... | collective-permute-start | bytes 393224 | tf_op jit(solution)/shard_map/ppermute | solution.py:563
  97.3 19.7 %collective-permute-start.10 = (bf16[256,256]{1,0:T(8,128)(2,1)}, bf16[256,256]{1,0:T(8,128)(2,1)S(1)}, u32[]{:S(2)}, u32[]{:S(2)}) collective-permute-start(bf16[256,256]{1,0:T(8,128)(2,1)} %get-tuple-element.82), channel_id=1, source_target_pairs={{0,2},{1,3},{2,0},{3,1},{4,6},{5,7},{6,4},{7,5},{8,10},{9,11},{10,... | collective-permute-start | bytes 393224 | tf_op jit(solution)/shard_map/ppermute | solution.py:563
  105.1 12.0 %collective-permute-start.11 = (bf16[256,256]{1,0:T(8,128)(2,1)}, bf16[256,256]{1,0:T(8,128)(2,1)S(1)}, u32[]{:S(2)}, u32[]{:S(2)}) collective-permute-start(bf16[256,256]{1,0:T(8,128)(2,1)} %get-tuple-element.83), channel_id=1, source_target_pairs={{0,3},{1,0},{2,1},{3,2},{4,7},{5,4},{6,5},{7,6},{8,11},{9,8},{10,9... | collective-permute-start | bytes 393224 | tf_op jit(solution)/shard_map/ppermute | solution.py:563
  112.6 12.4 %collective-permute-start.12 = (bf16[272,768]{1,0:T(8,128)(2,1)S(1)}, bf16[272,768]{1,0:T(8,128)(2,1)S(1)}, u32[]{:S(2)}, u32[]{:S(2)}) collective-permute-start(bf16[272,768]{1,0:T(8,128)(2,1)S(1)} %get-tuple-element.89), channel_id=1, source_target_pairs={{0,1},{1,2},{2,3},{3,0},{4,5},{5,6},{6,7},{7,4},{8,9},{9,10},{10,1... | collective-permute-start | bytes 1253384 | tf_op jit(solution)/shard_map/ppermute | solution.py:563
  114.3 20.9 %collective-permute-start.13 = (bf16[272,768]{1,0:T(8,128)(2,1)S(1)}, bf16[272,768]{1,0:T(8,128)(2,1)S(1)}, u32[]{:S(2)}, u32[]{:S(2)}) collective-permute-start(bf16[272,768]{1,0:T(8,128)(2,1)S(1)} %get-tuple-element.90), channel_id=1, source_target_pairs={{0,2},{1,3},{2,0},{3,1},{4,6},{5,7},{6,4},{7,5},{8,10},{9,11},{10,... | collective-permute-start | bytes 1253384 | tf_op jit(solution)/shard_map/ppermute | solution.py:563
  116.9 18.2 %collective-permute-start.14 = (bf16[272,768]{1,0:T(8,128)(2,1)S(1)}, bf16[272,768]{1,0:T(8,128)(2,1)S(1)}, u32[]{:S(2)}, u32[]{:S(2)}) collective-permute-start(bf16[272,768]{1,0:T(8,128)(2,1)S(1)} %get-tuple-element.91), channel_id=1, source_target_pairs={{0,3},{1,0},{2,1},{3,2},{4,7},{5,4},{6,5},{7,6},{8,11},{9,8},{10,9... | collective-permute-start | bytes 1253384 | tf_op jit(solution)/shard_map/ppermute | solution.py:563
